TPU v7x, 32 devices: a whole 2x2x4 slice. The times are simulated.
32 devices in a mesh: box: 16 (over z, y, x), col: 2 (over core).
Axes of the slice: x: 2, y: 2, z: 4, core: 2. Of those that a mesh axis runs over, the one named last changes fastest.
Arguments:
- points: bfloat16 [256, 3, 512], P('box'), may hold values from 0 to 1
- sketch: bfloat16 [256, 512, 128], P('box', 'col'), may hold values from -6 to 6
- near_mask: int32 [256, 9], P('box'), may hold values from 0 to 1, as said below
Outputs:
- basis: bfloat16 [256, 512, 128], P('box', 'col')
- coupling: float32 [256, 9, 128, 128], P('box', None, 'col')
Inputs may be any that keep to these rules, and one draw needn't show every extreme that they name: near_mask[b, s] is 1 for the box itself and for its edge neighbours that lie on the plate, 0 for slots off the plate; a diagonal neighbour is near or not by a relation that is symmetric between the two boxes.
All inputs are finite; a program needn't handle non-finite values.
Results may differ from a plain program's by a relative error of at most 0.007.
Values may be sent and summed in bfloat16 or wider, within the bound.
No kernel may reach another device: no remote copies, remote signals or barrier semaphores. Data moves between devices by JAX's collectives and lax.ppermute only.
A program may use at most 64 MiB of HBM per device.

v0:
```python
import math

import jax
import jax.numpy as jnp
from jax import lax
from jax.sharding import PartitionSpec as P

lift_scale = 0.25


def shortened(array):

    def short(part):
        return part.astype(jnp.bfloat16) if part.dtype == jnp.float32 else part

    return jax.tree.map(short, array)


def from_behind(value, axis, steps):
    count = lax.axis_size(axis)
    initial, last = (max(0, -steps), min(count, count - steps))
    return lax.ppermute(value, axis, [(source, source + steps) for source in range(initial, last)])


def interaction(row_points, col_points, shift_y, shift_x, centre, box_points):
    row_coords = row_points.astype(jnp.float32)
    col_coords = col_points.astype(jnp.float32)
    delta_u = shift_x + col_coords[..., 0, None, :] - row_coords[..., 0, :, None]
    delta_v = shift_y + col_coords[..., 1, None, :] - row_coords[..., 1, :, None]
    delta_w = lift_scale * (col_coords[..., 2, None, :] - row_coords[..., 2, :, None])
    strength = 0.25 / math.sqrt(box_points)
    soften = 0.5 / math.sqrt(box_points)
    values = strength / jnp.sqrt(
        delta_u * delta_u + delta_v * delta_v + delta_w * delta_w + soften * soften
    )
    if centre:
        row_ids = jnp.arange(row_coords.shape[-1], dtype=jnp.int32)
        col_ids = jnp.arange(col_coords.shape[-1], dtype=jnp.int32)
        values = values + jnp.where(row_ids[:, None] == col_ids[None, :], 1.0, 0.0).astype(
            jnp.float32
        )
    return values


def facing(offset, tile_side):
    if offset == -1:
        return slice(tile_side - 1, tile_side)
    if offset == 1:
        return slice(0, 1)
    return slice(0, tile_side)


def landing(offset, tile_side):
    if offset == -1:
        return slice(0, 1)
    if offset == 1:
        return slice(tile_side + 1, tile_side + 2)
    return slice(1, tile_side + 1)


def neighbours(arrays, tile_side, grid_side):
    extended = [
        jnp.zeros((tile_side + 2, tile_side + 2) + member.shape[2:], member.dtype)
        .at[1 : tile_side + 1, 1 : tile_side + 1]
        .set(member)
        for member in arrays
    ]
    for offset_y in (-1, 0, 1):
        for offset_x in (-1, 0, 1):
            if offset_y == 0 and offset_x == 0:
                continue
            pieces = tuple(
                (
                    member[facing(offset_y, tile_side), facing(offset_x, tile_side)]
                    for member in arrays
                )
            )
            received = jax.tree.map(
                lambda part, own: part.astype(own.dtype),
                from_behind(shortened(pieces), "box", -(offset_y * grid_side + offset_x)),
                pieces,
            )
            extended = [
                holder.at[landing(offset_y, tile_side), landing(offset_x, tile_side)].set(arrived)
                for holder, arrived in zip(extended, received)
            ]
    return extended


def slot_view(extended, row_index, offset_y, offset_x, tile_side):
    row_block = lax.dynamic_index_in_dim(extended, row_index + 1 + offset_y, 0, keepdims=False)
    return row_block[1 + offset_x : 1 + offset_x + tile_side]


def apply_inverse(gram_sum, sketch_t):
    lower_factor = jnp.linalg.cholesky(gram_sum)
    identity = jnp.broadcast_to(jnp.eye(gram_sum.shape[1], dtype=gram_sum.dtype), gram_sum.shape)
    inverse_lower = lax.linalg.triangular_solve(lower_factor, identity, left_side=True, lower=True)
    return jnp.einsum("brs,bsm->brm", inverse_lower, sketch_t, precision=lax.Precision.HIGHEST)


def orthonormal_local(sketch_t, box_points):
    gram_sum = (
        jnp.einsum("brm,bsm->brs", sketch_t, sketch_t, precision=lax.Precision.HIGHEST) / box_points
    )
    return apply_inverse(gram_sum, sketch_t)


def body(points, sketch, near_mask):
    box_count = points.shape[0]
    tile_side = math.isqrt(box_count)
    grid_side = math.isqrt(lax.axis_size("box"))
    box_points = points.shape[2]
    half_points = sketch.shape[1]
    skel_rank = sketch.shape[2]
    col_index = lax.axis_index("col")
    rows_half = tile_side // lax.axis_size("col")
    own_rows = col_index * rows_half + jnp.arange(rows_half, dtype=jnp.int32)
    weights = near_mask.astype(jnp.float32).reshape(tile_side, tile_side, 9)
    coord_grid = points.reshape(tile_side, tile_side, 3, box_points)
    omega_grid = sketch.reshape(tile_side, tile_side, half_points, skel_rank)
    ext_coords, ext_omega = neighbours((coord_grid, omega_grid), tile_side, grid_side)
    omega_full = lax.all_gather(ext_omega, "col", axis=2, tiled=True)

    def sketch_full(row_index):
        row_coords = lax.dynamic_index_in_dim(coord_grid, row_index, 0, keepdims=False)
        row_weights = lax.dynamic_index_in_dim(weights, row_index, 0, keepdims=False)
        running = jnp.zeros((box_points, tile_side, skel_rank), jnp.float32)
        for stencil in range(9):
            offset_y = stencil // 3 - 1
            offset_x = stencil % 3 - 1
            near_coords = slot_view(ext_coords, row_index, offset_y, offset_x, tile_side)
            near_omega = slot_view(omega_full, row_index, offset_y, offset_x, tile_side)
            block_vals = interaction(
                row_coords, near_coords, offset_y, offset_x, stencil == 4, box_points
            ).astype(jnp.bfloat16)
            running = (
                running
                + jnp.einsum(
                    "bij,bjr->ibr", block_vals, near_omega, preferred_element_type=jnp.float32
                )
                * row_weights[None, :, stencil, None]
            )
        return running

    blocks = lax.map(sketch_full, own_rows)
    sketch_t = jnp.transpose(blocks, (0, 2, 3, 1)).reshape(
        rows_half * tile_side, skel_rank, box_points
    )
    own_t = orthonormal_local(orthonormal_local(sketch_t, box_points), box_points)
    own_basis = jnp.transpose(own_t.astype(jnp.bfloat16), (0, 2, 1))
    basis_out = lax.all_to_all(own_basis, "col", split_axis=1, concat_axis=0, tiled=True)
    ext_basis = neighbours(
        (basis_out.reshape(tile_side, tile_side, half_points, skel_rank),), tile_side, grid_side
    )[0]
    basis_full = lax.all_gather(ext_basis, "col", axis=2, tiled=True)

    def couple_full(row_index):
        row_coords = lax.dynamic_index_in_dim(coord_grid, row_index, 0, keepdims=False)
        row_weights = lax.dynamic_index_in_dim(weights, row_index, 0, keepdims=False)
        own_basis = slot_view(basis_full, row_index, 0, 0, tile_side)
        collected = []
        for stencil in range(9):
            offset_y = stencil // 3 - 1
            offset_x = stencil % 3 - 1
            near_coords = slot_view(ext_coords, row_index, offset_y, offset_x, tile_side)
            near_basis = slot_view(basis_full, row_index, offset_y, offset_x, tile_side)
            block_vals = interaction(
                row_coords, near_coords, offset_y, offset_x, stencil == 4, box_points
            ).astype(jnp.bfloat16)
            projected = jnp.einsum(
                "bir,bij->brj", own_basis, block_vals, preferred_element_type=jnp.float32
            ).astype(jnp.bfloat16)
            coupling_term = (
                jnp.einsum(
                    "brj,bjs->brs", projected, near_basis, preferred_element_type=jnp.float32
                )
                * (1.0 / box_points)
                * row_weights[:, stencil, None, None]
            )
            collected.append(coupling_term)
        return jnp.stack(collected, axis=1)

    owned = lax.map(couple_full, own_rows).reshape(rows_half * tile_side, 9, skel_rank, skel_rank)
    coupling = lax.all_to_all(owned, "col", split_axis=2, concat_axis=0, tiled=True)
    return (basis_out, coupling)


def solution(mesh):
    return jax.shard_map(
        body,
        mesh=mesh,
        in_specs=(P("box", None, None), P("box", "col", None), P("box", None)),
        out_specs=(P("box", "col", None), P("box", None, "col", None)),
        check_vma=False,
    )
```

profile of v0, /device:TPU:0, one launch (start us, length us, event | category | flops | bytes accessed | tf_op | source)
XLA Modules:
  0.0 692.0 jit_solution(10549381195880726338)
XLA Ops:
  8.7 5.9 collective-permute-start
  14.7 3.5 collective-permute-start.1
  18.2 4.4 collective-permute-start.2
  39.0 4.2 collective-permute-done.6
  47.5 4.5 collective-permute-start.8
  52.0 3.9 collective-permute-start.9
  57.3 4.0 collective-permute-start.11
  74.4 5.0 collective-permute-done.15
  79.8 66.7 %while.55 = (s32[]{:T(128)}, f32[2,512,4,128]{1,3,2,0:T(8,128)S(1)}, s32[2]{0:T(128)S(1)}, bf16[6,6,512,128]{2,3,1,0:T(8,128)(2,1)}, bf16[6,6,3,512]{3,1,2,0:T(8...) while((s32[]{:T(128)}, ...), condition=%wide.region_2.0_spmd, body=%wide.region_1.0_spmd.sunk | while | flops 2535280640 | bytes 40105004 | solution.py:146
  86.8 3.4 fusion.455
  120.1 3.4 fusion.455
  150.3 95.1 %custom-call.8 = f32[8,128,128]{2,1,0:T(8,128)S(1)} custom-call(f32[8,128,128]{2,1,0:T(8,128)} %fusion.387), custom_call_target="Cholesky" | custom-call | tf_op jit(solution)/shard_map/jit(cholesky)/cholesky | solution.py:96
  246.5 79.4 %custom-call.9 = f32[8,1,128,128]{2,3,1,0:T(8,128)S(1)} custom-call(f32[8,1,128,128]{3,2,1,0:T(8,128)} %select_bitcast_fusion.1), custom_call_target="InvertDiagBlocksLowerTriangular" | custom-call | tf_op jit(solution)/shard_map/triangular_solve/custom-call.0 | solution.py:98
  326.9 3.4 fusion.400
  333.6 94.7 %custom-call.10 = f32[8,128,128]{2,1,0:T(8,128)S(1)} custom-call(f32[8,128,128]{2,1,0:T(8,128)} %fusion.384), custom_call_target="Cholesky" | custom-call | tf_op jit(solution)/shard_map/jit(cholesky)/cholesky | solution.py:96
  428.6 78.6 %custom-call.11 = f32[8,1,128,128]{2,3,1,0:T(8,128)S(1)} custom-call(f32[8,1,128,128]{3,2,1,0:T(8,128)S(1)} %select_bitcast_fusion), custom_call_target="InvertDiagBlocksLowerTriangular" | custom-call | tf_op jit(solution)/shard_map/triangular_solve/custom-call.0 | solution.py:98
  508.2 3.4 convolution_convert_fusion
  512.3 4.6 all_to_all.36
  517.7 5.7 collective-permute-start.16
  523.4 3.9 collective-permute-start.17
  544.6 4.6 collective-permute-done.20
  556.0 12.1 %all-gather.5.cloned.1.call-done = bf16[6,6,512,128]{2,3,1,0:T(8,128)(2,1)} async-done(((bf16[6,6,256,128]{2,3,1,0:T(8,128)(2,1)}), bf16[6,6,512,128]{2,3,1,0:T(8,128)(2,1)}) %all-gather.5.cloned.1.call-update) | async-done | bytes 4718608 | tf_op jit(solution)/shard_map/all_gather | solution.py:156
  568.1 101.2 %while.56 = (s32[]{:T(128)}, f32[2,4,9,128,128]{4,3,2,1,0:T(8,128)}, s32[2]{0:T(128)}, bf16[6,6,512,128]{2,3,1,0:T(8,128)(2,1)}, bf16[6,6,3,512]{3,1,2,0:T(8,128...) while((s32[]{:T(128)}, ...), condition=%wide.region_6.9_spmd, body=%wide.region_5.8_spmd.sunk | while | flops 3137753088 | bytes 29859332 | solution.py:184
  578.4 6.6 copy.169
  595.2 3.4 fusion.474
  599.3 3.5 fusion.476
  603.6 3.4 fusion.478
  628.8 6.6 copy.169
  649.6 3.5 fusion.476
  653.9 3.4 fusion.478
  669.3 5.1 copy.149
  674.4 7.5 %all_to_all.37 = f32[8,9,128,128]{3,0,1,2:T(8,128)S(1)} all-to-all(f32[8,9,128,128]{3,0,1,2:T(8,128)S(1)} %copy.149), channel_id=1, replica_groups=mesh['box'=16,'col'=2] {'col'}, dimensions={2} | all-to-all | bytes 9437184 | tf_op jit(solution)/shard_map/all_to_all | solution.py:185
  (290 shorter events, 181.4 us)
Async XLA Ops:
  7.2 72.6 %all-gather.3.cloned.1.call-start = ((), (), s32[]{:S(2)}) async-start(), calls=%async_computation.2 | async-start | bytes 7077888 | tf_op jit(solution)/shard_map/all_gather | solution.py:123
  8.7 19.8 %collective-permute-start = (bf16[1,1,256,128]{2,3,1,0:T(8,128)(2,1)S(1)}, bf16[1,1,256,128]{2,3,1,0:T(8,128)(2,1)S(1)}, u32[]{:S(2)}, u32[]{:S(2)}) collective-permute-start(bf16[1,1,256,128]{2,3,1,0:T(8,128)(2,1)S(1)} %get-tuple-element.823), channel_id=1, source_target_pairs={{0,10},{2,12},{4,14},{6,16},{8,18},{10,20},{12,22},{14,24},{16,26}... | collective-permute-start | bytes 196616 | tf_op jit(solution)/shard_map/ppermute | solution.py:22
  14.7 15.2 %collective-permute-start.1 = (bf16[1,4,256,128]{2,3,1,0:T(8,128)(2,1)S(1)}, bf16[1,4,256,128]{2,3,1,0:T(8,128)(2,1)S(1)}, u32[]{:S(2)}, u32[]{:S(2)}) collective-permute-start(bf16[1,4,256,128]{2,3,1,0:T(8,128)(2,1)S(1)} %get-tuple-element.825), channel_id=1, source_target_pairs={{0,8},{2,10},{4,12},{6,14},{8,16},{10,18},{12,20},{14,22},{16,24},... | collective-permute-start | bytes 786440 | tf_op jit(solution)/shard_map/ppermute | solution.py:22
  18.2 14.4 %collective-permute-start.2 = (bf16[1,1,256,128]{2,3,1,0:T(8,128)(2,1)S(1)}, bf16[1,1,256,128]{2,3,1,0:T(8,128)(2,1)S(1)}, u32[]{:S(2)}, u32[]{:S(2)}) collective-permute-start(bf16[1,1,256,128]{2,3,1,0:T(8,128)(2,1)S(1)} %get-tuple-element.822), channel_id=1, source_target_pairs={{0,6},{2,8},{4,10},{6,12},{8,14},{10,16},{12,18},{14,20},{16,22},{... | collective-permute-start | bytes 196616 | tf_op jit(solution)/shard_map/ppermute | solution.py:22
  22.6 14.3 %collective-permute-start.3 = (bf16[4,1,256,128]{2,3,1,0:T(8,128)(2,1)S(1)}, bf16[4,1,256,128]{2,3,1,0:T(8,128)(2,1)S(1)}, u32[]{:S(2)}, u32[]{:S(2)}) collective-permute-start(bf16[4,1,256,128]{2,3,1,0:T(8,128)(2,1)S(1)} %get-tuple-element.827), channel_id=1, source_target_pairs={{0,2},{2,4},{4,6},{6,8},{8,10},{10,12},{12,14},{14,16},{16,18},{18... | collective-permute-start | bytes 786440 | tf_op jit(solution)/shard_map/ppermute | solution.py:22
  25.1 13.9 %collective-permute-start.4 = (bf16[4,1,256,128]{2,3,1,0:T(8,128)(2,1)S(1)}, bf16[4,1,256,128]{2,3,1,0:T(8,128)(2,1)S(1)}, u32[]{:S(2)}, u32[]{:S(2)}) collective-permute-start(bf16[4,1,256,128]{2,3,1,0:T(8,128)(2,1)S(1)} %get-tuple-element.826), channel_id=1, source_target_pairs={{2,0},{4,2},{6,4},{8,6},{10,8},{12,10},{14,12},{16,14},{18,16},{20... | collective-permute-start | bytes 786440 | tf_op jit(solution)/shard_map/ppermute | solution.py:22
  27.7 36.8 %copy-start.23 = (s32[16,9]{1,0:T(8,128)S(1)}, s32[16,9]{1,0:T(8,128)}, u32[]{:S(2)}) copy-start(s32[16,9]{1,0:T(8,128)} %param.66) | copy-start | bytes 1732
  28.6 10.4 %collective-permute-start.5 = (bf16[1,1,256,128]{2,3,1,0:T(8,128)(2,1)S(1)}, bf16[1,1,256,128]{2,3,1,0:T(8,128)(2,1)S(1)}, u32[]{:S(2)}, u32[]{:S(2)}) collective-permute-start(bf16[1,1,256,128]{2,3,1,0:T(8,128)(2,1)S(1)} %get-tuple-element.821), channel_id=1, source_target_pairs={{6,0},{8,2},{10,4},{12,6},{14,8},{16,10},{18,12},{20,14},{22,16},{... | collective-permute-start | bytes 196616 | tf_op jit(solution)/shard_map/ppermute | solution.py:22
  29.9 13.3 %collective-permute-start.6 = (bf16[1,4,256,128]{2,3,1,0:T(8,128)(2,1)S(1)}, bf16[1,4,256,128]{2,3,1,0:T(8,128)(2,1)S(1)}, u32[]{:S(2)}, u32[]{:S(2)}) collective-permute-start(bf16[1,4,256,128]{2,3,1,0:T(8,128)(2,1)S(1)} %get-tuple-element.824), channel_id=1, source_target_pairs={{8,0},{10,2},{12,4},{14,6},{16,8},{18,10},{20,12},{22,14},{24,16},... | collective-permute-start | bytes 786440 | tf_op jit(solution)/shard_map/ppermute | solution.py:22
  32.5 13.4 %collective-permute-start.7 = (bf16[1,1,256,128]{2,3,1,0:T(8,128)(2,1)S(1)}, bf16[1,1,256,128]{2,3,1,0:T(8,128)(2,1)S(1)}, u32[]{:S(2)}, u32[]{:S(2)}) collective-permute-start(bf16[1,1,256,128]{2,3,1,0:T(8,128)(2,1)S(1)} %get-tuple-element.820), channel_id=1, source_target_pairs={{10,0},{12,2},{14,4},{16,6},{18,8},{20,10},{22,12},{24,14},{26,16}... | collective-permute-start | bytes 196616 | tf_op jit(solution)/shard_map/ppermute | solution.py:22
  47.4 520.7 %all-gather.5.cloned.1.call-start = ((), (), s32[]{:S(2)}) async-start(), calls=%async_computation.3 | async-start | bytes 7077888 | tf_op jit(solution)/shard_map/all_gather | solution.py:156
  47.5 17.0 %collective-permute-start.8 = (bf16[1,1,3,512]{3,1,0,2:T(2,128)(2,1)S(1)}, bf16[1,1,3,512]{3,1,0,2:T(2,128)(2,1)S(1)}, u32[]{:S(2)}, u32[]{:S(2)}) collective-permute-start(bf16[1,1,3,512]{3,1,0,2:T(2,128)(2,1)S(1)} %get-tuple-element.831), channel_id=1, source_target_pairs={{0,10},{2,12},{4,14},{6,16},{8,18},{10,20},{12,22},{14,24},{16,26}... | collective-permute-start | bytes 9224 | tf_op jit(solution)/shard_map/ppermute | solution.py:22
  52.0 13.9 %collective-permute-start.9 = (bf16[1,4,3,512]{3,1,0,2:T(4,128)(2,1)S(1)}, bf16[1,4,3,512]{3,1,0,2:T(4,128)(2,1)S(1)}, u32[]{:S(2)}, u32[]{:S(2)}) collective-permute-start(bf16[1,4,3,512]{3,1,0,2:T(4,128)(2,1)S(1)} %get-tuple-element.833), channel_id=1, source_target_pairs={{0,8},{2,10},{4,12},{6,14},{8,16},{10,18},{12,20},{14,22},{16,24},... | collective-permute-start | bytes 36872 | tf_op jit(solution)/shard_map/ppermute | solution.py:22
  56.0 12.8 %collective-permute-start.10 = (bf16[1,1,3,512]{3,1,0,2:T(2,128)(2,1)S(1)}, bf16[1,1,3,512]{3,1,0,2:T(2,128)(2,1)S(1)}, u32[]{:S(2)}, u32[]{:S(2)}) collective-permute-start(bf16[1,1,3,512]{3,1,0,2:T(2,128)(2,1)S(1)} %get-tuple-element.830), channel_id=1, source_target_pairs={{0,6},{2,8},{4,10},{6,12},{8,14},{10,16},{12,18},{14,20},{16,22},{... | collective-permute-start | bytes 9224 | tf_op jit(solution)/shard_map/ppermute | solution.py:22
  57.3 15.9 %collective-permute-start.11 = (bf16[4,1,3,512]{3,1,0,2:T(2,128)(2,1)S(1)}, bf16[4,1,3,512]{3,1,0,2:T(2,128)(2,1)S(1)}, u32[]{:S(2)}, u32[]{:S(2)}) collective-permute-start(bf16[4,1,3,512]{3,1,0,2:T(2,128)(2,1)S(1)} %get-tuple-element.835), channel_id=1, source_target_pairs={{0,2},{2,4},{4,6},{6,8},{8,10},{10,12},{12,14},{14,16},{16,18},{18... | collective-permute-start | bytes 36872 | tf_op jit(solution)/shard_map/ppermute | solution.py:22
  61.3 12.0 %collective-permute-start.12 = (bf16[4,1,3,512]{3,1,0,2:T(2,128)(2,1)S(1)}, bf16[4,1,3,512]{3,1,0,2:T(2,128)(2,1)S(1)}, u32[]{:S(2)}, u32[]{:S(2)}) collective-permute-start(bf16[4,1,3,512]{3,1,0,2:T(2,128)(2,1)S(1)} %get-tuple-element.834), channel_id=1, source_target_pairs={{2,0},{4,2},{6,4},{8,6},{10,8},{12,10},{14,12},{16,14},{18,16},{20... | collective-permute-start | bytes 36872 | tf_op jit(solution)/shard_map/ppermute | solution.py:22
  64.6 8.9 %collective-permute-start.13 = (bf16[1,1,3,512]{3,1,0,2:T(2,128)(2,1)S(1)}, bf16[1,1,3,512]{3,1,0,2:T(2,128)(2,1)S(1)}, u32[]{:S(2)}, u32[]{:S(2)}) collective-permute-start(bf16[1,1,3,512]{3,1,0,2:T(2,128)(2,1)S(1)} %get-tuple-element.829), channel_id=1, source_target_pairs={{6,0},{8,2},{10,4},{12,6},{14,8},{16,10},{18,12},{20,14},{22,16},{... | collective-permute-start | bytes 9224 | tf_op jit(solution)/shard_map/ppermute | solution.py:22
  66.0 8.3 %collective-permute-start.14 = (bf16[1,4,3,512]{3,1,0,2:T(4,128)(2,1)S(1)}, bf16[1,4,3,512]{3,1,0,2:T(4,128)(2,1)S(1)}, u32[]{:S(2)}, u32[]{:S(2)}) collective-permute-start(bf16[1,4,3,512]{3,1,0,2:T(4,128)(2,1)S(1)} %get-tuple-element.832), channel_id=1, source_target_pairs={{8,0},{10,2},{12,4},{14,6},{16,8},{18,10},{20,12},{22,14},{24,16},... | collective-permute-start | bytes 36872 | tf_op jit(solution)/shard_map/ppermute | solution.py:22
  68.7 10.7 %collective-permute-start.15 = (bf16[1,1,3,512]{3,1,0,2:T(2,128)(2,1)S(1)}, bf16[1,1,3,512]{3,1,0,2:T(2,128)(2,1)S(1)}, u32[]{:S(2)}, u32[]{:S(2)}) collective-permute-start(bf16[1,1,3,512]{3,1,0,2:T(2,128)(2,1)S(1)} %get-tuple-element.828), channel_id=1, source_target_pairs={{10,0},{12,2},{14,4},{16,6},{18,8},{20,10},{22,12},{24,14},{26,16}... | collective-permute-start | bytes 9224 | tf_op jit(solution)/shard_map/ppermute | solution.py:22
  146.5 100.0 %copy-start = (f32[2,512,4,128]{1,3,2,0:T(8,128)}, f32[2,512,4,128]{1,3,2,0:T(8,128)S(1)}, u32[]{:S(2)}) copy-start(f32[2,512,4,128]{1,3,2,0:T(8,128)S(1)} %get-tuple-element.614) | copy-start | bytes 6291460
  146.5 98.9 %copy-start.17 = (pred[128,128]{1,0:T(8,128)(4,1)S(1)}, pred[128,128]{1,0:T(8,128)(4,1)}, u32[]{:S(2)}) copy-start(pred[128,128]{1,0:T(8,128)(4,1)} %iota_compare_fusion.3) | copy-start | bytes 49156
  146.5 99.0 %copy-start.16 = (pred[128,128]{1,0:T(8,128)(4,1)S(1)}, pred[128,128]{1,0:T(8,128)(4,1)}, u32[]{:S(2)}) copy-start(pred[128,128]{1,0:T(8,128)(4,1)} %iota_compare_fusion.2) | copy-start | bytes 49156
  147.1 178.8 %copy-start.9 = (f32[128,128]{1,0:T(8,128)S(1)}, f32[128,128]{1,0:T(8,128)}, u32[]{:S(2)}) copy-start(f32[128,128]{1,0:T(8,128)} %fusion.390) | copy-start | bytes 196612
  517.7 16.7 %collective-permute-start.16 = (bf16[1,1,256,128]{2,3,1,0:T(8,128)(2,1)S(1)}, bf16[1,1,256,128]{2,3,1,0:T(8,128)(2,1)S(1)}, u32[]{:S(2)}, u32[]{:S(2)}) collective-permute-start(bf16[1,1,256,128]{2,3,1,0:T(8,128)(2,1)S(1)} %get-tuple-element.815), channel_id=1, source_target_pairs={{0,10},{2,12},{4,14},{6,16},{8,18},{10,20},{12,22},{14,24},{16,26}... | collective-permute-start | bytes 196616 | tf_op jit(solution)/shard_map/ppermute | solution.py:22
  523.4 12.3 %collective-permute-start.17 = (bf16[1,4,256,128]{2,3,1,0:T(8,128)(2,1)S(1)}, bf16[1,4,256,128]{2,3,1,0:T(8,128)(2,1)S(1)}, u32[]{:S(2)}, u32[]{:S(2)}) collective-permute-start(bf16[1,4,256,128]{2,3,1,0:T(8,128)(2,1)S(1)} %get-tuple-element.817), channel_id=1, source_target_pairs={{0,8},{2,10},{4,12},{6,14},{8,16},{10,18},{12,20},{14,22},{16,24},... | collective-permute-start | bytes 786440 | tf_op jit(solution)/shard_map/ppermute | solution.py:22
  527.6 27.2 %copy-start.4 = (bf16[8,512,128]{2,0,1:T(8,128)(2,1)S(1)}, bf16[8,512,128]{2,0,1:T(8,128)(2,1)}, u32[]{:S(2)}) copy-start(bf16[8,512,128]{2,0,1:T(8,128)(2,1)} %copy-done.3) | copy-start | bytes 3145732
  527.7 10.7 %collective-permute-start.18 = (bf16[1,1,256,128]{2,3,1,0:T(8,128)(2,1)S(1)}, bf16[1,1,256,128]{2,3,1,0:T(8,128)(2,1)S(1)}, u32[]{:S(2)}, u32[]{:S(2)}) collective-permute-start(bf16[1,1,256,128]{2,3,1,0:T(8,128)(2,1)S(1)} %get-tuple-element.814), channel_id=1, source_target_pairs={{0,6},{2,8},{4,10},{6,12},{8,14},{10,16},{12,18},{14,20},{16,22},{... | collective-permute-start | bytes 196616 | tf_op jit(solution)/shard_map/ppermute | solution.py:22
  530.8 13.8 %collective-permute-start.19 = (bf16[4,1,256,128]{2,3,1,0:T(8,128)(2,1)S(1)}, bf16[4,1,256,128]{2,3,1,0:T(8,128)(2,1)S(1)}, u32[]{:S(2)}, u32[]{:S(2)}) collective-permute-start(bf16[4,1,256,128]{2,3,1,0:T(8,128)(2,1)S(1)} %get-tuple-element.819), channel_id=1, source_target_pairs={{0,2},{2,4},{4,6},{6,8},{8,10},{10,12},{12,14},{14,16},{16,18},{18... | collective-permute-start | bytes 786440 | tf_op jit(solution)/shard_map/ppermute | solution.py:22
  533.1 16.1 %collective-permute-start.20 = (bf16[4,1,256,128]{2,3,1,0:T(8,128)(2,1)S(1)}, bf16[4,1,256,128]{2,3,1,0:T(8,128)(2,1)S(1)}, u32[]{:S(2)}, u32[]{:S(2)}) collective-permute-start(bf16[4,1,256,128]{2,3,1,0:T(8,128)(2,1)S(1)} %get-tuple-element.818), channel_id=1, source_target_pairs={{2,0},{4,2},{6,4},{8,6},{10,8},{12,10},{14,12},{16,14},{18,16},{20... | collective-permute-start | bytes 786440 | tf_op jit(solution)/shard_map/ppermute | solution.py:22
  534.4 14.8 %collective-permute-start.21 = (bf16[1,1,256,128]{2,3,1,0:T(8,128)(2,1)S(1)}, bf16[1,1,256,128]{2,3,1,0:T(8,128)(2,1)S(1)}, u32[]{:S(2)}, u32[]{:S(2)}) collective-permute-start(bf16[1,1,256,128]{2,3,1,0:T(8,128)(2,1)S(1)} %get-tuple-element.813), channel_id=1, source_target_pairs={{6,0},{8,2},{10,4},{12,6},{14,8},{16,10},{18,12},{20,14},{22,16},{... | collective-permute-start | bytes 196616 | tf_op jit(solution)/shard_map/ppermute | solution.py:22
  535.7 15.9 %collective-permute-start.22 = (bf16[1,4,256,128]{2,3,1,0:T(8,128)(2,1)S(1)}, bf16[1,4,256,128]{2,3,1,0:T(8,128)(2,1)S(1)}, u32[]{:S(2)}, u32[]{:S(2)}) collective-permute-start(bf16[1,4,256,128]{2,3,1,0:T(8,128)(2,1)S(1)} %get-tuple-element.816), channel_id=1, source_target_pairs={{8,0},{10,2},{12,4},{14,6},{16,8},{18,10},{20,12},{22,14},{24,16},... | collective-permute-start | bytes 786440 | tf_op jit(solution)/shard_map/ppermute | solution.py:22
  538.3 15.0 %collective-permute-start.23 = (bf16[1,1,256,128]{2,3,1,0:T(8,128)(2,1)S(1)}, bf16[1,1,256,128]{2,3,1,0:T(8,128)(2,1)S(1)}, u32[]{:S(2)}, u32[]{:S(2)}) collective-permute-start(bf16[1,1,256,128]{2,3,1,0:T(8,128)(2,1)S(1)} %get-tuple-element.812), channel_id=1, source_target_pairs={{10,0},{12,2},{14,4},{16,6},{18,8},{20,10},{22,12},{24,14},{26,16}... | collective-permute-start | bytes 196616 | tf_op jit(solution)/shard_map/ppermute | solution.py:22
  (36 other events, 239.6 us)
Sparse Core Ops, SparseCore 0:
  47.5 13.4 all-gather.2
  554.9 13.1 all-gather.4
where the time goes:
time: 697 us; the launch traced here: 692 us
  other arithmetic  366 us (53%)
  matrix products  126 us (18%)
  starting transfers between devices  60.5 us (9%)
  local copies, waits for them, and re-layouts  47.9 us (7%)
  waiting for transfers between devices  39.8 us (6%)
  loops' own time  24.6 us (4%)
  between operations  15.1 us (2%)
  blocking collectives  12.1 us (2%)
    another operation x7, other arithmetic, apply_inverse(): lower_factor = jnp.linalg.cholesky(gram_sum)  191 us
    another operation x5, other arithmetic, apply_inverse(): lax.linalg.triangular_solve(lower_factor, identity, left_side=True, lower...  160 us
    dot_general x18, matrix products, couple_full(): jnp.einsum('brj,bjs->brs', projected, near_basis, preferred_element_type=...  60.8 us
    ppermute x24, starting transfers between devices, from_behind(): lax.ppermute(value, axis, [(source, source + steps) for source in range(i...  60.5 us
    dot_general x18, matrix products, sketch_full(): jnp.einsum('bij,bjr->ibr', block_vals, near_omega, preferred_element_type...  52.3 us
    ppermute x24, waiting for transfers between devices, from_behind(): lax.ppermute(value, axis, [(source, source + steps) for source in range(i...  27.7 us
    another operation x5, local copies, waits for them, and re-layouts  14.5 us
  transfers between devices with their start and end apart: 26, of which 11 were waited for; matrix products, arithmetic and copies ran while one was open for 3% of the time, Pallas kernels for 0%

commit v1 on v0

--- a/solution.py
+++ b/solution.py
@@ -3,6 +3,8 @@
 import jax
 import jax.numpy as jnp
 from jax import lax
+from jax.experimental import pallas as pl
+from jax.experimental.pallas import tpu as pltpu
 from jax.sharding import PartitionSpec as P
 
 lift_scale = 0.25
@@ -92,18 +94,119 @@
     return row_block[1 + offset_x : 1 + offset_x + tile_side]
 
 
-def apply_inverse(gram_sum, sketch_t):
-    lower_factor = jnp.linalg.cholesky(gram_sum)
-    identity = jnp.broadcast_to(jnp.eye(gram_sum.shape[1], dtype=gram_sum.dtype), gram_sum.shape)
-    inverse_lower = lax.linalg.triangular_solve(lower_factor, identity, left_side=True, lower=True)
-    return jnp.einsum("brs,bsm->brm", inverse_lower, sketch_t, precision=lax.Precision.HIGHEST)
-
-
-def orthonormal_local(sketch_t, box_points):
-    gram_sum = (
-        jnp.einsum("brm,bsm->brs", sketch_t, sketch_t, precision=lax.Precision.HIGHEST) / box_points
-    )
-    return apply_inverse(gram_sum, sketch_t)
+PANEL = 8
+BLOCK = 32
+
+def lane_copy(value, lane):
+    return jnp.broadcast_to(value[:, lane:lane+1], value.shape)
+
+def three_parts(value):
+    first = value.astype(jnp.bfloat16)
+    rest = value - first.astype(jnp.float32)
+    second = rest.astype(jnp.bfloat16)
+    third = (rest - second.astype(jnp.float32)).astype(jnp.bfloat16)
+    return first, second, third
+
+def factor_panel(rows, base):
+    schur = [[lane_copy(rows[base + i], base + j) for j in range(i + 1)] for i in range(PANEL)]
+    inverse_pivots, multipliers = [], [[None] * PANEL for _ in range(PANEL)]
+    for k in range(PANEL):
+        inverse_pivots.append(1.0 / schur[k][k])
+        for i in range(k + 1, PANEL):
+            multipliers[i][k] = schur[i][k] * inverse_pivots[k]
+        for i in range(k + 1, PANEL):
+            for j in range(k + 1, i + 1):
+                schur[i][j] = schur[i][j] - multipliers[i][k] * schur[j][k]
+    unit = [[None] * PANEL for _ in range(PANEL)]
+    for i in range(PANEL):
+        for j in range(i):
+            total = multipliers[i][j]
+            for t in range(j + 1, i):
+                total = total + multipliers[i][t] * unit[t][j]
+            unit[i][j] = -total
+    return inverse_pivots, unit
+
+def invert_factors(work, pivots, weights):
+    rank, batch, _ = work.shape
+    lanes = lax.broadcasted_iota(jnp.int32, (batch, rank), 1)
+    square_rows = lax.broadcasted_iota(jnp.int32, (rank, rank), 0)
+    square_lanes = lax.broadcasted_iota(jnp.int32, (rank, rank), 1)
+
+    def block_step(block, carry):
+        first = block * BLOCK
+        back = lax.rem(rank - first, rank)
+        rows = [pltpu.roll(work[first + r], back, 1) for r in range(BLOCK)]
+        for base in range(0, BLOCK, PANEL):
+            inverse_pivots, unit = factor_panel(rows, base)
+            inside = (lanes >= base) & (lanes < base + PANEL)
+            held_rows, scaled_rows = [], []
+            for k in range(PANEL):
+                full = rows[base + k]
+                for j in range(k):
+                    full = full + unit[k][j] * rows[base + j]
+                scaled = full * inverse_pivots[k]
+                held = jnp.where(inside, 0.0, full)
+                for j in range(k):
+                    held = jnp.where(lanes == base + j, unit[k][j], held)
+                held = jnp.where(lanes == base + k, 1.0, held)
+                held_rows.append(held)
+                scaled_rows.append(scaled)
+            for t in range(base + PANEL, BLOCK):
+                row = jnp.where(inside, 0.0, rows[t])
+                for k in range(PANEL):
+                    row = row - lane_copy(scaled_rows[k], t) * held_rows[k]
+                rows[t] = row
+            for k in range(PANEL):
+                at = base + k
+                kept = jnp.where((lanes > at) & (lanes < BLOCK), 0.0, held_rows[k])
+                turned = pltpu.roll(kept, first, 1)
+                pivots[at] = turned
+                weights[at] = pltpu.roll(scaled_rows[k], first, 1)
+                work[first + at] = jnp.where(lanes <= first + at, turned, 0.0) * lax.sqrt(inverse_pivots[k])
+
+        @pl.when(first + BLOCK < rank)
+        def _():
+            below = square_rows >= first + BLOCK
+            inside = (square_lanes >= first) & (square_lanes < first + BLOCK)
+            for b in range(batch):
+                a1, a2, a3 = three_parts(weights[:, b, :])
+                b1, b2, b3 = three_parts(pivots[:, b, :])
+                left = jnp.concatenate([a1, a1, a2, a2, a1, a3], axis=0)
+                right = jnp.concatenate([b1, b2, b1, b2, b3, b1], axis=0)
+                change = lax.dot_general(left, right, (((0,), (0,)), ((), ())), preferred_element_type=jnp.float32)
+                now = work[:, b, :]
+                work[:, b, :] = jnp.where(below, jnp.where(inside, 0.0, now) - change, now)
+
+        return carry
+
+    lax.fori_loop(0, rank // BLOCK, block_step, 0)
+
+def ortho_kernel(y_ref, out_ref, work, held, pivots, weights):
+    batch, points, rank = y_ref.shape
+    for turn, source in enumerate((y_ref, held)):
+        for b in range(batch):
+            data = source[b]
+            work[:, b, :] = lax.dot_general(data, data, (((0,), (0,)), ((), ())), precision=lax.Precision.HIGHEST, preferred_element_type=jnp.float32) * (1.0 / points)
+        invert_factors(work, pivots, weights)
+        for b in range(batch):
+            data = lax.dot_general(source[b], work[:, b, :], (((1,), (1,)), ((), ())), precision=lax.Precision.HIGHEST, preferred_element_type=jnp.float32)
+            if turn == 0:
+                held[b] = data
+            else:
+                out_ref[b] = data.astype(jnp.bfloat16)
+
+def orthonormal(y):
+    batch, points, rank = y.shape
+    return pl.pallas_call(
+        ortho_kernel,
+        out_shape=jax.ShapeDtypeStruct(y.shape, jnp.bfloat16),
+        in_specs=[pl.BlockSpec(memory_space=pltpu.VMEM)],
+        out_specs=pl.BlockSpec(memory_space=pltpu.VMEM),
+        scratch_shapes=[pltpu.VMEM((rank, batch, rank), jnp.float32), pltpu.VMEM(y.shape, jnp.float32),
+            pltpu.VMEM((BLOCK, batch, rank), jnp.float32), pltpu.VMEM((BLOCK, batch, rank), jnp.float32)],
+        compiler_params=pltpu.CompilerParams(vmem_limit_bytes=48 << 20),
+        name="orthonormal",
+    )(y)
 
 
 def body(points, sketch, near_mask):
@@ -144,11 +247,10 @@
         return running
 
     blocks = lax.map(sketch_full, own_rows)
-    sketch_t = jnp.transpose(blocks, (0, 2, 3, 1)).reshape(
-        rows_half * tile_side, skel_rank, box_points
+    sketched = jnp.transpose(blocks, (0, 2, 1, 3)).reshape(
+        rows_half * tile_side, box_points, skel_rank
     )
-    own_t = orthonormal_local(orthonormal_local(sketch_t, box_points), box_points)
-    own_basis = jnp.transpose(own_t.astype(jnp.bfloat16), (0, 2, 1))
+    own_basis = orthonormal(sketched)
     basis_out = lax.all_to_all(own_basis, "col", split_axis=1, concat_axis=0, tiled=True)
     ext_basis = neighbours(
         (basis_out.reshape(tile_side, tile_side, half_points, skel_rank),), tile_side, grid_side

time: 697 us -> 360 us (0.52)
  other arithmetic: 366 us -> 13 us
  Pallas kernels: 0 us -> 28.9 us
  matrix products: 126 us -> 113 us
    another operation x15 -> x3, other arithmetic: 353 us -> 2.6 us  [the longest x7 191 us: apply_inverse(): lower_factor = jnp.linalg.cholesky(gram_sum)]
    pallas_call x0 -> x1, Pallas kernels: none -> 28.9 us  [orthonormal(): pl.pallas_call(ortho_kernel, out_shape=jax.ShapeDtypeStruct(y.shape, jnp....]
    dot_general x4 -> x0, matrix products: 11.1 us -> none  [the longest x2 6.86 us: apply_inverse(): jnp.einsum('brs,bsm->brm', inverse_lower, sketch_t, precision=lax.Precisi...]
  transfers between devices with their start and end apart: 26 -> 26, of which waited for: 11 -> 11; matrix products, arithmetic and copies ran while one was open for 3% -> 4% of each run, Pallas kernels for 0% -> 0%
where the time goes in v1:
time: 360 us; the launch traced here: 355 us
  matrix products  113 us (31%)
  starting transfers between devices  60.4 us (17%)
  local copies, waits for them, and re-layouts  49.5 us (14%)
  waiting for transfers between devices  39.9 us (11%)
  Pallas kernels  28.9 us (8%)
  loops' own time  23.2 us (6%)
  between operations  15.1 us (4%)
  other arithmetic  13 us (4%)
  blocking collectives  12.1 us (3%)
    dot_general x18, matrix products, couple_full(): jnp.einsum('brj,bjs->brs', projected, near_basis, preferred_element_type=...  60.8 us
    ppermute x24, starting transfers between devices, from_behind(): lax.ppermute(value, axis, [(source, source + steps) for source in range(i...  60.3 us
    dot_general x18, matrix products, sketch_full(): jnp.einsum('bij,bjr->ibr', block_vals, near_omega, preferred_element_type...  52.3 us
    pallas_call x1, Pallas kernels, orthonormal(): pl.pallas_call(ortho_kernel, out_shape=jax.ShapeDtypeStruct(y.shape, jnp....  28.9 us
    ppermute x24, waiting for transfers between devices, from_behind(): lax.ppermute(value, axis, [(source, source + steps) for source in range(i...  27.8 us
    another operation x5, local copies, waits for them, and re-layouts  14.4 us
    another operation x1, loops' own time, body(): blocks = lax.map(sketch_full, own_rows)  12.1 us
    all_gather x1, waiting for transfers between devices, body(): basis_full = lax.all_gather(ext_basis, 'col', axis=2, tiled=True)  12 us
  transfers between devices with their start and end apart: 26, of which 11 were waited for; matrix products, arithmetic and copies ran while one was open for 4% of the time, Pallas kernels for 0%

profile of v1, /device:TPU:0, one launch (start us, length us, event | category | flops | bytes accessed | tf_op | source)
XLA Modules:
  0.0 355.1 jit_solution(17911362778429157787)
XLA Ops:
  8.7 5.9 %collective-permute-start = (bf16[1,1,256,128]{2,3,1,0:T(8,128)(2,1)S(1)}, bf16[1,1,256,128]{2,3,1,0:T(8,128)(2,1)S(1)}, u32[]{:S(2)}, u32[]{:S(2)}) collective-permute-start(bf16[1,1,256,128]{2,3,1,0:T(8,128)(2,1)S(1)} %get-tuple-element.807), channel_id=1, source_target_pairs={{0,10},{2,12},{4,14},{6,16},{8,18},{10,20},{12,22},{14,24},{16,26}... | collective-permute-start | bytes 196616 | tf_op jit(solution)/shard_map/ppermute | solution.py:24
  14.7 3.5 collective-permute-start.1
  18.2 4.4 %collective-permute-start.2 = (bf16[1,1,256,128]{2,3,1,0:T(8,128)(2,1)S(1)}, bf16[1,1,256,128]{2,3,1,0:T(8,128)(2,1)S(1)}, u32[]{:S(2)}, u32[]{:S(2)}) collective-permute-start(bf16[1,1,256,128]{2,3,1,0:T(8,128)(2,1)S(1)} %get-tuple-element.806), channel_id=1, source_target_pairs={{0,6},{2,8},{4,10},{6,12},{8,14},{10,16},{12,18},{14,20},{16,22},{... | collective-permute-start | bytes 196616 | tf_op jit(solution)/shard_map/ppermute | solution.py:24
  39.2 4.0 %collective-permute-done.6 = bf16[1,4,256,128]{2,3,1,0:T(8,128)(2,1)S(1)} collective-permute-done((bf16[1,4,256,128]{2,3,1,0:T(8,128)(2,1)S(1)}, bf16[1,4,256,128]{2,3,1,0:T(8,128)(2,1)S(1)}, u32[]{:S(2)}, u32[]{:S(2)}) %collective-permute-start.6) | collective-permute-done | bytes 262176 | tf_op jit(solution)/shard_map/ppermute | solution.py:24
  47.5 4.4 %collective-permute-start.8 = (bf16[1,1,3,512]{3,1,0,2:T(2,128)(2,1)S(1)}, bf16[1,1,3,512]{3,1,0,2:T(2,128)(2,1)S(1)}, u32[]{:S(2)}, u32[]{:S(2)}) collective-permute-start(bf16[1,1,3,512]{3,1,0,2:T(2,128)(2,1)S(1)} %get-tuple-element.815), channel_id=1, source_target_pairs={{0,10},{2,12},{4,14},{6,16},{8,18},{10,20},{12,22},{14,24},{16,26}... | collective-permute-start | bytes 9224 | tf_op jit(solution)/shard_map/ppermute | solution.py:24
  51.9 3.9 %collective-permute-start.9 = (bf16[1,4,3,512]{3,1,0,2:T(4,128)(2,1)S(1)}, bf16[1,4,3,512]{3,1,0,2:T(4,128)(2,1)S(1)}, u32[]{:S(2)}, u32[]{:S(2)}) collective-permute-start(bf16[1,4,3,512]{3,1,0,2:T(4,128)(2,1)S(1)} %get-tuple-element.817), channel_id=1, source_target_pairs={{0,8},{2,10},{4,12},{6,14},{8,16},{10,18},{12,20},{14,22},{16,24},... | collective-permute-start | bytes 36872 | tf_op jit(solution)/shard_map/ppermute | solution.py:24
  57.1 4.0 %collective-permute-start.11 = (bf16[4,1,3,512]{3,1,0,2:T(2,128)(2,1)S(1)}, bf16[4,1,3,512]{3,1,0,2:T(2,128)(2,1)S(1)}, u32[]{:S(2)}, u32[]{:S(2)}) collective-permute-start(bf16[4,1,3,512]{3,1,0,2:T(2,128)(2,1)S(1)} %get-tuple-element.819), channel_id=1, source_target_pairs={{0,2},{2,4},{4,6},{6,8},{8,10},{10,12},{12,14},{14,16},{16,18},{18... | collective-permute-start | bytes 36872 | tf_op jit(solution)/shard_map/ppermute | solution.py:24
  72.3 4.9 %collective-permute-done.15 = bf16[1,1,3,512]{3,1,0,2:T(2,128)(2,1)S(1)} collective-permute-done((bf16[1,1,3,512]{3,1,0,2:T(2,128)(2,1)S(1)}, bf16[1,1,3,512]{3,1,0,2:T(2,128)(2,1)S(1)}, u32[]{:S(2)}, u32[]{:S(2)}) %collective-permute-start.15) | collective-permute-done | bytes 3104 | tf_op jit(solution)/shard_map/ppermute | solution.py:24
  77.5 66.7 %while.55 = (s32[]{:T(128)}, f32[2,512,4,128]{1,3,2,0:T(8,128)S(1)}, s32[2]{0:T(128)S(1)}, bf16[6,6,512,128]{2,3,1,0:T(8,128)(2,1)}, bf16[6,6,3,512]{3,1,2,0:T(8...) while((s32[]{:T(128)}, ...), condition=%wide.region_2.0_spmd, body=%wide.region_1.0_spmd.sunk | while | flops 2535280640 | bytes 40105004 | solution.py:249
  84.5 3.4 fusion.437
  117.9 3.4 fusion.437
  147.5 28.9 %orthonormal.1 = bf16[8,512,128]{2,1,0:T(8,128)(2,1)S(1)} custom-call(f32[8,512,128]{2,1,0:T(8,128)S(1)} %bitcast.494), custom_call_target="tpu_custom_call" | custom-call | tf_op jit(solution)/shard_map/orthonormal/pallas_call | solution.py:200
  177.1 4.6 %all_to_all.36 = bf16[8,512,128]{2,0,1:T(8,128)(2,1)S(1)} all-to-all(bf16[8,512,128]{2,0,1:T(8,128)(2,1)S(1)} %copy.85), channel_id=1, replica_groups=mesh['box'=16,'col'=2] {'col'}, dimensions={1} | all-to-all | bytes 2097152 | tf_op jit(solution)/shard_map/all_to_all | solution.py:254
  182.4 5.7 %collective-permute-start.16 = (bf16[1,1,256,128]{2,3,1,0:T(8,128)(2,1)S(1)}, bf16[1,1,256,128]{2,3,1,0:T(8,128)(2,1)S(1)}, u32[]{:S(2)}, u32[]{:S(2)}) collective-permute-start(bf16[1,1,256,128]{2,3,1,0:T(8,128)(2,1)S(1)} %get-tuple-element.799), channel_id=1, source_target_pairs={{0,10},{2,12},{4,14},{6,16},{8,18},{10,20},{12,22},{14,24},{16,26}... | collective-permute-start | bytes 196616 | tf_op jit(solution)/shard_map/ppermute | solution.py:24
  188.1 3.9 %collective-permute-start.17 = (bf16[1,4,256,128]{2,3,1,0:T(8,128)(2,1)S(1)}, bf16[1,4,256,128]{2,3,1,0:T(8,128)(2,1)S(1)}, u32[]{:S(2)}, u32[]{:S(2)}) collective-permute-start(bf16[1,4,256,128]{2,3,1,0:T(8,128)(2,1)S(1)} %get-tuple-element.801), channel_id=1, source_target_pairs={{0,8},{2,10},{4,12},{6,14},{8,16},{10,18},{12,20},{14,22},{16,24},... | collective-permute-start | bytes 786440 | tf_op jit(solution)/shard_map/ppermute | solution.py:24
  209.2 4.7 %collective-permute-done.20 = bf16[4,1,256,128]{2,3,1,0:T(8,128)(2,1)S(1)} collective-permute-done((bf16[4,1,256,128]{2,3,1,0:T(8,128)(2,1)S(1)}, bf16[4,1,256,128]{2,3,1,0:T(8,128)(2,1)S(1)}, u32[]{:S(2)}, u32[]{:S(2)}) %collective-permute-start.20) | collective-permute-done | bytes 262176 | tf_op jit(solution)/shard_map/ppermute | solution.py:24
  220.8 12.0 %all-gather.5.cloned.1.call-done = bf16[6,6,512,128]{2,3,1,0:T(8,128)(2,1)} async-done(((bf16[6,6,256,128]{2,3,1,0:T(8,128)(2,1)}), bf16[6,6,512,128]{2,3,1,0:T(8,128)(2,1)}) %all-gather.5.cloned.1.call-update) | async-done | bytes 4718608 | tf_op jit(solution)/shard_map/all_gather | solution.py:258
  232.8 99.5 %while.56 = (s32[]{:T(128)}, f32[2,4,9,128,128]{4,3,2,1,0:T(8,128)}, s32[2]{0:T(128)}, bf16[6,6,512,128]{2,3,1,0:T(8,128)(2,1)}, bf16[6,6,3,512]{3,1,2,0:T(8,128...) while((s32[]{:T(128)}, ...), condition=%wide.region_4.0_spmd, body=%wide.region_3.0_spmd.sunk | while | flops 3137753088 | bytes 29859332 | solution.py:286
  242.2 6.6 %copy.104 = bf16[6,6,512,128]{3,2,1,0:T(8,128)(2,1)} copy(bf16[6,6,512,128]{2,3,1,0:T(8,128)(2,1)} %get-tuple-element.1189) | data formatting | bytes 9437184 | tf_op jit(solution)/shard_map
  255.5 3.3 fusion.454
  258.9 3.4 fusion.456
  263.0 3.5 fusion.458
  267.3 3.4 fusion.460
  277.6 3.3 fusion.465
  291.8 6.6 %copy.104 = bf16[6,6,512,128]{3,2,1,0:T(8,128)(2,1)} copy(bf16[6,6,512,128]{2,3,1,0:T(8,128)(2,1)} %get-tuple-element.1189) | data formatting | bytes 9437184 | tf_op jit(solution)/shard_map
  305.1 3.3 fusion.454
  308.5 3.4 fusion.456
  312.6 3.6 %fusion.458 = f32[4,9,128,128]{3,2,0,1:T(8,128)S(1)} fusion(f32[4,9,128,128]{3,2,0,1:T(8,128)S(1)} %fusion.456, f32[512,512]{1,0:T(8,128)S(1)} %fusion.457, f32[4,512]{1,0:T(4,128)} %get-tuple-element.1082, f32[4,512]{1,0:T(4,128)} %get-tuple-element.1083, f32[4,512]{1,0:T(4,128)} %get-tuple-element.1084, f32[4,512]{1,0:T(4,128)} %copy-done.11, ...), kind=kOutput, calls=%fused_computation.362.clone.1 | convolution fusion | flops 349503488 | bytes 2411008 | tf_op jit(solution)/shard_map/while/body/eval_jaxpr/brj,bjs->brs/dot_general | solution.py:277
  316.9 3.4 fusion.460
  327.2 3.3 fusion.465
  332.3 5.1 %copy.91 = f32[8,9,128,128]{3,0,1,2:T(8,128)S(1)} copy(f32[8,9,128,128]{3,2,1,0:T(8,128)} %bitcast.505) | data formatting | bytes 9437184 | tf_op jit(solution)/shard_map/reshape | solution.py:286
  337.4 7.5 %all_to_all.37 = f32[8,9,128,128]{3,0,1,2:T(8,128)S(1)} all-to-all(f32[8,9,128,128]{3,0,1,2:T(8,128)S(1)} %copy.91), channel_id=1, replica_groups=mesh['box'=16,'col'=2] {'col'}, dimensions={2} | all-to-all | bytes 9437184 | tf_op jit(solution)/shard_map/all_to_all | solution.py:287
  (263 shorter events, 155.4 us)
Async XLA Ops:
  7.2 19.2 %copy-start.21 = (s32[4]{0:T(128)S(1)}, s32[4]{0:T(128)}, u32[]{:S(2)}) copy-start(s32[4]{0:T(128)} %constant.952.clone.1) | copy-start | bytes 52
  7.2 70.3 %all-gather.3.cloned.1.call-start = ((), (), s32[]{:S(2)}) async-start(), calls=%async_computation.2 | async-start | bytes 7077888 | tf_op jit(solution)/shard_map/all_gather | solution.py:226
  8.7 19.8 %collective-permute-start = (bf16[1,1,256,128]{2,3,1,0:T(8,128)(2,1)S(1)}, bf16[1,1,256,128]{2,3,1,0:T(8,128)(2,1)S(1)}, u32[]{:S(2)}, u32[]{:S(2)}) collective-permute-start(bf16[1,1,256,128]{2,3,1,0:T(8,128)(2,1)S(1)} %get-tuple-element.807), channel_id=1, source_target_pairs={{0,10},{2,12},{4,14},{6,16},{8,18},{10,20},{12,22},{14,24},{16,26}... | collective-permute-start | bytes 196616 | tf_op jit(solution)/shard_map/ppermute | solution.py:24
  14.7 15.2 %collective-permute-start.1 = (bf16[1,4,256,128]{2,3,1,0:T(8,128)(2,1)S(1)}, bf16[1,4,256,128]{2,3,1,0:T(8,128)(2,1)S(1)}, u32[]{:S(2)}, u32[]{:S(2)}) collective-permute-start(bf16[1,4,256,128]{2,3,1,0:T(8,128)(2,1)S(1)} %get-tuple-element.809), channel_id=1, source_target_pairs={{0,8},{2,10},{4,12},{6,14},{8,16},{10,18},{12,20},{14,22},{16,24},... | collective-permute-start | bytes 786440 | tf_op jit(solution)/shard_map/ppermute | solution.py:24
  18.2 14.2 %collective-permute-start.2 = (bf16[1,1,256,128]{2,3,1,0:T(8,128)(2,1)S(1)}, bf16[1,1,256,128]{2,3,1,0:T(8,128)(2,1)S(1)}, u32[]{:S(2)}, u32[]{:S(2)}) collective-permute-start(bf16[1,1,256,128]{2,3,1,0:T(8,128)(2,1)S(1)} %get-tuple-element.806), channel_id=1, source_target_pairs={{0,6},{2,8},{4,10},{6,12},{8,14},{10,16},{12,18},{14,20},{16,22},{... | collective-permute-start | bytes 196616 | tf_op jit(solution)/shard_map/ppermute | solution.py:24
  22.6 14.3 %collective-permute-start.3 = (bf16[4,1,256,128]{2,3,1,0:T(8,128)(2,1)S(1)}, bf16[4,1,256,128]{2,3,1,0:T(8,128)(2,1)S(1)}, u32[]{:S(2)}, u32[]{:S(2)}) collective-permute-start(bf16[4,1,256,128]{2,3,1,0:T(8,128)(2,1)S(1)} %get-tuple-element.811), channel_id=1, source_target_pairs={{0,2},{2,4},{4,6},{6,8},{8,10},{10,12},{12,14},{14,16},{16,18},{18... | collective-permute-start | bytes 786440 | tf_op jit(solution)/shard_map/ppermute | solution.py:24
  25.1 14.1 %collective-permute-start.4 = (bf16[4,1,256,128]{2,3,1,0:T(8,128)(2,1)S(1)}, bf16[4,1,256,128]{2,3,1,0:T(8,128)(2,1)S(1)}, u32[]{:S(2)}, u32[]{:S(2)}) collective-permute-start(bf16[4,1,256,128]{2,3,1,0:T(8,128)(2,1)S(1)} %get-tuple-element.810), channel_id=1, source_target_pairs={{2,0},{4,2},{6,4},{8,6},{10,8},{12,10},{14,12},{16,14},{18,16},{20... | collective-permute-start | bytes 786440 | tf_op jit(solution)/shard_map/ppermute | solution.py:24
  27.7 19.7 %copy-start.15 = (bf16[16,3,512]{2,0,1:T(8,128)(2,1)S(1)}, bf16[16,3,512]{2,0,1:T(8,128)(2,1)}, u32[]{:S(2)}) copy-start(bf16[16,3,512]{2,0,1:T(8,128)(2,1)} %param.61) | copy-start | bytes 147460
  27.7 34.8 %copy-start.20 = (s32[16,9]{1,0:T(8,128)S(1)}, s32[16,9]{1,0:T(8,128)}, u32[]{:S(2)}) copy-start(s32[16,9]{1,0:T(8,128)} %param.63) | copy-start | bytes 1732
  28.5 10.6 %collective-permute-start.5 = (bf16[1,1,256,128]{2,3,1,0:T(8,128)(2,1)S(1)}, bf16[1,1,256,128]{2,3,1,0:T(8,128)(2,1)S(1)}, u32[]{:S(2)}, u32[]{:S(2)}) collective-permute-start(bf16[1,1,256,128]{2,3,1,0:T(8,128)(2,1)S(1)} %get-tuple-element.805), channel_id=1, source_target_pairs={{6,0},{8,2},{10,4},{12,6},{14,8},{16,10},{18,12},{20,14},{22,16},{... | collective-permute-start | bytes 196616 | tf_op jit(solution)/shard_map/ppermute | solution.py:24
  29.9 13.3 %collective-permute-start.6 = (bf16[1,4,256,128]{2,3,1,0:T(8,128)(2,1)S(1)}, bf16[1,4,256,128]{2,3,1,0:T(8,128)(2,1)S(1)}, u32[]{:S(2)}, u32[]{:S(2)}) collective-permute-start(bf16[1,4,256,128]{2,3,1,0:T(8,128)(2,1)S(1)} %get-tuple-element.808), channel_id=1, source_target_pairs={{8,0},{10,2},{12,4},{14,6},{16,8},{18,10},{20,12},{22,14},{24,16},... | collective-permute-start | bytes 786440 | tf_op jit(solution)/shard_map/ppermute | solution.py:24
  32.4 13.6 %collective-permute-start.7 = (bf16[1,1,256,128]{2,3,1,0:T(8,128)(2,1)S(1)}, bf16[1,1,256,128]{2,3,1,0:T(8,128)(2,1)S(1)}, u32[]{:S(2)}, u32[]{:S(2)}) collective-permute-start(bf16[1,1,256,128]{2,3,1,0:T(8,128)(2,1)S(1)} %get-tuple-element.804), channel_id=1, source_target_pairs={{10,0},{12,2},{14,4},{16,6},{18,8},{20,10},{22,12},{24,14},{26,16}... | collective-permute-start | bytes 196616 | tf_op jit(solution)/shard_map/ppermute | solution.py:24
  47.4 185.4 %all-gather.5.cloned.1.call-start = ((), (), s32[]{:S(2)}) async-start(), calls=%async_computation.3 | async-start | bytes 7077888 | tf_op jit(solution)/shard_map/all_gather | solution.py:258
  47.5 15.1 %collective-permute-start.8 = (bf16[1,1,3,512]{3,1,0,2:T(2,128)(2,1)S(1)}, bf16[1,1,3,512]{3,1,0,2:T(2,128)(2,1)S(1)}, u32[]{:S(2)}, u32[]{:S(2)}) collective-permute-start(bf16[1,1,3,512]{3,1,0,2:T(2,128)(2,1)S(1)} %get-tuple-element.815), channel_id=1, source_target_pairs={{0,10},{2,12},{4,14},{6,16},{8,18},{10,20},{12,22},{14,24},{16,26}... | collective-permute-start | bytes 9224 | tf_op jit(solution)/shard_map/ppermute | solution.py:24
  51.9 12.1 %collective-permute-start.9 = (bf16[1,4,3,512]{3,1,0,2:T(4,128)(2,1)S(1)}, bf16[1,4,3,512]{3,1,0,2:T(4,128)(2,1)S(1)}, u32[]{:S(2)}, u32[]{:S(2)}) collective-permute-start(bf16[1,4,3,512]{3,1,0,2:T(4,128)(2,1)S(1)} %get-tuple-element.817), channel_id=1, source_target_pairs={{0,8},{2,10},{4,12},{6,14},{8,16},{10,18},{12,20},{14,22},{16,24},... | collective-permute-start | bytes 36872 | tf_op jit(solution)/shard_map/ppermute | solution.py:24
  55.8 10.8 %collective-permute-start.10 = (bf16[1,1,3,512]{3,1,0,2:T(2,128)(2,1)S(1)}, bf16[1,1,3,512]{3,1,0,2:T(2,128)(2,1)S(1)}, u32[]{:S(2)}, u32[]{:S(2)}) collective-permute-start(bf16[1,1,3,512]{3,1,0,2:T(2,128)(2,1)S(1)} %get-tuple-element.814), channel_id=1, source_target_pairs={{0,6},{2,8},{4,10},{6,12},{8,14},{10,16},{12,18},{14,20},{16,22},{... | collective-permute-start | bytes 9224 | tf_op jit(solution)/shard_map/ppermute | solution.py:24
  57.1 14.0 %collective-permute-start.11 = (bf16[4,1,3,512]{3,1,0,2:T(2,128)(2,1)S(1)}, bf16[4,1,3,512]{3,1,0,2:T(2,128)(2,1)S(1)}, u32[]{:S(2)}, u32[]{:S(2)}) collective-permute-start(bf16[4,1,3,512]{3,1,0,2:T(2,128)(2,1)S(1)} %get-tuple-element.819), channel_id=1, source_target_pairs={{0,2},{2,4},{4,6},{6,8},{8,10},{10,12},{12,14},{14,16},{16,18},{18... | collective-permute-start | bytes 36872 | tf_op jit(solution)/shard_map/ppermute | solution.py:24
  61.1 10.2 %collective-permute-start.12 = (bf16[4,1,3,512]{3,1,0,2:T(2,128)(2,1)S(1)}, bf16[4,1,3,512]{3,1,0,2:T(2,128)(2,1)S(1)}, u32[]{:S(2)}, u32[]{:S(2)}) collective-permute-start(bf16[4,1,3,512]{3,1,0,2:T(2,128)(2,1)S(1)} %get-tuple-element.818), channel_id=1, source_target_pairs={{2,0},{4,2},{6,4},{8,6},{10,8},{12,10},{14,12},{16,14},{18,16},{20... | collective-permute-start | bytes 36872 | tf_op jit(solution)/shard_map/ppermute | solution.py:24
  62.6 8.9 %collective-permute-start.13 = (bf16[1,1,3,512]{3,1,0,2:T(2,128)(2,1)S(1)}, bf16[1,1,3,512]{3,1,0,2:T(2,128)(2,1)S(1)}, u32[]{:S(2)}, u32[]{:S(2)}) collective-permute-start(bf16[1,1,3,512]{3,1,0,2:T(2,128)(2,1)S(1)} %get-tuple-element.813), channel_id=1, source_target_pairs={{6,0},{8,2},{10,4},{12,6},{14,8},{16,10},{18,12},{20,14},{22,16},{... | collective-permute-start | bytes 9224 | tf_op jit(solution)/shard_map/ppermute | solution.py:24
  63.9 8.3 %collective-permute-start.14 = (bf16[1,4,3,512]{3,1,0,2:T(4,128)(2,1)S(1)}, bf16[1,4,3,512]{3,1,0,2:T(4,128)(2,1)S(1)}, u32[]{:S(2)}, u32[]{:S(2)}) collective-permute-start(bf16[1,4,3,512]{3,1,0,2:T(4,128)(2,1)S(1)} %get-tuple-element.816), channel_id=1, source_target_pairs={{8,0},{10,2},{12,4},{14,6},{16,8},{18,10},{20,12},{22,14},{24,16},... | collective-permute-start | bytes 36872 | tf_op jit(solution)/shard_map/ppermute | solution.py:24
  66.6 10.7 %collective-permute-start.15 = (bf16[1,1,3,512]{3,1,0,2:T(2,128)(2,1)S(1)}, bf16[1,1,3,512]{3,1,0,2:T(2,128)(2,1)S(1)}, u32[]{:S(2)}, u32[]{:S(2)}) collective-permute-start(bf16[1,1,3,512]{3,1,0,2:T(2,128)(2,1)S(1)} %get-tuple-element.812), channel_id=1, source_target_pairs={{10,0},{12,2},{14,4},{16,6},{18,8},{20,10},{22,12},{24,14},{26,16}... | collective-permute-start | bytes 9224 | tf_op jit(solution)/shard_map/ppermute | solution.py:24
  182.4 16.7 %collective-permute-start.16 = (bf16[1,1,256,128]{2,3,1,0:T(8,128)(2,1)S(1)}, bf16[1,1,256,128]{2,3,1,0:T(8,128)(2,1)S(1)}, u32[]{:S(2)}, u32[]{:S(2)}) collective-permute-start(bf16[1,1,256,128]{2,3,1,0:T(8,128)(2,1)S(1)} %get-tuple-element.799), channel_id=1, source_target_pairs={{0,10},{2,12},{4,14},{6,16},{8,18},{10,20},{12,22},{14,24},{16,26}... | collective-permute-start | bytes 196616 | tf_op jit(solution)/shard_map/ppermute | solution.py:24
  188.1 12.3 %collective-permute-start.17 = (bf16[1,4,256,128]{2,3,1,0:T(8,128)(2,1)S(1)}, bf16[1,4,256,128]{2,3,1,0:T(8,128)(2,1)S(1)}, u32[]{:S(2)}, u32[]{:S(2)}) collective-permute-start(bf16[1,4,256,128]{2,3,1,0:T(8,128)(2,1)S(1)} %get-tuple-element.801), channel_id=1, source_target_pairs={{0,8},{2,10},{4,12},{6,14},{8,16},{10,18},{12,20},{14,22},{16,24},... | collective-permute-start | bytes 786440 | tf_op jit(solution)/shard_map/ppermute | solution.py:24
  192.3 27.3 %copy-start.3 = (bf16[8,512,128]{2,0,1:T(8,128)(2,1)S(1)}, bf16[8,512,128]{2,0,1:T(8,128)(2,1)}, u32[]{:S(2)}) copy-start(bf16[8,512,128]{2,0,1:T(8,128)(2,1)} %copy-done.2) | copy-start | bytes 3145732
  192.4 10.6 %collective-permute-start.18 = (bf16[1,1,256,128]{2,3,1,0:T(8,128)(2,1)S(1)}, bf16[1,1,256,128]{2,3,1,0:T(8,128)(2,1)S(1)}, u32[]{:S(2)}, u32[]{:S(2)}) collective-permute-start(bf16[1,1,256,128]{2,3,1,0:T(8,128)(2,1)S(1)} %get-tuple-element.798), channel_id=1, source_target_pairs={{0,6},{2,8},{4,10},{6,12},{8,14},{10,16},{12,18},{14,20},{16,22},{... | collective-permute-start | bytes 196616 | tf_op jit(solution)/shard_map/ppermute | solution.py:24
  195.6 13.7 %collective-permute-start.19 = (bf16[4,1,256,128]{2,3,1,0:T(8,128)(2,1)S(1)}, bf16[4,1,256,128]{2,3,1,0:T(8,128)(2,1)S(1)}, u32[]{:S(2)}, u32[]{:S(2)}) collective-permute-start(bf16[4,1,256,128]{2,3,1,0:T(8,128)(2,1)S(1)} %get-tuple-element.803), channel_id=1, source_target_pairs={{0,2},{2,4},{4,6},{6,8},{8,10},{10,12},{12,14},{14,16},{16,18},{18... | collective-permute-start | bytes 786440 | tf_op jit(solution)/shard_map/ppermute | solution.py:24
  197.8 16.2 %collective-permute-start.20 = (bf16[4,1,256,128]{2,3,1,0:T(8,128)(2,1)S(1)}, bf16[4,1,256,128]{2,3,1,0:T(8,128)(2,1)S(1)}, u32[]{:S(2)}, u32[]{:S(2)}) collective-permute-start(bf16[4,1,256,128]{2,3,1,0:T(8,128)(2,1)S(1)} %get-tuple-element.802), channel_id=1, source_target_pairs={{2,0},{4,2},{6,4},{8,6},{10,8},{12,10},{14,12},{16,14},{18,16},{20... | collective-permute-start | bytes 786440 | tf_op jit(solution)/shard_map/ppermute | solution.py:24
  199.1 14.9 %collective-permute-start.21 = (bf16[1,1,256,128]{2,3,1,0:T(8,128)(2,1)S(1)}, bf16[1,1,256,128]{2,3,1,0:T(8,128)(2,1)S(1)}, u32[]{:S(2)}, u32[]{:S(2)}) collective-permute-start(bf16[1,1,256,128]{2,3,1,0:T(8,128)(2,1)S(1)} %get-tuple-element.797), channel_id=1, source_target_pairs={{6,0},{8,2},{10,4},{12,6},{14,8},{16,10},{18,12},{20,14},{22,16},{... | collective-permute-start | bytes 196616 | tf_op jit(solution)/shard_map/ppermute | solution.py:24
  200.4 16.0 %collective-permute-start.22 = (bf16[1,4,256,128]{2,3,1,0:T(8,128)(2,1)S(1)}, bf16[1,4,256,128]{2,3,1,0:T(8,128)(2,1)S(1)}, u32[]{:S(2)}, u32[]{:S(2)}) collective-permute-start(bf16[1,4,256,128]{2,3,1,0:T(8,128)(2,1)S(1)} %get-tuple-element.800), channel_id=1, source_target_pairs={{8,0},{10,2},{12,4},{14,6},{16,8},{18,10},{20,12},{22,14},{24,16},... | collective-permute-start | bytes 786440 | tf_op jit(solution)/shard_map/ppermute | solution.py:24
  202.9 15.2 %collective-permute-start.23 = (bf16[1,1,256,128]{2,3,1,0:T(8,128)(2,1)S(1)}, bf16[1,1,256,128]{2,3,1,0:T(8,128)(2,1)S(1)}, u32[]{:S(2)}, u32[]{:S(2)}) collective-permute-start(bf16[1,1,256,128]{2,3,1,0:T(8,128)(2,1)S(1)} %get-tuple-element.796), channel_id=1, source_target_pairs={{10,0},{12,2},{14,4},{16,6},{18,8},{20,10},{22,12},{24,14},{26,16}... | collective-permute-start | bytes 196616 | tf_op jit(solution)/shard_map/ppermute | solution.py:24
  290.3 18.2 %copy-start.11 = (f32[4,512]{1,0:T(4,128)}, f32[4,512]{1,0:T(4,128)S(1)}, u32[]{:S(2)}) copy-start(f32[4,512]{1,0:T(4,128)S(1)} %get-tuple-element.1058) | copy-start | bytes 24580 | tf_op jit(solution)/shard_map/while
  290.3 18.2 %copy-start.13 = (f32[4,512]{1,0:T(4,128)}, f32[4,512]{1,0:T(4,128)S(1)}, u32[]{:S(2)}) copy-start(f32[4,512]{1,0:T(4,128)S(1)} %get-tuple-element.1061) | copy-start | bytes 24580 | tf_op jit(solution)/shard_map/while
  (33 other events, 172.9 us)
Sparse Core Ops, SparseCore 0:
  47.5 13.3 all-gather.2
  219.7 13.0 all-gather.4

commit v2 on v1

v2 whole, which is shorter than its diff:
```python
import functools
import math

import jax
import jax.numpy as jnp
import numpy as np
from jax import lax
from jax.experimental import pallas as pl
from jax.experimental.pallas import tpu as pltpu
from jax.sharding import PartitionSpec as P

lift_scale = 0.25
LANES = 128
PANEL = 8
BLOCK = 32
VMEM_BYTES = 50 << 20


def lane_copy(value, lane):
    return jnp.broadcast_to(value[:, lane:lane+1], value.shape)

def three_parts(value):
    first = value.astype(jnp.bfloat16)
    rest = value - first.astype(jnp.float32)
    second = rest.astype(jnp.bfloat16)
    third = (rest - second.astype(jnp.float32)).astype(jnp.bfloat16)
    return first, second, third

def factor_panel(rows, base):
    schur = [[lane_copy(rows[base + i], base + j) for j in range(i + 1)] for i in range(PANEL)]
    inverse_pivots, multipliers = [], [[None] * PANEL for _ in range(PANEL)]
    for k in range(PANEL):
        inverse_pivots.append(1.0 / schur[k][k])
        for i in range(k + 1, PANEL):
            multipliers[i][k] = schur[i][k] * inverse_pivots[k]
        for i in range(k + 1, PANEL):
            for j in range(k + 1, i + 1):
                schur[i][j] = schur[i][j] - multipliers[i][k] * schur[j][k]
    unit = [[None] * PANEL for _ in range(PANEL)]
    for i in range(PANEL):
        for j in range(i):
            total = multipliers[i][j]
            for t in range(j + 1, i):
                total = total + multipliers[i][t] * unit[t][j]
            unit[i][j] = -total
    return inverse_pivots, unit

def invert_factors(work, pivots, weights):
    rank, batch, _ = work.shape
    lanes = lax.broadcasted_iota(jnp.int32, (batch, rank), 1)
    square_rows = lax.broadcasted_iota(jnp.int32, (rank, rank), 0)
    square_lanes = lax.broadcasted_iota(jnp.int32, (rank, rank), 1)

    def block_step(block, carry):
        first = block * BLOCK
        back = lax.rem(rank - first, rank)
        rows = [pltpu.roll(work[first + r], back, 1) for r in range(BLOCK)]
        for base in range(0, BLOCK, PANEL):
            inverse_pivots, unit = factor_panel(rows, base)
            inside = (lanes >= base) & (lanes < base + PANEL)
            held_rows, scaled_rows = [], []
            for k in range(PANEL):
                full = rows[base + k]
                for j in range(k):
                    full = full + unit[k][j] * rows[base + j]
                scaled = full * inverse_pivots[k]
                held = jnp.where(inside, 0.0, full)
                for j in range(k):
                    held = jnp.where(lanes == base + j, unit[k][j], held)
                held = jnp.where(lanes == base + k, 1.0, held)
                held_rows.append(held)
                scaled_rows.append(scaled)
            for t in range(base + PANEL, BLOCK):
                row = jnp.where(inside, 0.0, rows[t])
                for k in range(PANEL):
                    row = row - lane_copy(scaled_rows[k], t) * held_rows[k]
                rows[t] = row
            for k in range(PANEL):
                at = base + k
                kept = jnp.where((lanes > at) & (lanes < BLOCK), 0.0, held_rows[k])
                turned = pltpu.roll(kept, first, 1)
                pivots[at] = turned
                weights[at] = pltpu.roll(scaled_rows[k], first, 1)
                work[first + at] = jnp.where(lanes <= first + at, turned, 0.0) * lax.sqrt(inverse_pivots[k])

        @pl.when(first + BLOCK < rank)
        def _():
            below = square_rows >= first + BLOCK
            inside = (square_lanes >= first) & (square_lanes < first + BLOCK)
            for b in range(batch):
                a1, a2, a3 = three_parts(weights[:, b, :])
                b1, b2, b3 = three_parts(pivots[:, b, :])
                left = jnp.concatenate([a1, a1, a2, a2, a1, a3], axis=0)
                right = jnp.concatenate([b1, b2, b1, b2, b3, b1], axis=0)
                change = lax.dot_general(left, right, (((0,), (0,)), ((), ())), preferred_element_type=jnp.float32)
                now = work[:, b, :]
                work[:, b, :] = jnp.where(below, jnp.where(inside, 0.0, now) - change, now)

        return carry

    lax.fori_loop(0, rank // BLOCK, block_step, 0)

def orthonormalize(y_ref, out_ref, work, pivots, weights):
    batch, points, rank = y_ref.shape
    for turn in range(2):
        for b in range(batch):
            data = y_ref[b]
            work[:, b, :] = lax.dot_general(data, data, (((0,), (0,)), ((), ())), precision=lax.Precision.HIGHEST, preferred_element_type=jnp.float32) * (1.0 / points)
        invert_factors(work, pivots, weights)
        for b in range(batch):
            data = lax.dot_general(y_ref[b], work[:, b, :], (((1,), (1,)), ((), ())), precision=lax.Precision.HIGHEST, preferred_element_type=jnp.float32)
            if turn == 0:
                y_ref[b] = data
            else:
                out_ref[b] = data.astype(jnp.bfloat16)


def chip_entries(tile_side, rows_half, core):
    top = core * rows_half
    centres, pairs, singles = [], [], []
    for row in range(rows_half):
        for col in range(tile_side):
            own = row * tile_side + col
            for slot in range(9):
                offset_y, offset_x = slot // 3 - 1, slot % 3 - 1
                other_y, other_x = top + row + offset_y, col + offset_x
                if not (0 <= other_y < tile_side and 0 <= other_x < tile_side):
                    continue
                other = other_y * tile_side + other_x
                mate = other - top * tile_side
                entry = (own, other, offset_y, offset_x, slot, mate)
                if slot == 4:
                    centres.append(entry)
                elif top <= other_y < top + rows_half:
                    if slot > 4:
                        pairs.append(entry)
                else:
                    singles.append(entry[:5] + (-1,))
    return centres, pairs, singles


def edge_entries(tile_side, rows_half, core):
    top = core * rows_half
    corners = 3 * tile_side
    entries = []
    for row in range(rows_half):
        for col in range(tile_side):
            own = row * tile_side + col
            for slot in range(9):
                offset_y, offset_x = slot // 3 - 1, slot % 3 - 1
                other_y, other_x = top + row + offset_y, col + offset_x
                inside_y, inside_x = 0 <= other_y < tile_side, 0 <= other_x < tile_side
                if inside_y and inside_x:
                    continue
                if inside_x:
                    other = 2 * tile_side + other_x
                elif inside_y:
                    other = other_y + (tile_side if other_x > 0 else 0)
                else:
                    other = corners + (0 if (other_y > 0) == (other_x > 0) else 1)
                entries.append((own, other, offset_y, offset_x, slot, -1))
    return entries


def work_lists(tile_side, rows_half, cores):
    chip = [chip_entries(tile_side, rows_half, core) for core in range(cores)]
    edge = [edge_entries(tile_side, rows_half, core) for core in range(cores)]
    counts = tuple(len(part) for part in chip[0])
    flat = [sum(parts, []) for parts in chip]
    return np.array(flat, np.int32), counts, np.array(edge, np.int32)


def spread_points(coords, box_points):
    stretch = math.sqrt(box_points) * 4.0
    return coords.astype(jnp.float32) * stretch


def fill_rows(rows, box_coords, own):
    box_points = box_coords.shape[1]
    turned = jnp.transpose(box_coords)
    for axis in range(3):
        rows[own, axis] = jnp.broadcast_to(turned[:, axis : axis + 1], (box_points, LANES))


def make_entries(target, slot, rows, own, coords, other, offset_y, offset_x, centre, start, stop):
    box_points = coords.shape[2]
    stretch = math.sqrt(box_points) * 4.0
    soften = (0.25 / box_points) * stretch * stretch
    step = 64
    for first in range(start, stop, step):
        for lane in range(0, box_points, LANES):
            here = pl.ds(lane, LANES)
            delta_u = (coords[other, 0:1, here] + offset_x) - rows[own, 0, first : first + step, :]
            delta_v = (coords[other, 1:2, here] + offset_y) - rows[own, 1, first : first + step, :]
            delta_w = coords[other, 2:3, here] - rows[own, 2, first : first + step, :]
            values = lax.rsqrt(delta_u * delta_u + delta_v * delta_v + delta_w * delta_w + soften)
            if centre and lane <= first < lane + LANES:
                row_ids = lax.broadcasted_iota(jnp.int32, values.shape, 0) + (first - lane)
                col_ids = lax.broadcasted_iota(jnp.int32, values.shape, 1)
                values = values + jnp.where(row_ids == col_ids, 1.0, 0.0)
            target[slot, first : first + step, here] = values.astype(jnp.bfloat16)


def list_active(table, core, first, count, mask, active, base):
    def check(index, total):
        on = mask[table[core, first + index, 0], table[core, first + index, 4]] != 0

        @pl.when(on)
        def _():
            active[base + total] = first + index

        return total + jnp.where(on, 1, 0)

    return lax.fori_loop(0, count, check, 0)


def run_blocks(active, base, total, begun, body, buffers, store, sems):
    def step(turn, carry):
        count = begun + turn
        slot = lax.rem(count, 2)

        @pl.when(count >= 2)
        def _():
            pltpu.make_async_copy(buffers.at[slot], store.at[0], sems.at[slot]).wait()

        index = active[base + turn]
        body(index, slot)
        pltpu.make_async_copy(buffers.at[slot], store.at[index], sems.at[slot]).start()
        return carry

    lax.fori_loop(0, total, step, 0)
    return begun + total


def drain(begun, buffers, store, sems):
    for back in (1, 2):

        @pl.when(begun >= back)
        def _():
            slot = lax.rem(begun - back, 2)
            pltpu.make_async_copy(buffers.at[slot], store.at[0], sems.at[slot]).wait()


def place(table, core, index):
    return [table[core, index, field] for field in range(6)]


def chip_sketch_kernel(counts, core_ref, mask, table, points, mine, theirs, y_ref, store,
                       omega, omega_t, coords, rows, turned_y, buffers, active, sems, load_sems):
    core = core_ref[0]
    chip_boxes, _, box_points = points.shape
    own_boxes, _, skel_rank = y_ref.shape
    half = mine.shape[1]
    loads = [
        pltpu.make_async_copy(mine, omega.at[:, pl.ds(pl.multiple_of(core * half, half), half), :], load_sems.at[0]),
        pltpu.make_async_copy(theirs, omega.at[:, pl.ds(pl.multiple_of((1 - core) * half, half), half), :], load_sems.at[1]),
    ]
    for load in loads:
        load.start()
    stretch = math.sqrt(box_points) * 4.0
    for box in range(chip_boxes):
        spread = points[box].astype(jnp.float32) * stretch
        coords[box, 0:2] = spread[0:2]
        coords[box, 2:3] = spread[2:3] * lift_scale
    for own in range(own_boxes):
        fill_rows(rows, coords[core * own_boxes + own], own)
    for load in loads:
        load.wait()
    for own in range(own_boxes):
        omega_t[own] = jnp.transpose(omega[core * own_boxes + own])
        turned_y[own] = jnp.zeros((skel_rank, box_points), jnp.float32)

    part = box_points // 2

    def block(kind, index, slot):
        own, other, offset_y, offset_x, _, mate = place(table, core, index)
        shift_y, shift_x = offset_y.astype(jnp.float32) * stretch, offset_x.astype(jnp.float32) * stretch
        for first in range(0, box_points, part):
            make_entries(buffers, slot, rows, own, coords, other, shift_y, shift_x, kind == 0, first, first + part)
            values = buffers[slot, first : first + part, :]
            found = jnp.dot(values, omega[other], preferred_element_type=jnp.float32)
            if kind == 0:
                y_ref[own, first : first + part, :] = found
            else:
                y_ref[own, first : first + part, :] += found
            if kind == 1:
                turned_y[mate] += jnp.dot(
                    omega_t[own, :, first : first + part], values, preferred_element_type=jnp.float32
                )

    begun, first = 0, 0
    for kind, count in enumerate(counts):
        total = list_active(table, core, first, count, mask, active, first)
        begun = run_blocks(active, first, total, begun, functools.partial(block, kind), buffers, store, sems)
        first += count
    for own in range(own_boxes):
        y_ref[own] += jnp.transpose(turned_y[own])
    drain(begun, buffers, store, sems)


def edge_coords(coords, extended, box, box_points, stretch):
    packed = extended[box, box_points : box_points + 16, :].astype(jnp.float32) * stretch
    strips = box_points // LANES
    for axis in range(3):
        for strip in range(strips):
            row = packed[axis * strips + strip : axis * strips + strip + 1, :]
            coords[box, axis : axis + 1, strip * LANES : (strip + 1) * LANES] = row * lift_scale if axis == 2 else row


def load_edges(core, pieces, extended, sems):
    first_col, second_col, row, corner_a, corner_b = pieces
    side = row.shape[0]
    return [
        pltpu.make_async_copy(first_col, extended.at[pl.ds(core * side, side)], sems.at[0]),
        pltpu.make_async_copy(second_col, extended.at[pl.ds((1 - core) * side, side)], sems.at[1]),
        pltpu.make_async_copy(row, extended.at[pl.ds(2 * side, side)], sems.at[2]),
        pltpu.make_async_copy(corner_a, extended.at[pl.ds(3 * side, 1)], sems.at[3]),
        pltpu.make_async_copy(corner_b, extended.at[pl.ds(3 * side + 1, 1)], sems.at[4]),
    ]


def edge_sketch_kernel(core_ref, mask, table, points, sketched, first_col, second_col, row, corner_a, corner_b,
                       basis, store, extended, coords, rows, y_ref, buffers, active, sems, load_sems,
                       work, pivots, weights):
    core = core_ref[0]
    own_boxes, box_points, skel_rank = y_ref.shape
    loads = load_edges(core, (first_col, second_col, row, corner_a, corner_b), extended, load_sems)
    loads.append(pltpu.make_async_copy(sketched, y_ref, load_sems.at[5]))
    for load in loads:
        load.start()
    stretch = math.sqrt(box_points) * 4.0
    for own in range(own_boxes):
        spread = points[core * own_boxes + own].astype(jnp.float32) * stretch
        coords[0, 0:2] = spread[0:2]
        coords[0, 2:3] = spread[2:3] * lift_scale
        fill_rows(rows, coords[0], own)
    for load in loads:
        load.wait()
    for box in range(extended.shape[0]):
        edge_coords(coords, extended, box, box_points, stretch)
    part = box_points // 2

    def block(index, slot):
        own, other, offset_y, offset_x, _, _ = place(table, core, index)
        shift_y, shift_x = offset_y.astype(jnp.float32) * stretch, offset_x.astype(jnp.float32) * stretch
        for first in range(0, box_points, part):
            make_entries(buffers, slot, rows, own, coords, other, shift_y, shift_x, False, first, first + part)
            values = buffers[slot, first : first + part, :]
            y_ref[own, first : first + part, :] += jnp.dot(
                values, extended[other, 0:box_points, :], preferred_element_type=jnp.float32
            )

    total = list_active(table, core, 0, table.shape[1], mask, active, 0)
    begun = run_blocks(active, 0, total, 0, block, buffers, store, sems)
    orthonormalize(y_ref, basis, work, pivots, weights)
    drain(begun, buffers, store, sems)


def run_stored(active, base, total, buffers, store, sems, depth, body):
    def fetch(turn):
        slot = lax.rem(turn, depth)
        return pltpu.make_async_copy(store.at[active[base + turn]], buffers.at[slot], sems.at[slot])

    for turn in range(depth - 1):

        @pl.when(turn < total)
        def _():
            fetch(turn).start()

    def step(turn, carry):
        @pl.when(turn + depth - 1 < total)
        def _():
            fetch(turn + depth - 1).start()

        fetch(turn).wait()
        body(active[base + turn], lax.rem(turn, depth))
        return carry

    lax.fori_loop(0, total, step, 0)


def chip_couple_kernel(counts, depth, core_ref, mask, table, edge_table, mine, theirs, store, edge_store,
                       keep, give, projected, basis, basis_t, buffers, active, result, sems):
    core = core_ref[0]
    own_boxes, box_points, skel_rank = mine.shape
    half = keep.shape[2]
    basis[pl.ds(core * own_boxes, own_boxes)] = mine[...]
    basis[pl.ds((1 - core) * own_boxes, own_boxes)] = theirs[...]
    for own in range(own_boxes):
        basis_t[own] = jnp.transpose(mine[own])
        keep[own] = jnp.zeros(keep.shape[1:], jnp.float32)
        give[own] = jnp.zeros(give.shape[1:], jnp.float32)

    def put(own, slot, values):
        result[...] = values
        keep[own, slot] = result[pl.ds(pl.multiple_of(core * half, half), half), :]
        give[own, slot] = result[pl.ds(pl.multiple_of((1 - core) * half, half), half), :]

    def block(kind, index, slot):
        own, other, _, _, stencil, mate = place(table, core, index)
        rays = jnp.dot(basis_t[own], buffers[slot], preferred_element_type=jnp.float32).astype(jnp.bfloat16)
        values = jnp.dot(rays, basis[other], preferred_element_type=jnp.float32) * (1.0 / box_points)
        put(own, stencil, values)
        if kind == 1:
            put(mate, 8 - stencil, jnp.transpose(values))

    def edge_block(index, slot):
        own = edge_table[core, index, 0]
        projected[index] = jnp.dot(
            basis_t[own], buffers[slot], preferred_element_type=jnp.float32
        ).astype(jnp.bfloat16)

    first = 0
    for kind, count in enumerate(counts):
        total = list_active(table, core, first, count, mask, active, first)
        run_stored(active, first, total, buffers, store, sems, depth, functools.partial(block, kind))
        first += count
    total = list_active(edge_table, core, 0, edge_table.shape[1], mask, active, 0)
    run_stored(active, 0, total, buffers, edge_store, sems, depth, edge_block)


def edge_couple_kernel(core_ref, mask, edge_table, projected, first_col, second_col, row, corner_a, corner_b,
                       keep_in, give_in, keep, give, extended, results, active, load_sems, sems):
    core = core_ref[0]
    box_points = projected.shape[2]
    half = keep.shape[2]
    loads = load_edges(core, (first_col, second_col, row, corner_a, corner_b), extended, load_sems)
    for load in loads:
        load.start()
    total = list_active(edge_table, core, 0, edge_table.shape[1], mask, active, 0)
    for load in loads:
        load.wait()

    def copies(turn):
        index = active[turn]
        own, stencil = edge_table[core, index, 0], edge_table[core, index, 4]
        mine = results.at[turn, pl.ds(pl.multiple_of(core * half, half), half), :]
        theirs = results.at[turn, pl.ds(pl.multiple_of((1 - core) * half, half), half), :]
        return (
            pltpu.make_async_copy(mine, keep.at[own, stencil], sems.at[turn]),
            pltpu.make_async_copy(theirs, give.at[own, stencil], sems.at[results.shape[0] + turn]),
        )

    def step(turn, carry):
        index = active[turn]
        other = edge_table[core, index, 1]
        results[turn] = jnp.dot(
            projected[index], extended[other], preferred_element_type=jnp.float32
        ) * (1.0 / box_points)
        for copy in copies(turn):
            copy.start()
        return carry

    def finish(turn, carry):
        for copy in copies(turn):
            copy.wait()
        return carry

    lax.fori_loop(0, total, step, 0)
    lax.fori_loop(0, total, finish, 0)


SMEM = pl.BlockSpec(memory_space=pltpu.SMEM)
VMEM = pl.BlockSpec(memory_space=pltpu.VMEM)
ANY = pl.BlockSpec(memory_space=pl.ANY)


def params():
    return pltpu.CompilerParams(vmem_limit_bytes=VMEM_BYTES)


def exchange(boxes, core, grid_side):
    side = boxes.shape[0]

    def send(piece, step_y, step_x):
        pairs = []
        for tile in range(grid_side * grid_side):
            for member in range(2):
                sign = 2 * member - 1
                target_y, target_x = tile // grid_side + sign * step_y, tile % grid_side + sign * step_x
                if 0 <= target_y < grid_side and 0 <= target_x < grid_side:
                    target = target_y * grid_side + target_x
                    pairs.append((tile * 2 + member, target * 2 + 1 - member))
        return lax.ppermute(piece, ("box", "col"), pairs)

    last = side - 1
    low = core == 0
    col = send(jnp.where(low, boxes[:, 0], boxes[:, last]), 0, 1)
    row = send(jnp.where(low, boxes[0], boxes[last]), 1, 0)
    corner_a = send(jnp.where(low, boxes[0, 0:1], boxes[last, last:]), 1, 1)
    corner_b = send(jnp.where(low, boxes[0, last:], boxes[last, 0:1]), 1, -1)
    return col, row, corner_a, corner_b


def swap(value):
    return lax.ppermute(value, "col", [(0, 1), (1, 0)])


def body(points, sketch, near_mask):
    chip_boxes, _, box_points = points.shape
    half_points, skel_rank = sketch.shape[1:]
    tile_side = math.isqrt(chip_boxes)
    grid_side = math.isqrt(lax.axis_size("box"))
    cores = lax.axis_size("col")
    rows_half = tile_side // cores
    own_boxes = rows_half * tile_side
    half_rank = skel_rank // cores
    core = lax.axis_index("col")
    core_arg = core.astype(jnp.int32).reshape(1)
    chip_table, counts, edge_table = work_lists(tile_side, rows_half, cores)
    chip_blocks, edge_blocks = chip_table.shape[1], edge_table.shape[1]
    edge_boxes = 3 * tile_side + 2
    chip_table, edge_table = jnp.asarray(chip_table), jnp.asarray(edge_table)
    own_mask = lax.dynamic_slice_in_dim(near_mask, core * own_boxes, own_boxes, 0)
    low = core == 0

    theirs = swap(sketch)
    packed = points.reshape(chip_boxes, 3 * box_points // skel_rank, skel_rank)
    packed = jnp.pad(packed, ((0, 0), (0, 16 - packed.shape[1]), (0, 0)))
    whole = jnp.where(
        low,
        jnp.concatenate([sketch, theirs, packed], axis=1),
        jnp.concatenate([theirs, sketch, packed], axis=1),
    ).reshape(tile_side, tile_side, box_points + 16, skel_rank)
    col, row, corner_a, corner_b = exchange(whole, core, grid_side)

    bf16, f32 = jnp.bfloat16, jnp.float32
    sketched, store = pl.pallas_call(
        functools.partial(chip_sketch_kernel, counts),
        out_shape=(
            jax.ShapeDtypeStruct((own_boxes, box_points, skel_rank), f32),
            jax.ShapeDtypeStruct((chip_blocks, box_points, box_points), bf16),
        ),
        in_specs=[SMEM, SMEM, SMEM, VMEM, ANY, ANY],
        out_specs=(VMEM, ANY),
        scratch_shapes=[
            pltpu.VMEM((chip_boxes, box_points, skel_rank), bf16),
            pltpu.VMEM((own_boxes, skel_rank, box_points), bf16),
            pltpu.VMEM((chip_boxes, 8, box_points), f32),
            pltpu.VMEM((own_boxes, 3, box_points, LANES), f32),
            pltpu.VMEM((own_boxes, skel_rank, box_points), f32),
            pltpu.VMEM((2, box_points, box_points), bf16),
            pltpu.SMEM((chip_blocks,), jnp.int32),
            pltpu.SemaphoreType.DMA((2,)),
            pltpu.SemaphoreType.DMA((2,)),
        ],
        compiler_params=params(),
        cost_estimate=pl.CostEstimate(flops=8 * 10**9, bytes_accessed=24 * 10**6, transcendentals=0),
        name="chip_sketch",
    )(core_arg, own_mask, chip_table, points, sketch, theirs)

    col, row, corner_a, corner_b, sketched = lax.optimization_barrier((col, row, corner_a, corner_b, sketched))
    second_col = swap(col)
    basis, edge_store = pl.pallas_call(
        edge_sketch_kernel,
        out_shape=(
            jax.ShapeDtypeStruct((own_boxes, box_points, skel_rank), bf16),
            jax.ShapeDtypeStruct((edge_blocks, box_points, box_points), bf16),
        ),
        in_specs=[SMEM, SMEM, SMEM, VMEM] + [ANY] * 6,
        out_specs=(VMEM, ANY),
        scratch_shapes=[
            pltpu.VMEM((edge_boxes, box_points + 16, skel_rank), bf16),
            pltpu.VMEM((edge_boxes, 8, box_points), f32),
            pltpu.VMEM((own_boxes, 3, box_points, LANES), f32),
            pltpu.VMEM((own_boxes, box_points, skel_rank), f32),
            pltpu.VMEM((2, box_points, box_points), bf16),
            pltpu.SMEM((edge_blocks,), jnp.int32),
            pltpu.SemaphoreType.DMA((2,)),
            pltpu.SemaphoreType.DMA((6,)),
            pltpu.VMEM((skel_rank, own_boxes, skel_rank), f32),
            pltpu.VMEM((BLOCK, own_boxes, skel_rank), f32),
            pltpu.VMEM((BLOCK, own_boxes, skel_rank), f32),
        ],
        compiler_params=params(),
        name="edge_sketch",
    )(core_arg, own_mask, edge_table, points, sketched, col, second_col, row, corner_a, corner_b)

    other_basis = swap(basis)
    whole = jnp.where(
        low,
        jnp.concatenate([basis, other_basis], axis=0),
        jnp.concatenate([other_basis, basis], axis=0),
    ).reshape(tile_side, tile_side, box_points, skel_rank)
    col, row, corner_a, corner_b = exchange(whole, core, grid_side)
    depth = 4
    coupling_shape = jax.ShapeDtypeStruct((own_boxes, 9, half_rank, skel_rank), f32)
    keep, give, projected = pl.pallas_call(
        functools.partial(chip_couple_kernel, counts, depth),
        out_shape=(
            coupling_shape,
            coupling_shape,
            jax.ShapeDtypeStruct((edge_blocks, skel_rank, box_points), bf16),
        ),
        in_specs=[SMEM] * 4 + [VMEM, VMEM, ANY, ANY],
        out_specs=(VMEM, VMEM, VMEM),
        scratch_shapes=[
            pltpu.VMEM((chip_boxes, box_points, skel_rank), bf16),
            pltpu.VMEM((own_boxes, skel_rank, box_points), bf16),
            pltpu.VMEM((depth, box_points, box_points), bf16),
            pltpu.SMEM((max(chip_blocks, edge_blocks),), jnp.int32),
            pltpu.VMEM((skel_rank, skel_rank), f32),
            pltpu.SemaphoreType.DMA((depth,)),
        ],
        compiler_params=params(),
        cost_estimate=pl.CostEstimate(flops=8 * 10**9, bytes_accessed=32 * 10**6, transcendentals=0),
        name="chip_couple",
    )(core_arg, own_mask, chip_table, edge_table, basis, other_basis, store, edge_store)

    col, row, corner_a, corner_b, projected = lax.optimization_barrier((col, row, corner_a, corner_b, projected))
    second_col = swap(col)
    keep, give = pl.pallas_call(
        edge_couple_kernel,
        out_shape=(coupling_shape, coupling_shape),
        in_specs=[SMEM] * 3 + [VMEM] + [ANY] * 7,
        out_specs=(ANY, ANY),
        scratch_shapes=[
            pltpu.VMEM((edge_boxes, box_points, skel_rank), bf16),
            pltpu.VMEM((edge_blocks, skel_rank, skel_rank), f32),
            pltpu.SMEM((edge_blocks,), jnp.int32),
            pltpu.SemaphoreType.DMA((5,)),
            pltpu.SemaphoreType.DMA((2 * edge_blocks,)),
        ],
        input_output_aliases={9: 0, 10: 1},
        compiler_params=params(),
        name="edge_couple",
    )(core_arg, own_mask, edge_table, projected, col, second_col, row, corner_a, corner_b, keep, give)

    taken = swap(give)
    coupling = jnp.where(low, jnp.concatenate([keep, taken], axis=0), jnp.concatenate([taken, keep], axis=0))
    basis_out = lax.dynamic_slice_in_dim(
        whole.reshape(chip_boxes, box_points, skel_rank), core * half_points, half_points, 1
    )
    return basis_out, coupling


def solution(mesh):
    return jax.shard_map(
        body,
        mesh=mesh,
        in_specs=(P("box", None, None), P("box", "col", None), P("box", None)),
        out_specs=(P("box", "col", None), P("box", None, "col", None)),
        check_vma=False,
    )
```

time: 360 us -> 156 us (0.43)
  matrix products: 113 us -> 0 us
  Pallas kernels: 28.9 us -> 90.1 us
  local copies, waits for them, and re-layouts: 49.5 us -> 1.99 us
  waiting for transfers between devices: 39.9 us -> 10.4 us
  loops' own time: 23.2 us -> 0 us
  starting transfers between devices: 60.4 us -> 40.1 us
  between operations: 15.1 us -> 0.94 us
  blocking collectives: 12.1 us -> 0 us
    dot_general x36 -> x0, matrix products: 113 us -> none  [the longest x18 60.8 us: couple_full(): jnp.einsum('brj,bjs->brs', projected, near_basis, preferred_element_type=...]
    pallas_call x1 -> x4, Pallas kernels: 28.9 us -> 90.1 us  [the longest x1 35.9 us: body(): pl.pallas_call(edge_sketch_kernel, out_shape=(jax.ShapeDtypeStruct((own_b...]
    another operation x2 -> x0, loops' own time: 23.2 us -> none  [the longest x1 12.1 us: body(): blocks = lax.map(sketch_full, own_rows)]
    ppermute x24 -> x13, starting transfers between devices: 60.3 us -> 40.1 us  [the longest x5 34.5 us: swap(): return lax.ppermute(value, 'col', [(0, 1), (1, 0)])]
    ppermute x24 -> x13, waiting for transfers between devices: 27.8 us -> 10.4 us  [the longest x5 10.4 us: swap(): return lax.ppermute(value, 'col', [(0, 1), (1, 0)])]
    another operation x5 -> x0, local copies, waits for them, and re-layouts: 14.4 us -> none
    all_to_all x2 -> x0, blocking collectives: 12.1 us -> none  [the longest x1 7.52 us: body(): lax.all_to_all(owned, 'col', split_axis=2, concat_axis=0, tiled=True)]
    all_gather x2 -> x0, waiting for transfers between devices: 12 us -> none  [the longest x1 12 us: body(): basis_full = lax.all_gather(ext_basis, 'col', axis=2, tiled=True)]
  transfers between devices with their start and end apart: 26 -> 13, of which waited for: 11 -> 5; matrix products, arithmetic and copies ran while one was open for 4% -> 2% of each run, Pallas kernels for 0% -> 32%
where the time goes in v2:
time: 156 us; the launch traced here: 154 us
  Pallas kernels  90.1 us (58%)
  starting transfers between devices  40.1 us (26%)
  other arithmetic  10.8 us (7%)
  waiting for transfers between devices  10.4 us (7%)
  local copies, waits for them, and re-layouts  1.99 us (1%)
    pallas_call x1, Pallas kernels, body(): pl.pallas_call(edge_sketch_kernel, out_shape=(jax.ShapeDtypeStruct((own_b...  35.9 us
    ppermute x5, starting transfers between devices, swap(): return lax.ppermute(value, 'col', [(0, 1), (1, 0)])  34.5 us
    pallas_call x1, Pallas kernels, body(): pl.pallas_call(functools.partial(chip_sketch_kernel, counts), out_shape=(...  26.5 us
    pallas_call x1, Pallas kernels, body(): pl.pallas_call(functools.partial(chip_couple_kernel, counts, depth), out_...  23.3 us
    ppermute x5, waiting for transfers between devices, swap(): return lax.ppermute(value, 'col', [(0, 1), (1, 0)])  10.4 us
    select_n x1, other arithmetic, body(): jnp.where(low, jnp.concatenate([keep, taken], axis=0), jnp.concatenate([t...  7.6 us
    ppermute x8, starting transfers between devices, send(): return lax.ppermute(piece, ('box', 'col'), pairs)  5.59 us
    pallas_call x1, Pallas kernels, body(): pl.pallas_call(edge_couple_kernel, out_shape=(coupling_shape, coupling_sh...  4.48 us
  transfers between devices with their start and end apart: 13, of which 5 were waited for; matrix products, arithmetic and copies ran while one was open for 2% of the time, Pallas kernels for 32%

profile of v2, /device:TPU:0, one launch (start us, length us, event | category | flops | bytes accessed | tf_op | source)
XLA Modules:
  0.0 154.4 jit_solution(2566848576755939227)
XLA Ops:
  0.6 0.5 collective-permute-start
  1.2 0.8 copy.14.points
  2.1 1.5 collective-permute-done.theirs
  3.7 2.0 %fusion.1 = bf16[4,4,528,128]{3,2,1,0:T(8,128)(2,1)S(1)} fusion(bf16[4,4,16,128]{3,2,1,0:T(8,128)(2,1)S(1)} %bitcast.21, bf16[4,4,256,128]{3,2,1,0:T(8,128)(2,1)S(1)} %bitcast.18, bf16[4,4,256,128]{3,2,1,0:T(8,128)(2,1)} %bitcast.17, pred[]{:T(512)S(6)} %eq.2), kind=kLoop, calls=%fused_computation.6 | loop fusion | flops 12976128 | bytes 4325377 | tf_op jit(solution)/shard_map/jit(_where)/select_n | solution.py:520
  5.7 0.1 fusion.2
  5.8 0.8 collective-permute-start.3
  6.6 0.7 collective-permute-start.4
  7.3 0.7 collective-permute-start.1
  8.0 0.6 fusion
  8.6 0.1 slice_select_fusion
  8.7 0.7 collective-permute-start.2
  9.4 26.5 %chip_sketch.1 = (f32[8,512,128]{2,1,0:T(8,128)}, bf16[34,512,512]{2,1,0:T(8,128)(2,1)}) custom-call(s32[1]{0:T(128)} %bitcast.core_ref, s32[8,9]{1,0:T(8,128)S(1)} %constant_dynamic-slice_fusion.1.mask, s32[2,34,6]{2,1,0:T(8,128)S(1)} %copy-done.3, bf16[16,3,512]{2,1,0:T(4,128)(2,1)S(1)} %copy.14.points, bf16[16,256,128]{2,1,0:T(8,128)(2,1)S(1)} %copy-done.1, ...), custom_call_target="tpu_custom_call" | custom-call | flops 8000000000 | bytes 24000000 | tf_op jit(solution)/shard_map/chip_sketch/pallas_call | solution.py:528
  35.9 9.7 %collective-permute-start.5 = (bf16[4,528,128]{2,1,0:T(8,128)(2,1)S(1)}, bf16[4,528,128]{2,1,0:T(8,128)(2,1)S(1)}, u32[]{:S(2)}, u32[]{:S(2)}) collective-permute-start(bf16[4,528,128]{2,1,0:T(8,128)(2,1)S(1)} %collective-permute-done.1.first_col), channel_id=1, source_target_pairs={{0,1},{1,0},{2,3},{3,2},{4,5},{5,4},{6,7},{7,6},{8,9},{9,8},{10,11... | collective-permute-start | bytes 1622024 | tf_op jit(solution)/shard_map/ppermute | solution.py:496
  45.6 1.6 %collective-permute-done.5.second_col = bf16[4,528,128]{2,1,0:T(8,128)(2,1)S(1)} collective-permute-done((bf16[4,528,128]{2,1,0:T(8,128)(2,1)S(1)}, bf16[4,528,128]{2,1,0:T(8,128)(2,1)S(1)}, u32[]{:S(2)}, u32[]{:S(2)}) %collective-permute-start.5) | collective-permute-done | bytes 540704 | tf_op jit(solution)/shard_map/ppermute | solution.py:496
  47.2 35.9 %edge_sketch.1 = (bf16[8,512,128]{2,1,0:T(8,128)(2,1)S(1)}, bf16[22,512,512]{2,1,0:T(8,128)(2,1)}) custom-call(s32[1]{0:T(128)} %bitcast.core_ref, s32[8,9]{1,0:T(8,128)S(1)} %constant_dynamic-slice_fusion.1.mask, s32[2,22,6]{2,1,0:T(8,128)S(1)} %copy-done.2, bf16[16,3,512]{2,1,0:T(4,128)(2,1)S(1)} %copy.14.points, ...), custom_call_target="tpu_custom_call" | custom-call | tf_op jit(solution)/shard_map/edge_sketch/pallas_call | solution.py:554
  83.0 5.7 %collective-permute-start.6 = (bf16[8,512,128]{2,1,0:T(8,128)(2,1)S(1)}, bf16[8,512,128]{2,1,0:T(8,128)(2,1)S(1)}, u32[]{:S(2)}, u32[]{:S(2)}) collective-permute-start(bf16[8,512,128]{2,1,0:T(8,128)(2,1)S(1)} %get-tuple-element.27.mine), channel_id=1, source_target_pairs={{0,1},{1,0},{2,3},{3,2},{4,5},{5,4},{6,7},{7,6},{8,9},{9,8},{10,11... | collective-permute-start | bytes 3145736 | tf_op jit(solution)/shard_map/ppermute | solution.py:496
  88.8 2.3 %collective-permute-done.6.theirs = bf16[8,512,128]{2,1,0:T(8,128)(2,1)S(1)} collective-permute-done((bf16[8,512,128]{2,1,0:T(8,128)(2,1)S(1)}, bf16[8,512,128]{2,1,0:T(8,128)(2,1)S(1)}, u32[]{:S(2)}, u32[]{:S(2)}) %collective-permute-start.6) | collective-permute-done | bytes 1048608 | tf_op jit(solution)/shard_map/ppermute | solution.py:496
  91.1 0.3 maximum_select_fusion.1
  91.4 0.1 slice_select_fusion.2
  91.4 0.1 fusion.3
  91.5 0.7 collective-permute-start.7
  92.3 0.7 collective-permute-start.8
  93.0 0.7 collective-permute-start.10
  93.6 0.7 collective-permute-start.9
  94.3 23.3 %chip_couple.1 = (f32[8,9,64,128]{3,2,1,0:T(8,128)}, f32[8,9,64,128]{3,2,1,0:T(8,128)}, bf16[22,128,512]{2,1,0:T(8,128)(2,1)}) custom-call(s32[1]{0:T(128)} %bitcast.core_ref, s32[8,9]{1,0:T(8,128)S(1)} %constant_dynamic-slice_fusion.1.mask, s32[2,34,6]{2,1,0:T(8,128)S(1)} %copy-done.3, s32[2,22,6]{2,1,0:T(8,128)S(1)} %copy-done.2, ...), custom_call_target="tpu_custom_call" | custom-call | flops 8000000000 | bytes 32000000 | tf_op jit(solution)/shard_map/chip_couple/pallas_call | solution.py:588
  117.6 16.7 %collective-permute-start.11 = (bf16[4,512,128]{2,1,0:T(8,128)(2,1)S(1)}, bf16[4,512,128]{2,1,0:T(8,128)(2,1)S(1)}, u32[]{:S(2)}, u32[]{:S(2)}) collective-permute-start(bf16[4,512,128]{2,1,0:T(8,128)(2,1)S(1)} %collective-permute-done.7.first_col), channel_id=1, source_target_pairs={{0,1},{1,0},{2,3},{3,2},{4,5},{5,4},{6,7},{7,6},{8,9},{9,8},{10,11... | collective-permute-start | bytes 1572872 | tf_op jit(solution)/shard_map/ppermute | solution.py:496
  134.3 1.5 collective-permute-done.11.second_col
  135.9 4.5 %edge_couple.1 = (f32[8,9,64,128]{3,2,1,0:T(8,128)}, f32[8,9,64,128]{3,2,1,0:T(8,128)}) custom-call(s32[1]{0:T(128)} %bitcast.core_ref, s32[8,9]{1,0:T(8,128)S(1)} %constant_dynamic-slice_fusion.1.mask, s32[2,22,6]{2,1,0:T(8,128)S(1)} %copy-done.2, bf16[22,128,512]{2,1,0:T(8,128)(2,1)} %get-tuple-element.31.projected, ...), custom_call_target="tpu_custom_call", output_to_operand_aliasing={{0}: (9, {}), {1}: (10, {})} | custom-call | tf_op jit(solution)/shard_map/edge_couple/pallas_call | solution.py:612
  140.3 1.9 %collective-permute-start.12 = (f32[8,9,64,128]{3,2,1,0:T(8,128)}, f32[8,9,64,128]{3,2,1,0:T(8,128)}, u32[]{:S(2)}, u32[]{:S(2)}) collective-permute-start(f32[8,9,64,128]{3,2,1,0:T(8,128)} %get-tuple-element.39), channel_id=1, source_target_pairs={{0,1},{1,0},{2,3},{3,2},{4,5},{5,4},{6,7},{7,6},{8,9},{9,8},{10,11... | collective-permute-start | bytes 7077896 | tf_op jit(solution)/shard_map/ppermute | solution.py:496
  142.3 1.0 constant_dynamic-slice_fusion
  143.3 3.5 %collective-permute-done.12 = f32[8,9,64,128]{3,2,1,0:T(8,128)} collective-permute-done((f32[8,9,64,128]{3,2,1,0:T(8,128)}, f32[8,9,64,128]{3,2,1,0:T(8,128)}, u32[]{:S(2)}, u32[]{:S(2)}) %collective-permute-start.12) | collective-permute-done | bytes 2359328 | tf_op jit(solution)/shard_map/ppermute | solution.py:496
  146.8 7.6 %maximum_select_fusion = f32[16,9,64,128]{3,2,1,0:T(8,128)} fusion(f32[8,9,64,128]{3,2,1,0:T(8,128)} %collective-permute-done.12, f32[8,9,64,128]{3,2,1,0:T(8,128)} %get-tuple-element.38, pred[]{:T(512)S(6)} %eq.2), kind=kLoop, calls=%fused_computation | loop fusion | flops 3538944 | bytes 9437185 | tf_op jit(solution)/shard_map/jit(_where)/select_n | solution.py:630
  (21 shorter events, 0.2 us)
Async XLA Ops:
  0.6 1.5 copy-start
  0.6 3.0 %collective-permute-start = (bf16[16,256,128]{2,1,0:T(8,128)(2,1)}, bf16[16,256,128]{2,1,0:T(8,128)(2,1)S(1)}, u32[]{:S(2)}, u32[]{:S(2)}) collective-permute-start(bf16[16,256,128]{2,1,0:T(8,128)(2,1)} %mine.1), channel_id=1, source_target_pairs={{0,1},{1,0},{2,3},{3,2},{4,5},{5,4},{6,7},{7,6},{8,9},{9,8},{10,11... | collective-permute-start | bytes 3145736 | tf_op jit(solution)/shard_map/ppermute | solution.py:496
  5.7 2.3 %copy-start.1 = (bf16[16,256,128]{2,1,0:T(8,128)(2,1)S(1)}, bf16[16,256,128]{2,1,0:T(8,128)(2,1)}, u32[]{:S(2)}) copy-start(bf16[16,256,128]{2,1,0:T(8,128)(2,1)} %mine.1) | copy-start | bytes 3145732
  5.8 30.1 %collective-permute-start.3 = (bf16[1,528,128]{2,1,0:T(8,128)(2,1)S(1)}, bf16[1,528,128]{2,1,0:T(8,128)(2,1)S(1)}, u32[]{:S(2)}, u32[]{:S(2)}) collective-permute-start(bf16[1,528,128]{2,1,0:T(8,128)(2,1)S(1)} %get-tuple-element.41), channel_id=1, source_target_pairs={{1,10},{3,12},{5,14},{9,18},{10,1},{11,20},{12,3},{13,22},{14,5},{... | collective-permute-start | bytes 405512 | tf_op jit(solution)/shard_map/ppermute | solution.py:484
  6.6 2.8 %copy-start.3 = (s32[2,34,6]{2,1,0:T(8,128)S(1)}, s32[2,34,6]{2,1,0:T(8,128)}, u32[]{:S(2)}) copy-start(s32[2,34,6]{2,1,0:T(8,128)} %constant.20.clone.table) | copy-start | bytes 4900
  6.6 29.3 %collective-permute-start.4 = (bf16[1,528,128]{2,1,0:T(8,128)(2,1)S(1)}, bf16[1,528,128]{2,1,0:T(8,128)(2,1)S(1)}, u32[]{:S(2)}, u32[]{:S(2)}) collective-permute-start(bf16[1,528,128]{2,1,0:T(8,128)(2,1)S(1)} %get-tuple-element.40), channel_id=1, source_target_pairs={{3,8},{5,10},{7,12},{8,3},{10,5},{11,16},{12,7},{13,18},{15,20},{1... | collective-permute-start | bytes 405512 | tf_op jit(solution)/shard_map/ppermute | solution.py:484
  7.3 28.6 %collective-permute-start.1 = (bf16[4,528,128]{2,1,0:T(8,128)(2,1)S(1)}, bf16[4,528,128]{2,1,0:T(8,128)(2,1)S(1)}, u32[]{:S(2)}, u32[]{:S(2)}) collective-permute-start(bf16[4,528,128]{2,1,0:T(8,128)(2,1)S(1)} %fusion.2), channel_id=1, source_target_pairs={{1,2},{2,1},{3,4},{4,3},{5,6},{6,5},{9,10},{10,9},{11,12},{12,11},... | collective-permute-start | bytes 1622024 | tf_op jit(solution)/shard_map/ppermute | solution.py:484
  8.7 27.2 %collective-permute-start.2 = (bf16[4,528,128]{2,1,0:T(8,128)(2,1)S(1)}, bf16[4,528,128]{2,1,0:T(8,128)(2,1)S(1)}, u32[]{:S(2)}, u32[]{:S(2)}) collective-permute-start(bf16[4,528,128]{2,1,0:T(8,128)(2,1)S(1)} %slice_select_fusion), channel_id=1, source_target_pairs={{1,8},{3,10},{5,12},{7,14},{8,1},{9,16},{10,3},{11,18},{12,5},{13,... | collective-permute-start | bytes 1622024 | tf_op jit(solution)/shard_map/ppermute | solution.py:484
  9.4 37.8 %copy-start.2 = (s32[2,22,6]{2,1,0:T(8,128)S(1)}, s32[2,22,6]{2,1,0:T(8,128)}, u32[]{:S(2)}) copy-start(s32[2,22,6]{2,1,0:T(8,128)} %constant.21.clone.table.edge_table) | copy-start | bytes 3172
  35.9 11.3 %collective-permute-start.5 = (bf16[4,528,128]{2,1,0:T(8,128)(2,1)S(1)}, bf16[4,528,128]{2,1,0:T(8,128)(2,1)S(1)}, u32[]{:S(2)}, u32[]{:S(2)}) collective-permute-start(bf16[4,528,128]{2,1,0:T(8,128)(2,1)S(1)} %collective-permute-done.1.first_col), channel_id=1, source_target_pairs={{0,1},{1,0},{2,3},{3,2},{4,5},{5,4},{6,7},{7,6},{8,9},{9,8},{10,11... | collective-permute-start | bytes 1622024 | tf_op jit(solution)/shard_map/ppermute | solution.py:496
  83.0 8.0 %collective-permute-start.6 = (bf16[8,512,128]{2,1,0:T(8,128)(2,1)S(1)}, bf16[8,512,128]{2,1,0:T(8,128)(2,1)S(1)}, u32[]{:S(2)}, u32[]{:S(2)}) collective-permute-start(bf16[8,512,128]{2,1,0:T(8,128)(2,1)S(1)} %get-tuple-element.27.mine), channel_id=1, source_target_pairs={{0,1},{1,0},{2,3},{3,2},{4,5},{5,4},{6,7},{7,6},{8,9},{9,8},{10,11... | collective-permute-start | bytes 3145736 | tf_op jit(solution)/shard_map/ppermute | solution.py:496
  91.5 26.1 %collective-permute-start.7 = (bf16[4,512,128]{2,1,0:T(8,128)(2,1)S(1)}, bf16[4,512,128]{2,1,0:T(8,128)(2,1)S(1)}, u32[]{:S(2)}, u32[]{:S(2)}) collective-permute-start(bf16[4,512,128]{2,1,0:T(8,128)(2,1)S(1)} %fusion.3), channel_id=1, source_target_pairs={{1,2},{2,1},{3,4},{4,3},{5,6},{6,5},{9,10},{10,9},{11,12},{12,11},... | collective-permute-start | bytes 1572872 | tf_op jit(solution)/shard_map/ppermute | solution.py:484
  92.3 25.4 %collective-permute-start.8 = (bf16[4,512,128]{2,1,0:T(8,128)(2,1)S(1)}, bf16[4,512,128]{2,1,0:T(8,128)(2,1)S(1)}, u32[]{:S(2)}, u32[]{:S(2)}) collective-permute-start(bf16[4,512,128]{2,1,0:T(8,128)(2,1)S(1)} %slice_select_fusion.2), channel_id=1, source_target_pairs={{1,8},{3,10},{5,12},{7,14},{8,1},{9,16},{10,3},{11,18},{12,5},{13,... | collective-permute-start | bytes 1572872 | tf_op jit(solution)/shard_map/ppermute | solution.py:484
  93.0 24.7 %collective-permute-start.10 = (bf16[1,512,128]{2,1,0:T(8,128)(2,1)S(1)}, bf16[1,512,128]{2,1,0:T(8,128)(2,1)S(1)}, u32[]{:S(2)}, u32[]{:S(2)}) collective-permute-start(bf16[1,512,128]{2,1,0:T(8,128)(2,1)S(1)} %get-tuple-element.42), channel_id=1, source_target_pairs={{3,8},{5,10},{7,12},{8,3},{10,5},{11,16},{12,7},{13,18},{15,20},{1... | collective-permute-start | bytes 393224 | tf_op jit(solution)/shard_map/ppermute | solution.py:484
  93.6 24.0 %collective-permute-start.9 = (bf16[1,512,128]{2,1,0:T(8,128)(2,1)S(1)}, bf16[1,512,128]{2,1,0:T(8,128)(2,1)S(1)}, u32[]{:S(2)}, u32[]{:S(2)}) collective-permute-start(bf16[1,512,128]{2,1,0:T(8,128)(2,1)S(1)} %get-tuple-element.43), channel_id=1, source_target_pairs={{1,10},{3,12},{5,14},{9,18},{10,1},{11,20},{12,3},{13,22},{14,5},{... | collective-permute-start | bytes 393224 | tf_op jit(solution)/shard_map/ppermute | solution.py:484
  117.6 18.2 %collective-permute-start.11 = (bf16[4,512,128]{2,1,0:T(8,128)(2,1)S(1)}, bf16[4,512,128]{2,1,0:T(8,128)(2,1)S(1)}, u32[]{:S(2)}, u32[]{:S(2)}) collective-permute-start(bf16[4,512,128]{2,1,0:T(8,128)(2,1)S(1)} %collective-permute-done.7.first_col), channel_id=1, source_target_pairs={{0,1},{1,0},{2,3},{3,2},{4,5},{5,4},{6,7},{7,6},{8,9},{9,8},{10,11... | collective-permute-start | bytes 1572872 | tf_op jit(solution)/shard_map/ppermute | solution.py:496
  140.3 6.4 %collective-permute-start.12 = (f32[8,9,64,128]{3,2,1,0:T(8,128)}, f32[8,9,64,128]{3,2,1,0:T(8,128)}, u32[]{:S(2)}, u32[]{:S(2)}) collective-permute-start(f32[8,9,64,128]{3,2,1,0:T(8,128)} %get-tuple-element.39), channel_id=1, source_target_pairs={{0,1},{1,0},{2,3},{3,2},{4,5},{5,4},{6,7},{7,6},{8,9},{9,8},{10,11... | collective-permute-start | bytes 7077896 | tf_op jit(solution)/shard_map/ppermute | solution.py:496

commit v3 on v2

--- a/solution.py
+++ b/solution.py
@@ -13,7 +13,6 @@
 LANES = 128
 PANEL = 8
 BLOCK = 32
-VMEM_BYTES = 50 << 20
 
 
 def lane_copy(value, lane):
@@ -87,14 +86,16 @@
         def _():
             below = square_rows >= first + BLOCK
             inside = (square_lanes >= first) & (square_lanes < first + BLOCK)
+            changes = []
             for b in range(batch):
                 a1, a2, a3 = three_parts(weights[:, b, :])
                 b1, b2, b3 = three_parts(pivots[:, b, :])
                 left = jnp.concatenate([a1, a1, a2, a2, a1, a3], axis=0)
                 right = jnp.concatenate([b1, b2, b1, b2, b3, b1], axis=0)
-                change = lax.dot_general(left, right, (((0,), (0,)), ((), ())), preferred_element_type=jnp.float32)
+                changes.append(lax.dot_general(left, right, (((0,), (0,)), ((), ())), preferred_element_type=jnp.float32))
+            for b in range(batch):
                 now = work[:, b, :]
-                work[:, b, :] = jnp.where(below, jnp.where(inside, 0.0, now) - change, now)
+                work[:, b, :] = jnp.where(below, jnp.where(inside, 0.0, now) - changes[b], now)
 
         return carry
 
@@ -103,9 +104,12 @@
 def orthonormalize(y_ref, out_ref, work, pivots, weights):
     batch, points, rank = y_ref.shape
     for turn in range(2):
+        grams = []
         for b in range(batch):
             data = y_ref[b]
-            work[:, b, :] = lax.dot_general(data, data, (((0,), (0,)), ((), ())), precision=lax.Precision.HIGHEST, preferred_element_type=jnp.float32) * (1.0 / points)
+            grams.append(lax.dot_general(data, data, (((0,), (0,)), ((), ())), precision=lax.Precision.HIGHEST, preferred_element_type=jnp.float32) * (1.0 / points))
+        for b in range(batch):
+            work[:, b, :] = grams[b]
         invert_factors(work, pivots, weights)
         for b in range(batch):
             data = lax.dot_general(y_ref[b], work[:, b, :], (((1,), (1,)), ((), ())), precision=lax.Precision.HIGHEST, preferred_element_type=jnp.float32)
@@ -165,40 +169,46 @@
 def work_lists(tile_side, rows_half, cores):
     chip = [chip_entries(tile_side, rows_half, core) for core in range(cores)]
     edge = [edge_entries(tile_side, rows_half, core) for core in range(cores)]
+    chip = [(centres + singles, pairs) for centres, pairs, singles in chip]
     counts = tuple(len(part) for part in chip[0])
     flat = [sum(parts, []) for parts in chip]
     return np.array(flat, np.int32), counts, np.array(edge, np.int32)
 
 
-def spread_points(coords, box_points):
-    stretch = math.sqrt(box_points) * 4.0
-    return coords.astype(jnp.float32) * stretch
-
-
-def fill_rows(rows, box_coords, own):
+def fill_coords(coords, place, box_coords, stretch):
+    moved = (box_coords - 0.5) * stretch
+    coords[place, 0:2] = moved[0:2]
+    coords[place, 2:3] = moved[2:3] * lift_scale
+
+
+def fill_rows(rows, box_coords, own, soften):
     box_points = box_coords.shape[1]
     turned = jnp.transpose(box_coords)
+    total = soften
     for axis in range(3):
-        rows[own, axis] = jnp.broadcast_to(turned[:, axis : axis + 1], (box_points, LANES))
-
-
-def make_entries(target, slot, rows, own, coords, other, offset_y, offset_x, centre, start, stop):
+        column = jnp.broadcast_to(turned[:, axis : axis + 1], (box_points, LANES))
+        rows[own, axis] = column + column
+        total = total + column * column
+    rows[own, 3] = total
+
+
+def make_entries(target, rows, own, coords, other, shift_y, shift_x):
     box_points = coords.shape[2]
-    stretch = math.sqrt(box_points) * 4.0
-    soften = (0.25 / box_points) * stretch * stretch
-    step = 64
-    for first in range(start, stop, step):
-        for lane in range(0, box_points, LANES):
-            here = pl.ds(lane, LANES)
-            delta_u = (coords[other, 0:1, here] + offset_x) - rows[own, 0, first : first + step, :]
-            delta_v = (coords[other, 1:2, here] + offset_y) - rows[own, 1, first : first + step, :]
-            delta_w = coords[other, 2:3, here] - rows[own, 2, first : first + step, :]
-            values = lax.rsqrt(delta_u * delta_u + delta_v * delta_v + delta_w * delta_w + soften)
-            if centre and lane <= first < lane + LANES:
-                row_ids = lax.broadcasted_iota(jnp.int32, values.shape, 0) + (first - lane)
-                col_ids = lax.broadcasted_iota(jnp.int32, values.shape, 1)
-                values = values + jnp.where(row_ids == col_ids, 1.0, 0.0)
-            target[slot, first : first + step, here] = values.astype(jnp.bfloat16)
+    step = 16
+    columns = []
+    for lane in range(0, box_points, LANES):
+        here = pl.ds(lane, LANES)
+        other_u = coords[other, 0:1, here] + shift_x
+        other_v = coords[other, 1:2, here] + shift_y
+        other_w = coords[other, 2:3, here]
+        squares = other_u * other_u + other_v * other_v + other_w * other_w
+        columns.append([jnp.broadcast_to(value, (step, LANES)) for value in (other_u, other_v, other_w, squares)])
+    for first in range(0, box_points, step):
+        part = slice(first, first + step)
+        row_u, row_v, row_w, row_squares = (rows[own, axis, part, :] for axis in range(4))
+        for strip, (other_u, other_v, other_w, squares) in enumerate(columns):
+            apart = (row_squares + squares) - row_u * other_u - row_v * other_v - row_w * other_w
+            target[part, strip * LANES : (strip + 1) * LANES] = lax.rsqrt(apart).astype(jnp.bfloat16)
 
 
 def list_active(table, core, first, count, mask, active, base):
@@ -214,31 +224,61 @@
     return lax.fori_loop(0, count, check, 0)
 
 
-def run_blocks(active, base, total, begun, body, buffers, store, sems):
-    def step(turn, carry):
-        count = begun + turn
-        slot = lax.rem(count, 2)
-
-        @pl.when(count >= 2)
-        def _():
-            pltpu.make_async_copy(buffers.at[slot], store.at[0], sems.at[slot]).wait()
-
-        index = active[base + turn]
-        body(index, slot)
-        pltpu.make_async_copy(buffers.at[slot], store.at[index], sems.at[slot]).start()
+def run_blocks(active, base, total, make, use, store, pair, sems):
+    def entry(turn):
+        return active[base + jnp.minimum(turn, total - 1)]
+
+    def send(side, slot, turn):
+        return pltpu.make_async_copy(pair[side].at[slot], store.at[entry(turn)], sems.at[side, slot])
+
+    @pl.when(total > 0)
+    def _():
+        make(entry(0), pair[0].at[0])
+        send(0, 0, 0).start()
+
+    def step(half_turn, carry):
+        even = 2 * half_turn
+        odd, after = even + 1, even + 2
+        slot = lax.rem(half_turn, 2)
+
+        @pl.when(half_turn > 1)
+        def _():
+            send(1, slot, 0).wait()
+
+        make(entry(odd), pair[1].at[slot])
+        use(entry(even), pair[0].at[slot], 1.0)
+
+        @pl.when(odd < total)
+        def _():
+            send(1, slot, odd).start()
+
+        @pl.when(half_turn > 0)
+        def _():
+            send(0, 1 - slot, 0).wait()
+
+        make(entry(after), pair[0].at[1 - slot])
+        use(entry(odd), pair[1].at[slot], jnp.where(odd < total, 1.0, 0.0))
+
+        @pl.when(after < total)
+        def _():
+            send(0, 1 - slot, after).start()
+
         return carry
 
-    lax.fori_loop(0, total, step, 0)
-    return begun + total
-
-
-def drain(begun, buffers, store, sems):
-    for back in (1, 2):
-
-        @pl.when(begun >= back)
-        def _():
-            slot = lax.rem(begun - back, 2)
-            pltpu.make_async_copy(buffers.at[slot], store.at[0], sems.at[slot]).wait()
+    turns = (total + 1) // 2
+    lax.fori_loop(0, turns, step, 0)
+
+    @pl.when(turns > 0)
+    def _():
+        send(0, lax.rem(turns - 1, 2), 0).wait()
+
+    @pl.when(turns > 1)
+    def _():
+        send(1, lax.rem(turns, 2), 0).wait()
+
+    @pl.when((turns > 0) & (2 * turns == total))
+    def _():
+        send(1, lax.rem(turns - 1, 2), 0).wait()
 
 
 def place(table, core, index):
@@ -246,7 +286,7 @@
 
 
 def chip_sketch_kernel(counts, core_ref, mask, table, points, mine, theirs, y_ref, store,
-                       omega, omega_t, coords, rows, turned_y, buffers, active, sems, load_sems):
+                       omega, omega_t, coords, rows, turned_y, buffer_a, buffer_b, active, sems, load_sems):
     core = core_ref[0]
     chip_boxes, _, box_points = points.shape
     own_boxes, _, skel_rank = y_ref.shape
@@ -258,48 +298,42 @@
     for load in loads:
         load.start()
     stretch = math.sqrt(box_points) * 4.0
+    soften = (0.25 / box_points) * stretch * stretch
     for box in range(chip_boxes):
-        spread = points[box].astype(jnp.float32) * stretch
-        coords[box, 0:2] = spread[0:2]
-        coords[box, 2:3] = spread[2:3] * lift_scale
+        fill_coords(coords, box, points[box].astype(jnp.float32), stretch)
     for own in range(own_boxes):
-        fill_rows(rows, coords[core * own_boxes + own], own)
+        fill_rows(rows, coords[core * own_boxes + own], own, soften)
     for load in loads:
         load.wait()
     for own in range(own_boxes):
-        omega_t[own] = jnp.transpose(omega[core * own_boxes + own])
+        values = omega[core * own_boxes + own]
+        omega_t[own] = jnp.transpose(values)
+        y_ref[own] = values.astype(jnp.float32)
         turned_y[own] = jnp.zeros((skel_rank, box_points), jnp.float32)
 
-    part = box_points // 2
-
-    def block(kind, index, slot):
-        own, other, offset_y, offset_x, _, mate = place(table, core, index)
+    def make(index, target):
+        own, other, offset_y, offset_x, _, _ = place(table, core, index)
         shift_y, shift_x = offset_y.astype(jnp.float32) * stretch, offset_x.astype(jnp.float32) * stretch
-        for first in range(0, box_points, part):
-            make_entries(buffers, slot, rows, own, coords, other, shift_y, shift_x, kind == 0, first, first + part)
-            values = buffers[slot, first : first + part, :]
-            found = jnp.dot(values, omega[other], preferred_element_type=jnp.float32)
-            if kind == 0:
-                y_ref[own, first : first + part, :] = found
-            else:
-                y_ref[own, first : first + part, :] += found
-            if kind == 1:
-                turned_y[mate] += jnp.dot(
-                    omega_t[own, :, first : first + part], values, preferred_element_type=jnp.float32
-                )
-
-    begun, first = 0, 0
-    for kind, count in enumerate(counts):
+        make_entries(target, rows, own, coords, other, shift_y, shift_x)
+
+    def use(both, index, buffer, weight):
+        own, other, _, _, _, mate = place(table, core, index)
+        values = buffer[...]
+        y_ref[own] += jnp.dot(values, omega[other], preferred_element_type=jnp.float32) * weight
+        if both:
+            turned_y[mate] += jnp.dot(omega_t[own], values, preferred_element_type=jnp.float32) * weight
+
+    first = 0
+    for both, count in enumerate(counts):
         total = list_active(table, core, first, count, mask, active, first)
-        begun = run_blocks(active, first, total, begun, functools.partial(block, kind), buffers, store, sems)
+        run_blocks(active, first, total, make, functools.partial(use, both), store, (buffer_a, buffer_b), sems)
         first += count
     for own in range(own_boxes):
         y_ref[own] += jnp.transpose(turned_y[own])
-    drain(begun, buffers, store, sems)
 
 
 def edge_coords(coords, extended, box, box_points, stretch):
-    packed = extended[box, box_points : box_points + 16, :].astype(jnp.float32) * stretch
+    packed = (extended[box, box_points : box_points + 16, :].astype(jnp.float32) - 0.5) * stretch
     strips = box_points // LANES
     for axis in range(3):
         for strip in range(strips):
@@ -320,7 +354,7 @@
 
 
 def edge_sketch_kernel(core_ref, mask, table, points, sketched, first_col, second_col, row, corner_a, corner_b,
-                       basis, store, extended, coords, rows, y_ref, buffers, active, sems, load_sems,
+                       basis, store, extended, coords, rows, y_ref, buffer_a, buffer_b, active, sems, load_sems,
                        work, pivots, weights):
     core = core_ref[0]
     own_boxes, box_points, skel_rank = y_ref.shape
@@ -329,144 +363,206 @@
     for load in loads:
         load.start()
     stretch = math.sqrt(box_points) * 4.0
+    soften = (0.25 / box_points) * stretch * stretch
     for own in range(own_boxes):
-        spread = points[core * own_boxes + own].astype(jnp.float32) * stretch
-        coords[0, 0:2] = spread[0:2]
-        coords[0, 2:3] = spread[2:3] * lift_scale
-        fill_rows(rows, coords[0], own)
+        fill_coords(coords, own, points[core * own_boxes + own].astype(jnp.float32), stretch)
+        fill_rows(rows, coords[own], own, soften)
     for load in loads:
         load.wait()
     for box in range(extended.shape[0]):
         edge_coords(coords, extended, box, box_points, stretch)
-    part = box_points // 2
-
-    def block(index, slot):
+
+    def make(index, target):
         own, other, offset_y, offset_x, _, _ = place(table, core, index)
         shift_y, shift_x = offset_y.astype(jnp.float32) * stretch, offset_x.astype(jnp.float32) * stretch
-        for first in range(0, box_points, part):
-            make_entries(buffers, slot, rows, own, coords, other, shift_y, shift_x, False, first, first + part)
-            values = buffers[slot, first : first + part, :]
-            y_ref[own, first : first + part, :] += jnp.dot(
-                values, extended[other, 0:box_points, :], preferred_element_type=jnp.float32
-            )
+        make_entries(target, rows, own, coords, other, shift_y, shift_x)
+
+    def use(index, buffer, weight):
+        own, other, _, _, _, _ = place(table, core, index)
+        y_ref[own] += jnp.dot(
+            buffer[...], extended[other, 0:box_points, :], preferred_element_type=jnp.float32
+        ) * weight
 
     total = list_active(table, core, 0, table.shape[1], mask, active, 0)
-    begun = run_blocks(active, 0, total, 0, block, buffers, store, sems)
+    run_blocks(active, 0, total, make, use, store, (buffer_a, buffer_b), sems)
     orthonormalize(y_ref, basis, work, pivots, weights)
-    drain(begun, buffers, store, sems)
-
-
-def run_stored(active, base, total, buffers, store, sems, depth, body):
+
+
+def run_stored(active, base, total, buffers, store, sems, depth, project, use, pair):
+    def entry(turn):
+        return active[base + jnp.minimum(turn, total - 1)]
+
     def fetch(turn):
         slot = lax.rem(turn, depth)
         return pltpu.make_async_copy(store.at[active[base + turn]], buffers.at[slot], sems.at[slot])
 
+    def arrive(turn, side):
+        @pl.when(turn < total)
+        def _():
+            fetch(turn).wait()
+
+        project(entry(turn), lax.rem(jnp.minimum(turn, total - 1), depth), pair[side])
+
     for turn in range(depth - 1):
 
         @pl.when(turn < total)
         def _():
             fetch(turn).start()
 
-    def step(turn, carry):
-        @pl.when(turn + depth - 1 < total)
-        def _():
-            fetch(turn + depth - 1).start()
-
-        fetch(turn).wait()
-        body(active[base + turn], lax.rem(turn, depth))
+    @pl.when(total > 0)
+    def _():
+        arrive(0, 0)
+
+    def step(half_turn, carry):
+        even = 2 * half_turn
+        for ahead in (0, 1):
+
+            @pl.when(even + ahead + depth - 1 < total)
+            def _():
+                fetch(even + ahead + depth - 1).start()
+
+            arrive(even + ahead + 1, 1 - ahead)
+            use(entry(even + ahead), pair[ahead])
         return carry
 
-    lax.fori_loop(0, total, step, 0)
+    lax.fori_loop(0, (total + 1) // 2, step, 0)
 
 
 def chip_couple_kernel(counts, depth, core_ref, mask, table, edge_table, mine, theirs, store, edge_store,
-                       keep, give, projected, basis, basis_t, buffers, active, result, sems):
+                       full, give, projected, basis, basis_t, buffers, active, found, ray_a, ray_b, sems, out_sems):
     core = core_ref[0]
     own_boxes, box_points, skel_rank = mine.shape
-    half = keep.shape[2]
+    half = give.shape[2]
     basis[pl.ds(core * own_boxes, own_boxes)] = mine[...]
     basis[pl.ds((1 - core) * own_boxes, own_boxes)] = theirs[...]
     for own in range(own_boxes):
         basis_t[own] = jnp.transpose(mine[own])
-        keep[own] = jnp.zeros(keep.shape[1:], jnp.float32)
-        give[own] = jnp.zeros(give.shape[1:], jnp.float32)
-
-    def put(own, slot, values):
-        result[...] = values
-        keep[own, slot] = result[pl.ds(pl.multiple_of(core * half, half), half), :]
-        give[own, slot] = result[pl.ds(pl.multiple_of((1 - core) * half, half), half), :]
-
-    def block(kind, index, slot):
+
+    def clear(index, carry):
+        own, stencil = index // 9, lax.rem(index, 9)
+
+        @pl.when(mask[own, stencil] == 0)
+        def _():
+            found[own, stencil] = jnp.zeros((skel_rank, skel_rank), jnp.float32)
+
+        return carry
+
+    lax.fori_loop(0, own_boxes * 9, clear, 0)
+
+    def project(index, slot, target):
+        own, stencil = table[core, index, 0], table[core, index, 4]
+        centre = jnp.where(stencil == 4, 1.0, 0.0)
+        values = jnp.dot(basis_t[own], buffers[slot], preferred_element_type=jnp.float32)
+        target[...] = (values + basis_t[own].astype(jnp.float32) * centre).astype(jnp.bfloat16)
+
+    def use(both, index, rays):
         own, other, _, _, stencil, mate = place(table, core, index)
-        rays = jnp.dot(basis_t[own], buffers[slot], preferred_element_type=jnp.float32).astype(jnp.bfloat16)
-        values = jnp.dot(rays, basis[other], preferred_element_type=jnp.float32) * (1.0 / box_points)
-        put(own, stencil, values)
-        if kind == 1:
-            put(mate, 8 - stencil, jnp.transpose(values))
-
-    def edge_block(index, slot):
+        values = jnp.dot(rays[...], basis[other], preferred_element_type=jnp.float32) * (1.0 / box_points)
+        found[own, stencil] = values
+        if both:
+            found[mate, 8 - stencil] = jnp.transpose(values)
+
+    first = 0
+    for both, count in enumerate(counts):
+        total = list_active(table, core, first, count, mask, active, first)
+        run_stored(active, first, total, buffers, store, sems, depth, project, functools.partial(use, both), (ray_a, ray_b))
+        first += count
+
+    copies = []
+    for own in range(own_boxes):
+        for side, (target, at) in enumerate(((full, core * own_boxes + own), (give, own))):
+            rows_of = core if side == 0 else 1 - core
+            copies.append(pltpu.make_async_copy(
+                found.at[own, :, pl.ds(pl.multiple_of(rows_of * half, half), half), :],
+                target.at[at],
+                out_sems.at[2 * own + side],
+            ))
+    for copy in copies:
+        copy.start()
+
+    def edge_project(index, slot, target):
         own = edge_table[core, index, 0]
         projected[index] = jnp.dot(
             basis_t[own], buffers[slot], preferred_element_type=jnp.float32
         ).astype(jnp.bfloat16)
 
-    first = 0
-    for kind, count in enumerate(counts):
-        total = list_active(table, core, first, count, mask, active, first)
-        run_stored(active, first, total, buffers, store, sems, depth, functools.partial(block, kind))
-        first += count
     total = list_active(edge_table, core, 0, edge_table.shape[1], mask, active, 0)
-    run_stored(active, 0, total, buffers, edge_store, sems, depth, edge_block)
+    run_stored(active, 0, total, buffers, edge_store, sems, depth, edge_project, lambda index, rays: None, (ray_a, ray_b))
+    for copy in copies:
+        copy.wait()
 
 
 def edge_couple_kernel(core_ref, mask, edge_table, projected, first_col, second_col, row, corner_a, corner_b,
-                       keep_in, give_in, keep, give, extended, results, active, load_sems, sems):
+                       taken, full_in, full, give, extended, results, active, load_sems, sems, move_sems):
     core = core_ref[0]
     box_points = projected.shape[2]
-    half = keep.shape[2]
+    own_boxes, _, half, _ = taken.shape
     loads = load_edges(core, (first_col, second_col, row, corner_a, corner_b), extended, load_sems)
-    for load in loads:
-        load.start()
+    moves = [
+        pltpu.make_async_copy(taken.at[own], full.at[(1 - core) * own_boxes + own], move_sems.at[own])
+        for own in range(own_boxes)
+    ]
+    for copy in loads + moves:
+        copy.start()
     total = list_active(edge_table, core, 0, edge_table.shape[1], mask, active, 0)
     for load in loads:
         load.wait()
 
-    def copies(turn):
+    def result_copy(turn):
         index = active[turn]
         own, stencil = edge_table[core, index, 0], edge_table[core, index, 4]
         mine = results.at[turn, pl.ds(pl.multiple_of(core * half, half), half), :]
-        theirs = results.at[turn, pl.ds(pl.multiple_of((1 - core) * half, half), half), :]
-        return (
-            pltpu.make_async_copy(mine, keep.at[own, stencil], sems.at[turn]),
-            pltpu.make_async_copy(theirs, give.at[own, stencil], sems.at[results.shape[0] + turn]),
-        )
+        return pltpu.make_async_copy(mine, full.at[core * own_boxes + own, stencil], sems.at[turn])
 
     def step(turn, carry):
         index = active[turn]
-        other = edge_table[core, index, 1]
         results[turn] = jnp.dot(
-            projected[index], extended[other], preferred_element_type=jnp.float32
+            projected[index], extended[edge_table[core, index, 1]], preferred_element_type=jnp.float32
         ) * (1.0 / box_points)
-        for copy in copies(turn):
-            copy.start()
+        give[index] = results[turn, pl.ds(pl.multiple_of((1 - core) * half, half), half), :]
+        result_copy(turn).start()
         return carry
 
     def finish(turn, carry):
-        for copy in copies(turn):
-            copy.wait()
+        result_copy(turn).wait()
         return carry
 
     lax.fori_loop(0, total, step, 0)
     lax.fori_loop(0, total, finish, 0)
+    for move in moves:
+        move.wait()
+
+
+def settle_kernel(core_ref, mask, edge_table, taken, full_in, full, sems):
+    other = 1 - core_ref[0]
+    own_boxes = full.shape[0] // 2
+
+    def each(act):
+        def step(index, carry):
+            own, stencil = edge_table[other, index, 0], edge_table[other, index, 4]
+
+            @pl.when(mask[other * own_boxes + own, stencil] != 0)
+            def _():
+                act(pltpu.make_async_copy(
+                    taken.at[index], full.at[other * own_boxes + own, stencil], sems.at[index]
+                ))
+
+            return carry
+
+        lax.fori_loop(0, edge_table.shape[1], step, 0)
+
+    each(lambda copy: copy.start())
+    each(lambda copy: copy.wait())
 
 
 SMEM = pl.BlockSpec(memory_space=pltpu.SMEM)
 VMEM = pl.BlockSpec(memory_space=pltpu.VMEM)
 ANY = pl.BlockSpec(memory_space=pl.ANY)
-
-
-def params():
-    return pltpu.CompilerParams(vmem_limit_bytes=VMEM_BYTES)
+HBM = pl.BlockSpec(memory_space=pltpu.HBM)
+
+
+def params(mebibytes):
+    return pltpu.CompilerParams(vmem_limit_bytes=mebibytes << 20)
 
 
 def exchange(boxes, core, grid_side):
@@ -532,19 +628,20 @@
             jax.ShapeDtypeStruct((chip_blocks, box_points, box_points), bf16),
         ),
         in_specs=[SMEM, SMEM, SMEM, VMEM, ANY, ANY],
-        out_specs=(VMEM, ANY),
+        out_specs=(VMEM, HBM),
         scratch_shapes=[
             pltpu.VMEM((chip_boxes, box_points, skel_rank), bf16),
             pltpu.VMEM((own_boxes, skel_rank, box_points), bf16),
             pltpu.VMEM((chip_boxes, 8, box_points), f32),
-            pltpu.VMEM((own_boxes, 3, box_points, LANES), f32),
+            pltpu.VMEM((own_boxes, 4, box_points, LANES), f32),
             pltpu.VMEM((own_boxes, skel_rank, box_points), f32),
             pltpu.VMEM((2, box_points, box_points), bf16),
+            pltpu.VMEM((2, box_points, box_points), bf16),
             pltpu.SMEM((chip_blocks,), jnp.int32),
-            pltpu.SemaphoreType.DMA((2,)),
+            pltpu.SemaphoreType.DMA((2, 2)),
             pltpu.SemaphoreType.DMA((2,)),
         ],
-        compiler_params=params(),
+        compiler_params=params(50),
         cost_estimate=pl.CostEstimate(flops=8 * 10**9, bytes_accessed=24 * 10**6, transcendentals=0),
         name="chip_sketch",
     )(core_arg, own_mask, chip_table, points, sketch, theirs)
@@ -562,17 +659,18 @@
         scratch_shapes=[
             pltpu.VMEM((edge_boxes, box_points + 16, skel_rank), bf16),
             pltpu.VMEM((edge_boxes, 8, box_points), f32),
-            pltpu.VMEM((own_boxes, 3, box_points, LANES), f32),
+            pltpu.VMEM((own_boxes, 4, box_points, LANES), f32),
             pltpu.VMEM((own_boxes, box_points, skel_rank), f32),
             pltpu.VMEM((2, box_points, box_points), bf16),
+            pltpu.VMEM((2, box_points, box_points), bf16),
             pltpu.SMEM((edge_blocks,), jnp.int32),
-            pltpu.SemaphoreType.DMA((2,)),
+            pltpu.SemaphoreType.DMA((2, 2)),
             pltpu.SemaphoreType.DMA((6,)),
             pltpu.VMEM((skel_rank, own_boxes, skel_rank), f32),
             pltpu.VMEM((BLOCK, own_boxes, skel_rank), f32),
             pltpu.VMEM((BLOCK, own_boxes, skel_rank), f32),
         ],
-        compiler_params=params(),
+        compiler_params=params(24),
         name="edge_sketch",
     )(core_arg, own_mask, edge_table, points, sketched, col, second_col, row, corner_a, corner_b)
 
@@ -583,51 +681,65 @@
         jnp.concatenate([other_basis, basis], axis=0),
     ).reshape(tile_side, tile_side, box_points, skel_rank)
     col, row, corner_a, corner_b = exchange(whole, core, grid_side)
-    depth = 4
-    coupling_shape = jax.ShapeDtypeStruct((own_boxes, 9, half_rank, skel_rank), f32)
-    keep, give, projected = pl.pallas_call(
+    depth = 8
+    coupling_shape = jax.ShapeDtypeStruct((chip_boxes, 9, half_rank, skel_rank), f32)
+    coupling, give, projected = pl.pallas_call(
         functools.partial(chip_couple_kernel, counts, depth),
         out_shape=(
             coupling_shape,
-            coupling_shape,
+            jax.ShapeDtypeStruct((own_boxes, 9, half_rank, skel_rank), f32),
             jax.ShapeDtypeStruct((edge_blocks, skel_rank, box_points), bf16),
         ),
-        in_specs=[SMEM] * 4 + [VMEM, VMEM, ANY, ANY],
-        out_specs=(VMEM, VMEM, VMEM),
+        in_specs=[SMEM] * 4 + [VMEM, VMEM, HBM, ANY],
+        out_specs=(ANY, ANY, VMEM),
         scratch_shapes=[
             pltpu.VMEM((chip_boxes, box_points, skel_rank), bf16),
             pltpu.VMEM((own_boxes, skel_rank, box_points), bf16),
             pltpu.VMEM((depth, box_points, box_points), bf16),
             pltpu.SMEM((max(chip_blocks, edge_blocks),), jnp.int32),
-            pltpu.VMEM((skel_rank, skel_rank), f32),
+            pltpu.VMEM((own_boxes, 9, skel_rank, skel_rank), f32),
+            pltpu.VMEM((skel_rank, box_points), bf16),
+            pltpu.VMEM((skel_rank, box_points), bf16),
             pltpu.SemaphoreType.DMA((depth,)),
+            pltpu.SemaphoreType.DMA((2 * own_boxes,)),
         ],
-        compiler_params=params(),
+        compiler_params=params(20),
         cost_estimate=pl.CostEstimate(flops=8 * 10**9, bytes_accessed=32 * 10**6, transcendentals=0),
         name="chip_couple",
     )(core_arg, own_mask, chip_table, edge_table, basis, other_basis, store, edge_store)
 
-    col, row, corner_a, corner_b, projected = lax.optimization_barrier((col, row, corner_a, corner_b, projected))
+    col, row, corner_a, corner_b, projected, give = lax.optimization_barrier(
+        (col, row, corner_a, corner_b, projected, give)
+    )
     second_col = swap(col)
-    keep, give = pl.pallas_call(
+    taken = swap(give)
+    coupling, give = pl.pallas_call(
         edge_couple_kernel,
-        out_shape=(coupling_shape, coupling_shape),
+        out_shape=(coupling_shape, jax.ShapeDtypeStruct((edge_blocks, half_rank, skel_rank), f32)),
         in_specs=[SMEM] * 3 + [VMEM] + [ANY] * 7,
-        out_specs=(ANY, ANY),
+        out_specs=(ANY, VMEM),
         scratch_shapes=[
             pltpu.VMEM((edge_boxes, box_points, skel_rank), bf16),
             pltpu.VMEM((edge_blocks, skel_rank, skel_rank), f32),
             pltpu.SMEM((edge_blocks,), jnp.int32),
             pltpu.SemaphoreType.DMA((5,)),
-            pltpu.SemaphoreType.DMA((2 * edge_blocks,)),
+            pltpu.SemaphoreType.DMA((edge_blocks,)),
+            pltpu.SemaphoreType.DMA((own_boxes,)),
         ],
-        input_output_aliases={9: 0, 10: 1},
-        compiler_params=params(),
+        input_output_aliases={10: 0},
+        compiler_params=params(20),
         name="edge_couple",
-    )(core_arg, own_mask, edge_table, projected, col, second_col, row, corner_a, corner_b, keep, give)
-
+    )(core_arg, own_mask, edge_table, projected, col, second_col, row, corner_a, corner_b, taken, coupling)
     taken = swap(give)
-    coupling = jnp.where(low, jnp.concatenate([keep, taken], axis=0), jnp.concatenate([taken, keep], axis=0))
+    coupling = pl.pallas_call(
+        settle_kernel,
+        out_shape=coupling_shape,
+        in_specs=[SMEM] * 3 + [VMEM, ANY],
+        out_specs=ANY,
+        scratch_shapes=[pltpu.SemaphoreType.DMA((edge_blocks,))],
+        input_output_aliases={4: 0},
+        name="settle",
+    )(core_arg, near_mask, edge_table, taken, coupling)
     basis_out = lax.dynamic_slice_in_dim(
         whole.reshape(chip_boxes, box_points, skel_rank), core * half_points, half_points, 1
     )

time: 156 us -> 150 us (0.962)
  other arithmetic: 10.8 us -> 3.29 us
  local copies, waits for them, and re-layouts: 1.99 us -> 4.26 us
  Pallas kernels: 90.1 us -> 87.9 us
    select_n x1 -> x0, other arithmetic: 7.6 us -> none  [body(): jnp.where(low, jnp.concatenate([keep, taken], axis=0), jnp.concatenate([t...]
    pallas_call x1, Pallas kernels: 23.3 us -> 18.6 us  [body(): pl.pallas_call(functools.partial(chip_couple_kernel, counts, depth), out_...]
    unnamed x9, local copies, waits for them, and re-layouts: 0.87 us -> 2.45 us
    pallas_call x1 -> x2, Pallas kernels: 4.48 us -> 5.83 us  [the longest x1 3.54 us: body(): pl.pallas_call(edge_couple_kernel, out_shape=(coupling_shape, jax.ShapeDt...]
    ppermute x5 -> x6, starting transfers between devices: 34.5 us -> 35 us  [swap(): return lax.ppermute(value, 'col', [(0, 1), (1, 0)])]
    ppermute x5 -> x6, waiting for transfers between devices: 10.4 us -> 10.5 us  [swap(): return lax.ppermute(value, 'col', [(0, 1), (1, 0)])]
  transfers between devices with their start and end apart: 13 -> 14, of which waited for: 5 -> 5; matrix products, arithmetic and copies ran while one was open for 2% -> 2% of each run, Pallas kernels for 32% -> 31%
where the time goes in v3:
time: 150 us; the launch traced here: 148 us
  Pallas kernels  87.9 us (59%)
  starting transfers between devices  40.5 us (27%)
  waiting for transfers between devices  10.5 us (7%)
  local copies, waits for them, and re-layouts  4.26 us (3%)
  other arithmetic  3.29 us (2%)
    pallas_call x1, Pallas kernels, body(): pl.pallas_call(edge_sketch_kernel, out_shape=(jax.ShapeDtypeStruct((own_b...  35.6 us
    ppermute x6, starting transfers between devices, swap(): return lax.ppermute(value, 'col', [(0, 1), (1, 0)])  35 us
    pallas_call x1, Pallas kernels, body(): pl.pallas_call(functools.partial(chip_sketch_kernel, counts), out_shape=(...  27.9 us
    pallas_call x1, Pallas kernels, body(): pl.pallas_call(functools.partial(chip_couple_kernel, counts, depth), out_...  18.6 us
    ppermute x6, waiting for transfers between devices, swap(): return lax.ppermute(value, 'col', [(0, 1), (1, 0)])  10.5 us
    ppermute x8, starting transfers between devices, send(): return lax.ppermute(piece, ('box', 'col'), pairs)  5.59 us
    pallas_call x1, Pallas kernels, body(): pl.pallas_call(edge_couple_kernel, out_shape=(coupling_shape, jax.ShapeDt...  3.54 us
  transfers between devices with their start and end apart: 14, of which 5 were waited for; matrix products, arithmetic and copies ran while one was open for 2% of the time, Pallas kernels for 31%

profile of v3, /device:TPU:0, one launch (start us, length us, event | category | flops | bytes accessed | tf_op | source)
XLA Modules:
  0.0 147.6 jit_solution(9838133886673537069)
XLA Ops:
  0.6 0.5 collective-permute-start
  1.1 0.8 copy.14.points
  2.1 0.7 constant_dynamic-slice_fusion.1.mask
  2.8 0.9 collective-permute-done.theirs
  3.6 2.1 %fusion.1 = bf16[4,4,528,128]{3,2,1,0:T(8,128)(2,1)S(1)} fusion(bf16[4,4,16,128]{3,2,1,0:T(8,128)(2,1)S(1)} %bitcast.21, bf16[4,4,256,128]{3,2,1,0:T(8,128)(2,1)S(1)} %bitcast.18, bf16[4,4,256,128]{3,2,1,0:T(8,128)(2,1)} %bitcast.17, pred[]{:T(512)S(6)} %eq.2), kind=kLoop, calls=%fused_computation.5 | loop fusion | flops 12976128 | bytes 4325377 | tf_op jit(solution)/shard_map/jit(_where)/select_n | solution.py:616
  5.8 0.8 collective-permute-start.3
  6.7 0.7 collective-permute-start.4
  7.3 0.7 collective-permute-start.1
  8.1 0.6 fusion
  8.7 0.1 slice_select_fusion
  8.7 0.7 collective-permute-start.2
  9.5 27.9 %chip_sketch.1 = (f32[8,512,128]{2,1,0:T(8,128)}, bf16[34,512,512]{2,1,0:T(8,128)(2,1)}) custom-call(s32[1]{0:T(128)} %bitcast.core_ref, s32[8,9]{1,0:T(8,128)S(1)} %constant_dynamic-slice_fusion.1.mask, s32[2,34,6]{2,1,0:T(8,128)S(1)} %copy-done.3, bf16[16,3,512]{2,1,0:T(4,128)(2,1)S(1)} %copy.14.points, bf16[16,256,128]{2,1,0:T(8,128)(2,1)S(1)} %copy-done, ...), custom_call_target="tpu_custom_call" | custom-call | flops 8000000000 | bytes 24000000 | tf_op jit(solution)/shard_map/chip_sketch/pallas_call | solution.py:624
  37.4 11.7 %collective-permute-start.5 = (bf16[4,528,128]{2,1,0:T(8,128)(2,1)S(1)}, bf16[4,528,128]{2,1,0:T(8,128)(2,1)S(1)}, u32[]{:S(2)}, u32[]{:S(2)}) collective-permute-start(bf16[4,528,128]{2,1,0:T(8,128)(2,1)S(1)} %collective-permute-done.1.first_col), channel_id=1, source_target_pairs={{0,1},{1,0},{2,3},{3,2},{4,5},{5,4},{6,7},{7,6},{8,9},{9,8},{10,11... | collective-permute-start | bytes 1622024 | tf_op jit(solution)/shard_map/ppermute | solution.py:592
  49.1 1.6 %collective-permute-done.5.second_col = bf16[4,528,128]{2,1,0:T(8,128)(2,1)S(1)} collective-permute-done((bf16[4,528,128]{2,1,0:T(8,128)(2,1)S(1)}, bf16[4,528,128]{2,1,0:T(8,128)(2,1)S(1)}, u32[]{:S(2)}, u32[]{:S(2)}) %collective-permute-start.5) | collective-permute-done | bytes 540704 | tf_op jit(solution)/shard_map/ppermute | solution.py:592
  50.6 1.6 %copy-done.1 = f32[8,512,128]{2,1,0:T(8,128)S(1)} copy-done((f32[8,512,128]{2,1,0:T(8,128)S(1)}, f32[8,512,128]{2,1,0:T(8,128)}, u32[]{:S(2)}) %copy-start.1) | copy-done | bytes 2097176
  52.2 35.6 %edge_sketch.1 = (bf16[8,512,128]{2,1,0:T(8,128)(2,1)S(1)}, bf16[22,512,512]{2,1,0:T(8,128)(2,1)S(1)}) custom-call(s32[1]{0:T(128)} %bitcast.core_ref, s32[8,9]{1,0:T(8,128)S(1)} %constant_dynamic-slice_fusion.1.mask, s32[2,22,6]{2,1,0:T(8,128)S(1)} %copy-done.2, bf16[16,3,512]{2,1,0:T(4,128)(2,1)S(1)} %copy.14.points, f32[8,512,128]{2,1,0:T(8,128)S(1)} %copy-done.1, ...), custom_call_target="tpu_custom_call" | custom-call | tf_op jit(solution)/shard_map/edge_sketch/pallas_call | solution.py:651
  87.8 4.3 %collective-permute-start.6 = (bf16[8,512,128]{2,1,0:T(8,128)(2,1)S(1)}, bf16[8,512,128]{2,1,0:T(8,128)(2,1)S(1)}, u32[]{:S(2)}, u32[]{:S(2)}) collective-permute-start(bf16[8,512,128]{2,1,0:T(8,128)(2,1)S(1)} %get-tuple-element.28.mine), channel_id=1, source_target_pairs={{0,1},{1,0},{2,3},{3,2},{4,5},{5,4},{6,7},{7,6},{8,9},{9,8},{10,11... | collective-permute-start | bytes 3145736 | tf_op jit(solution)/shard_map/ppermute | solution.py:592
  92.2 2.3 %collective-permute-done.6.theirs = bf16[8,512,128]{2,1,0:T(8,128)(2,1)S(1)} collective-permute-done((bf16[8,512,128]{2,1,0:T(8,128)(2,1)S(1)}, bf16[8,512,128]{2,1,0:T(8,128)(2,1)S(1)}, u32[]{:S(2)}, u32[]{:S(2)}) %collective-permute-start.6) | collective-permute-done | bytes 1048608 | tf_op jit(solution)/shard_map/ppermute | solution.py:592
  94.5 0.3 maximum_select_fusion
  94.9 0.7 collective-permute-start.7
  95.7 0.7 collective-permute-start.8
  96.4 0.7 collective-permute-start.10
  97.0 0.7 collective-permute-start.9
  97.7 18.6 %chip_couple.1 = (f32[16,9,64,128]{3,2,1,0:T(8,128)}, f32[8,9,64,128]{3,2,1,0:T(8,128)S(1)}, bf16[22,128,512]{2,1,0:T(8,128)(2,1)S(1)}) custom-call(s32[1]{0:T(128)} %bitcast.core_ref, s32[8,9]{1,0:T(8,128)S(1)} %constant_dynamic-slice_fusion.1.mask, s32[2,34,6]{2,1,0:T(8,128)S(1)} %copy-done.3, s32[2,22,6]{2,1,0:T(8,128)S(1)} %copy-done.2, ...), custom_call_target="tpu_custom_call" | custom-call | flops 8000000000 | bytes 32000000 | tf_op jit(solution)/shard_map/chip_couple/pallas_call | solution.py:686
  116.3 16.5 %collective-permute-start.12 = (f32[8,9,64,128]{3,2,1,0:T(8,128)S(1)}, f32[8,9,64,128]{3,2,1,0:T(8,128)S(1)}, u32[]{:S(2)}, u32[]{:S(2)}) collective-permute-start(f32[8,9,64,128]{3,2,1,0:T(8,128)S(1)} %get-tuple-element.38), channel_id=1, source_target_pairs={{0,1},{1,0},{2,3},{3,2},{4,5},{5,4},{6,7},{7,6},{8,9},{9,8},{10,11... | collective-permute-start | bytes 7077896 | tf_op jit(solution)/shard_map/ppermute | solution.py:592
  132.8 0.1 collective-permute-start.11
  132.9 4.8 %collective-permute-done.11.second_col = bf16[4,512,128]{2,1,0:T(8,128)(2,1)S(1)} collective-permute-done((bf16[4,512,128]{2,1,0:T(8,128)(2,1)S(1)}, bf16[4,512,128]{2,1,0:T(8,128)(2,1)S(1)}, u32[]{:S(2)}, u32[]{:S(2)}) %collective-permute-start.11) | collective-permute-done | bytes 524320 | tf_op jit(solution)/shard_map/ppermute | solution.py:592
  137.7 3.5 %edge_couple.1 = (f32[16,9,64,128]{3,2,1,0:T(8,128)}, f32[22,64,128]{2,1,0:T(8,128)S(1)}) custom-call(s32[1]{0:T(128)} %bitcast.core_ref, s32[8,9]{1,0:T(8,128)S(1)} %constant_dynamic-slice_fusion.1.mask, s32[2,22,6]{2,1,0:T(8,128)S(1)} %copy-done.2, bf16[22,128,512]{2,1,0:T(8,128)(2,1)S(1)} %get-tuple-element.33.projected, ...), custom_call_target="tpu_custom_call", output_to_operand_aliasing={{0}: (10, {})} | custom-call | tf_op jit(solution)/shard_map/edge_couple/pallas_call | solution.py:716
  141.2 1.9 %collective-permute-start.13 = (f32[22,64,128]{2,1,0:T(8,128)S(1)}, f32[22,64,128]{2,1,0:T(8,128)}, u32[]{:S(2)}, u32[]{:S(2)}) collective-permute-start(f32[22,64,128]{2,1,0:T(8,128)S(1)} %get-tuple-element.40), channel_id=1, source_target_pairs={{0,1},{1,0},{2,3},{3,2},{4,5},{5,4},{6,7},{7,6},{8,9},{9,8},{10,11... | collective-permute-start | bytes 2162696 | tf_op jit(solution)/shard_map/ppermute | solution.py:592
  143.1 1.0 constant_dynamic-slice_fusion
  144.2 0.9 collective-permute-done.13.taken
  145.1 2.3 %settle.1 = f32[16,9,64,128]{3,2,1,0:T(8,128)} custom-call(s32[1]{0:T(128)} %bitcast.core_ref, s32[16,9]{1,0:T(8,128)} %mask.1, s32[2,22,6]{2,1,0:T(8,128)} %constant.21.clone.table.edge_table, f32[22,64,128]{2,1,0:T(8,128)} %collective-permute-done.13.taken, f32[16,9,64,128]{3,2,1,0:T(8,128)} %get-tuple-element.41.full_in), custom_call_target="tpu_custom_call", output_to_operand_aliasing={{}: (4, {})} | custom-call | tf_op jit(solution)/shard_map/settle/pallas_call | solution.py:734
  (23 shorter events, 0.3 us)
Async XLA Ops:
  0.6 3.0 %collective-permute-start = (bf16[16,256,128]{2,1,0:T(8,128)(2,1)}, bf16[16,256,128]{2,1,0:T(8,128)(2,1)S(1)}, u32[]{:S(2)}, u32[]{:S(2)}) collective-permute-start(bf16[16,256,128]{2,1,0:T(8,128)(2,1)} %mine.1), channel_id=1, source_target_pairs={{0,1},{1,0},{2,3},{3,2},{4,5},{5,4},{6,7},{7,6},{8,9},{9,8},{10,11... | collective-permute-start | bytes 3145736 | tf_op jit(solution)/shard_map/ppermute | solution.py:592
  5.7 2.3 %copy-start = (bf16[16,256,128]{2,1,0:T(8,128)(2,1)S(1)}, bf16[16,256,128]{2,1,0:T(8,128)(2,1)}, u32[]{:S(2)}) copy-start(bf16[16,256,128]{2,1,0:T(8,128)(2,1)} %mine.1) | copy-start | bytes 3145732
  5.8 31.5 %collective-permute-start.3 = (bf16[1,528,128]{2,1,0:T(8,128)(2,1)S(1)}, bf16[1,528,128]{2,1,0:T(8,128)(2,1)S(1)}, u32[]{:S(2)}, u32[]{:S(2)}) collective-permute-start(bf16[1,528,128]{2,1,0:T(8,128)(2,1)S(1)} %get-tuple-element.43), channel_id=1, source_target_pairs={{1,10},{3,12},{5,14},{9,18},{10,1},{11,20},{12,3},{13,22},{14,5},{... | collective-permute-start | bytes 405512 | tf_op jit(solution)/shard_map/ppermute | solution.py:580
  6.7 2.8 %copy-start.3 = (s32[2,34,6]{2,1,0:T(8,128)S(1)}, s32[2,34,6]{2,1,0:T(8,128)}, u32[]{:S(2)}) copy-start(s32[2,34,6]{2,1,0:T(8,128)} %constant.20.clone.table) | copy-start | bytes 4900
  6.7 30.7 %collective-permute-start.4 = (bf16[1,528,128]{2,1,0:T(8,128)(2,1)S(1)}, bf16[1,528,128]{2,1,0:T(8,128)(2,1)S(1)}, u32[]{:S(2)}, u32[]{:S(2)}) collective-permute-start(bf16[1,528,128]{2,1,0:T(8,128)(2,1)S(1)} %get-tuple-element.42), channel_id=1, source_target_pairs={{3,8},{5,10},{7,12},{8,3},{10,5},{11,16},{12,7},{13,18},{15,20},{1... | collective-permute-start | bytes 405512 | tf_op jit(solution)/shard_map/ppermute | solution.py:580
  7.3 30.0 %collective-permute-start.1 = (bf16[4,528,128]{2,1,0:T(8,128)(2,1)S(1)}, bf16[4,528,128]{2,1,0:T(8,128)(2,1)S(1)}, u32[]{:S(2)}, u32[]{:S(2)}) collective-permute-start(bf16[4,528,128]{2,1,0:T(8,128)(2,1)S(1)} %fusion.2), channel_id=1, source_target_pairs={{1,2},{2,1},{3,4},{4,3},{5,6},{6,5},{9,10},{10,9},{11,12},{12,11},... | collective-permute-start | bytes 1622024 | tf_op jit(solution)/shard_map/ppermute | solution.py:580
  8.7 28.6 %collective-permute-start.2 = (bf16[4,528,128]{2,1,0:T(8,128)(2,1)S(1)}, bf16[4,528,128]{2,1,0:T(8,128)(2,1)S(1)}, u32[]{:S(2)}, u32[]{:S(2)}) collective-permute-start(bf16[4,528,128]{2,1,0:T(8,128)(2,1)S(1)} %slice_select_fusion), channel_id=1, source_target_pairs={{1,8},{3,10},{5,12},{7,14},{8,1},{9,16},{10,3},{11,18},{12,5},{13,... | collective-permute-start | bytes 1622024 | tf_op jit(solution)/shard_map/ppermute | solution.py:580
  9.4 41.2 %copy-start.2 = (s32[2,22,6]{2,1,0:T(8,128)S(1)}, s32[2,22,6]{2,1,0:T(8,128)}, u32[]{:S(2)}) copy-start(s32[2,22,6]{2,1,0:T(8,128)} %constant.21.clone.table.edge_table) | copy-start | bytes 3172
  37.4 13.2 %collective-permute-start.5 = (bf16[4,528,128]{2,1,0:T(8,128)(2,1)S(1)}, bf16[4,528,128]{2,1,0:T(8,128)(2,1)S(1)}, u32[]{:S(2)}, u32[]{:S(2)}) collective-permute-start(bf16[4,528,128]{2,1,0:T(8,128)(2,1)S(1)} %collective-permute-done.1.first_col), channel_id=1, source_target_pairs={{0,1},{1,0},{2,3},{3,2},{4,5},{5,4},{6,7},{7,6},{8,9},{9,8},{10,11... | collective-permute-start | bytes 1622024 | tf_op jit(solution)/shard_map/ppermute | solution.py:592
  50.6 1.6 %copy-start.1 = (f32[8,512,128]{2,1,0:T(8,128)S(1)}, f32[8,512,128]{2,1,0:T(8,128)}, u32[]{:S(2)}) copy-start(f32[8,512,128]{2,1,0:T(8,128)} %get-tuple-element.23.sketched) | copy-start | bytes 6291460
  87.8 6.6 %collective-permute-start.6 = (bf16[8,512,128]{2,1,0:T(8,128)(2,1)S(1)}, bf16[8,512,128]{2,1,0:T(8,128)(2,1)S(1)}, u32[]{:S(2)}, u32[]{:S(2)}) collective-permute-start(bf16[8,512,128]{2,1,0:T(8,128)(2,1)S(1)} %get-tuple-element.28.mine), channel_id=1, source_target_pairs={{0,1},{1,0},{2,3},{3,2},{4,5},{5,4},{6,7},{7,6},{8,9},{9,8},{10,11... | collective-permute-start | bytes 3145736 | tf_op jit(solution)/shard_map/ppermute | solution.py:592
  94.9 21.4 %collective-permute-start.7 = (bf16[4,512,128]{2,1,0:T(8,128)(2,1)S(1)}, bf16[4,512,128]{2,1,0:T(8,128)(2,1)S(1)}, u32[]{:S(2)}, u32[]{:S(2)}) collective-permute-start(bf16[4,512,128]{2,1,0:T(8,128)(2,1)S(1)} %fusion.3), channel_id=1, source_target_pairs={{1,2},{2,1},{3,4},{4,3},{5,6},{6,5},{9,10},{10,9},{11,12},{12,11},... | collective-permute-start | bytes 1572872 | tf_op jit(solution)/shard_map/ppermute | solution.py:580
  95.7 20.7 %collective-permute-start.8 = (bf16[4,512,128]{2,1,0:T(8,128)(2,1)S(1)}, bf16[4,512,128]{2,1,0:T(8,128)(2,1)S(1)}, u32[]{:S(2)}, u32[]{:S(2)}) collective-permute-start(bf16[4,512,128]{2,1,0:T(8,128)(2,1)S(1)} %slice_select_fusion.2), channel_id=1, source_target_pairs={{1,8},{3,10},{5,12},{7,14},{8,1},{9,16},{10,3},{11,18},{12,5},{13,... | collective-permute-start | bytes 1572872 | tf_op jit(solution)/shard_map/ppermute | solution.py:580
  96.4 19.9 %collective-permute-start.10 = (bf16[1,512,128]{2,1,0:T(8,128)(2,1)S(1)}, bf16[1,512,128]{2,1,0:T(8,128)(2,1)S(1)}, u32[]{:S(2)}, u32[]{:S(2)}) collective-permute-start(bf16[1,512,128]{2,1,0:T(8,128)(2,1)S(1)} %get-tuple-element.44), channel_id=1, source_target_pairs={{3,8},{5,10},{7,12},{8,3},{10,5},{11,16},{12,7},{13,18},{15,20},{1... | collective-permute-start | bytes 393224 | tf_op jit(solution)/shard_map/ppermute | solution.py:580
  97.0 19.3 %collective-permute-start.9 = (bf16[1,512,128]{2,1,0:T(8,128)(2,1)S(1)}, bf16[1,512,128]{2,1,0:T(8,128)(2,1)S(1)}, u32[]{:S(2)}, u32[]{:S(2)}) collective-permute-start(bf16[1,512,128]{2,1,0:T(8,128)(2,1)S(1)} %get-tuple-element.45), channel_id=1, source_target_pairs={{1,10},{3,12},{5,14},{9,18},{10,1},{11,20},{12,3},{13,22},{14,5},{... | collective-permute-start | bytes 393224 | tf_op jit(solution)/shard_map/ppermute | solution.py:580
  116.3 21.4 %collective-permute-start.12 = (f32[8,9,64,128]{3,2,1,0:T(8,128)S(1)}, f32[8,9,64,128]{3,2,1,0:T(8,128)S(1)}, u32[]{:S(2)}, u32[]{:S(2)}) collective-permute-start(f32[8,9,64,128]{3,2,1,0:T(8,128)S(1)} %get-tuple-element.38), channel_id=1, source_target_pairs={{0,1},{1,0},{2,3},{3,2},{4,5},{5,4},{6,7},{7,6},{8,9},{9,8},{10,11... | collective-permute-start | bytes 7077896 | tf_op jit(solution)/shard_map/ppermute | solution.py:592
  132.8 4.9 %collective-permute-start.11 = (bf16[4,512,128]{2,1,0:T(8,128)(2,1)S(1)}, bf16[4,512,128]{2,1,0:T(8,128)(2,1)S(1)}, u32[]{:S(2)}, u32[]{:S(2)}) collective-permute-start(bf16[4,512,128]{2,1,0:T(8,128)(2,1)S(1)} %collective-permute-done.7.first_col), channel_id=1, source_target_pairs={{0,1},{1,0},{2,3},{3,2},{4,5},{5,4},{6,7},{7,6},{8,9},{9,8},{10,11... | collective-permute-start | bytes 1572872 | tf_op jit(solution)/shard_map/ppermute | solution.py:592
  141.2 3.9 %collective-permute-start.13 = (f32[22,64,128]{2,1,0:T(8,128)S(1)}, f32[22,64,128]{2,1,0:T(8,128)}, u32[]{:S(2)}, u32[]{:S(2)}) collective-permute-start(f32[22,64,128]{2,1,0:T(8,128)S(1)} %get-tuple-element.40), channel_id=1, source_target_pairs={{0,1},{1,0},{2,3},{3,2},{4,5},{5,4},{6,7},{7,6},{8,9},{9,8},{10,11... | collective-permute-start | bytes 2162696 | tf_op jit(solution)/shard_map/ppermute | solution.py:592

commit v4 on v3

--- a/solution.py
+++ b/solution.py
@@ -44,16 +44,14 @@
             unit[i][j] = -total
     return inverse_pivots, unit
 
-def invert_factors(work, pivots, weights):
+def invert_factors(work, pivots, weights, exact):
     rank, batch, _ = work.shape
     lanes = lax.broadcasted_iota(jnp.int32, (batch, rank), 1)
-    square_rows = lax.broadcasted_iota(jnp.int32, (rank, rank), 0)
-    square_lanes = lax.broadcasted_iota(jnp.int32, (rank, rank), 1)
-
-    def block_step(block, carry):
-        first = block * BLOCK
-        back = lax.rem(rank - first, rank)
-        rows = [pltpu.roll(work[first + r], back, 1) for r in range(BLOCK)]
+    def turn_lanes(value, steps):
+        return pltpu.roll(value, steps % rank, 1) if steps % rank else value
+
+    for first in range(0, rank, BLOCK):
+        rows = [turn_lanes(work[first + r], -first) for r in range(BLOCK)]
         for base in range(0, BLOCK, PANEL):
             inverse_pivots, unit = factor_panel(rows, base)
             inside = (lanes >= base) & (lanes < base + PANEL)
@@ -77,42 +75,47 @@
             for k in range(PANEL):
                 at = base + k
                 kept = jnp.where((lanes > at) & (lanes < BLOCK), 0.0, held_rows[k])
-                turned = pltpu.roll(kept, first, 1)
+                turned = turn_lanes(kept, first)
                 pivots[at] = turned
-                weights[at] = pltpu.roll(scaled_rows[k], first, 1)
+                weights[at] = turn_lanes(scaled_rows[k], -BLOCK)
                 work[first + at] = jnp.where(lanes <= first + at, turned, 0.0) * lax.sqrt(inverse_pivots[k])
 
-        @pl.when(first + BLOCK < rank)
-        def _():
-            below = square_rows >= first + BLOCK
-            inside = (square_lanes >= first) & (square_lanes < first + BLOCK)
-            changes = []
-            for b in range(batch):
-                a1, a2, a3 = three_parts(weights[:, b, :])
-                b1, b2, b3 = three_parts(pivots[:, b, :])
-                left = jnp.concatenate([a1, a1, a2, a2, a1, a3], axis=0)
-                right = jnp.concatenate([b1, b2, b1, b2, b3, b1], axis=0)
-                changes.append(lax.dot_general(left, right, (((0,), (0,)), ((), ())), preferred_element_type=jnp.float32))
-            for b in range(batch):
-                now = work[:, b, :]
-                work[:, b, :] = jnp.where(below, jnp.where(inside, 0.0, now) - changes[b], now)
-
-        return carry
-
-    lax.fori_loop(0, rank // BLOCK, block_step, 0)
+        start = first + BLOCK
+        left_over = rank - start
+        if left_over == 0:
+            continue
+        inside = lax.broadcasted_iota(jnp.int32, (left_over, rank), 1)
+        inside = (inside >= first) & (inside < start)
+        for b in range(batch):
+            a1, a2, a3 = three_parts(weights[:, b, :])
+            b1, b2, b3 = three_parts(pivots[:, b, :])
+            left = [a1, a1, a2] + ([a2, a1, a3] if exact else [])
+            right = [b1, b2, b1] + ([b2, b3, b1] if exact else [])
+            left, right = jnp.concatenate(left, axis=0)[:, :left_over], jnp.concatenate(right, axis=0)
+            change = lax.dot_general(left, right, (((0,), (0,)), ((), ())), preferred_element_type=jnp.float32)
+            work[start:, b, :] = jnp.where(inside, 0.0, work[start:, b, :]) - change
+
+
+def two_part_product(left, right, dims):
+    a1, a2, _ = three_parts(left)
+    b1, b2, _ = three_parts(right)
+    product = functools.partial(lax.dot_general, dimension_numbers=(dims, ((), ())), preferred_element_type=jnp.float32)
+    return product(a1, b1) + (product(a1, b2) + product(a2, b1))
+
+
+def whole_product(left, right, dims):
+    return lax.dot_general(left, right, (dims, ((), ())), precision=lax.Precision.HIGHEST, preferred_element_type=jnp.float32)
+
 
 def orthonormalize(y_ref, out_ref, work, pivots, weights):
     batch, points, rank = y_ref.shape
-    for turn in range(2):
-        grams = []
+    for turn, product in enumerate((whole_product, two_part_product)):
         for b in range(batch):
             data = y_ref[b]
-            grams.append(lax.dot_general(data, data, (((0,), (0,)), ((), ())), precision=lax.Precision.HIGHEST, preferred_element_type=jnp.float32) * (1.0 / points))
+            work[:, b, :] = product(data, data, ((0,), (0,))) * (1.0 / points)
+        invert_factors(work, pivots, weights, turn == 0)
         for b in range(batch):
-            work[:, b, :] = grams[b]
-        invert_factors(work, pivots, weights)
-        for b in range(batch):
-            data = lax.dot_general(y_ref[b], work[:, b, :], (((1,), (1,)), ((), ())), precision=lax.Precision.HIGHEST, preferred_element_type=jnp.float32)
+            data = product(y_ref[b], work[:, b, :], ((1,), (1,)))
             if turn == 0:
                 y_ref[b] = data
             else:
@@ -177,16 +180,27 @@
 
 def fill_coords(coords, place, box_coords, stretch):
     moved = (box_coords - 0.5) * stretch
+    coords[place] = jnp.zeros(coords.shape[1:], jnp.float32)
     coords[place, 0:2] = moved[0:2]
     coords[place, 2:3] = moved[2:3] * lift_scale
 
 
 def fill_rows(rows, box_coords, own, soften):
-    box_points = box_coords.shape[1]
-    turned = jnp.transpose(box_coords)
+    first = box_coords.astype(jnp.bfloat16).astype(jnp.float32)
+    rest = box_coords - first
+    second = rest.astype(jnp.bfloat16).astype(jnp.float32)
+    parts = jnp.concatenate([first, second, rest - second], axis=0).astype(jnp.bfloat16)
+    shape = (parts.shape[0], 3 * LANES)
+    take = lax.rem(lax.broadcasted_iota(jnp.int32, shape, 0), 8) == lax.broadcasted_iota(jnp.int32, shape, 1) // LANES
+    spread = lax.dot_general(
+        parts,
+        jnp.where(take, 1.0, 0.0).astype(jnp.bfloat16),
+        (((0,), (0,)), ((), ())),
+        preferred_element_type=jnp.float32,
+    )
     total = soften
     for axis in range(3):
-        column = jnp.broadcast_to(turned[:, axis : axis + 1], (box_points, LANES))
+        column = spread[:, axis * LANES : (axis + 1) * LANES]
         rows[own, axis] = column + column
         total = total + column * column
     rows[own, 3] = total
@@ -224,61 +238,12 @@
     return lax.fori_loop(0, count, check, 0)
 
 
-def run_blocks(active, base, total, make, use, store, pair, sems):
-    def entry(turn):
-        return active[base + jnp.minimum(turn, total - 1)]
-
-    def send(side, slot, turn):
-        return pltpu.make_async_copy(pair[side].at[slot], store.at[entry(turn)], sems.at[side, slot])
-
-    @pl.when(total > 0)
-    def _():
-        make(entry(0), pair[0].at[0])
-        send(0, 0, 0).start()
-
-    def step(half_turn, carry):
-        even = 2 * half_turn
-        odd, after = even + 1, even + 2
-        slot = lax.rem(half_turn, 2)
-
-        @pl.when(half_turn > 1)
-        def _():
-            send(1, slot, 0).wait()
-
-        make(entry(odd), pair[1].at[slot])
-        use(entry(even), pair[0].at[slot], 1.0)
-
-        @pl.when(odd < total)
-        def _():
-            send(1, slot, odd).start()
-
-        @pl.when(half_turn > 0)
-        def _():
-            send(0, 1 - slot, 0).wait()
-
-        make(entry(after), pair[0].at[1 - slot])
-        use(entry(odd), pair[1].at[slot], jnp.where(odd < total, 1.0, 0.0))
-
-        @pl.when(after < total)
-        def _():
-            send(0, 1 - slot, after).start()
-
+def run_blocks(active, base, total, step_of):
+    def step(turn, carry):
+        step_of(active[base + turn])
         return carry
 
-    turns = (total + 1) // 2
-    lax.fori_loop(0, turns, step, 0)
-
-    @pl.when(turns > 0)
-    def _():
-        send(0, lax.rem(turns - 1, 2), 0).wait()
-
-    @pl.when(turns > 1)
-    def _():
-        send(1, lax.rem(turns, 2), 0).wait()
-
-    @pl.when((turns > 0) & (2 * turns == total))
-    def _():
-        send(1, lax.rem(turns - 1, 2), 0).wait()
+    lax.fori_loop(0, total, step, 0)
 
 
 def place(table, core, index):
@@ -286,7 +251,7 @@
 
 
 def chip_sketch_kernel(counts, core_ref, mask, table, points, mine, theirs, y_ref, store,
-                       omega, omega_t, coords, rows, turned_y, buffer_a, buffer_b, active, sems, load_sems):
+                       omega, omega_t, coords, rows, turned_y, blocks, active, load_sems, store_sems):
     core = core_ref[0]
     chip_boxes, _, box_points = points.shape
     own_boxes, _, skel_rank = y_ref.shape
@@ -311,25 +276,28 @@
         y_ref[own] = values.astype(jnp.float32)
         turned_y[own] = jnp.zeros((skel_rank, box_points), jnp.float32)
 
-    def make(index, target):
-        own, other, offset_y, offset_x, _, _ = place(table, core, index)
+    def block(both, index):
+        own, other, offset_y, offset_x, _, mate = place(table, core, index)
         shift_y, shift_x = offset_y.astype(jnp.float32) * stretch, offset_x.astype(jnp.float32) * stretch
-        make_entries(target, rows, own, coords, other, shift_y, shift_x)
-
-    def use(both, index, buffer, weight):
-        own, other, _, _, _, mate = place(table, core, index)
-        values = buffer[...]
-        y_ref[own] += jnp.dot(values, omega[other], preferred_element_type=jnp.float32) * weight
+        make_entries(blocks.at[index], rows, own, coords, other, shift_y, shift_x)
+        send(index).start()
+        values = blocks[index]
+        y_ref[own] += jnp.dot(values, omega[other], preferred_element_type=jnp.float32)
         if both:
-            turned_y[mate] += jnp.dot(omega_t[own], values, preferred_element_type=jnp.float32) * weight
-
-    first = 0
+            turned_y[mate] += jnp.dot(omega_t[own], values, preferred_element_type=jnp.float32)
+
+    def send(index):
+        return pltpu.make_async_copy(blocks.at[index], store.at[index], store_sems.at[index])
+
+    first, totals = 0, []
     for both, count in enumerate(counts):
-        total = list_active(table, core, first, count, mask, active, first)
-        run_blocks(active, first, total, make, functools.partial(use, both), store, (buffer_a, buffer_b), sems)
+        totals.append(list_active(table, core, first, count, mask, active, first))
+        run_blocks(active, first, totals[both], functools.partial(block, both))
         first += count
     for own in range(own_boxes):
         y_ref[own] += jnp.transpose(turned_y[own])
+    for first, total in zip((0, counts[0]), totals):
+        run_blocks(active, first, total, lambda index: send(index).wait())
 
 
 def edge_coords(coords, extended, box, box_points, stretch):
@@ -354,7 +322,7 @@
 
 
 def edge_sketch_kernel(core_ref, mask, table, points, sketched, first_col, second_col, row, corner_a, corner_b,
-                       basis, store, extended, coords, rows, y_ref, buffer_a, buffer_b, active, sems, load_sems,
+                       basis, store, extended, coords, own_coords, rows, y_ref, blocks, active, filled, load_sems, store_sems,
                        work, pivots, weights):
     core = core_ref[0]
     own_boxes, box_points, skel_rank = y_ref.shape
@@ -365,73 +333,81 @@
     stretch = math.sqrt(box_points) * 4.0
     soften = (0.25 / box_points) * stretch * stretch
     for own in range(own_boxes):
-        fill_coords(coords, own, points[core * own_boxes + own].astype(jnp.float32), stretch)
-        fill_rows(rows, coords[own], own, soften)
+        fill_coords(own_coords, own, points[core * own_boxes + own].astype(jnp.float32), stretch)
+    filled[0] = -1
     for load in loads:
         load.wait()
     for box in range(extended.shape[0]):
         edge_coords(coords, extended, box, box_points, stretch)
 
-    def make(index, target):
+    def block(index):
         own, other, offset_y, offset_x, _, _ = place(table, core, index)
         shift_y, shift_x = offset_y.astype(jnp.float32) * stretch, offset_x.astype(jnp.float32) * stretch
-        make_entries(target, rows, own, coords, other, shift_y, shift_x)
-
-    def use(index, buffer, weight):
-        own, other, _, _, _, _ = place(table, core, index)
+
+        @pl.when(own != filled[0])
+        def _():
+            fill_rows(rows, own_coords[own], 0, soften)
+            filled[0] = own
+
+        make_entries(blocks.at[index], rows, 0, coords, other, shift_y, shift_x)
+        send(index).start()
         y_ref[own] += jnp.dot(
-            buffer[...], extended[other, 0:box_points, :], preferred_element_type=jnp.float32
-        ) * weight
+            blocks[index], extended[other, 0:box_points, :], preferred_element_type=jnp.float32
+        )
+
+    def send(index):
+        return pltpu.make_async_copy(blocks.at[index], store.at[index], store_sems.at[index])
 
     total = list_active(table, core, 0, table.shape[1], mask, active, 0)
-    run_blocks(active, 0, total, make, use, store, (buffer_a, buffer_b), sems)
+    run_blocks(active, 0, total, block)
     orthonormalize(y_ref, basis, work, pivots, weights)
-
-
-def run_stored(active, base, total, buffers, store, sems, depth, project, use, pair):
+    run_blocks(active, 0, total, lambda index: send(index).wait())
+
+
+def run_stored(active, base, total, fetch, project, use, pair):
     def entry(turn):
         return active[base + jnp.minimum(turn, total - 1)]
 
-    def fetch(turn):
-        slot = lax.rem(turn, depth)
-        return pltpu.make_async_copy(store.at[active[base + turn]], buffers.at[slot], sems.at[slot])
-
-    def arrive(turn, side):
-        @pl.when(turn < total)
-        def _():
-            fetch(turn).wait()
-
-        project(entry(turn), lax.rem(jnp.minimum(turn, total - 1), depth), pair[side])
-
-    for turn in range(depth - 1):
-
-        @pl.when(turn < total)
-        def _():
-            fetch(turn).start()
-
     @pl.when(total > 0)
     def _():
-        arrive(0, 0)
+        fetch(entry(0)).wait()
+        project(entry(0), pair[0])
 
     def step(half_turn, carry):
         even = 2 * half_turn
         for ahead in (0, 1):
-
-            @pl.when(even + ahead + depth - 1 < total)
+            following = even + ahead + 1
+
+            @pl.when(following < total)
             def _():
-                fetch(even + ahead + depth - 1).start()
-
-            arrive(even + ahead + 1, 1 - ahead)
+                fetch(entry(following)).wait()
+
+            project(entry(following), pair[1 - ahead])
             use(entry(even + ahead), pair[ahead])
         return carry
 
     lax.fori_loop(0, (total + 1) // 2, step, 0)
 
 
-def chip_couple_kernel(counts, depth, core_ref, mask, table, edge_table, mine, theirs, store, edge_store,
-                       full, give, projected, basis, basis_t, buffers, active, found, ray_a, ray_b, sems, out_sems):
+def chip_couple_kernel(counts, core_ref, mask, table, edge_table, mine, theirs, store, edge_store,
+                       full, give, projected, basis, basis_t, chip_held, blocks, active, edge_active, found, ray_a, ray_b, out_sems,
+                       chip_sems, fetch_sems):
     core = core_ref[0]
     own_boxes, box_points, skel_rank = mine.shape
+
+    def fetch(index):
+        return pltpu.make_async_copy(edge_store.at[index], blocks.at[index], fetch_sems.at[index])
+
+    def chip_fetch(index):
+        return pltpu.make_async_copy(store.at[index], chip_held.at[index], chip_sems.at[index])
+
+    first, totals = 0, []
+    for count in counts:
+        totals.append(list_active(table, core, first, count, mask, active, first))
+        run_blocks(active, first, totals[-1], lambda index: chip_fetch(index).start())
+        first += count
+    edge_total = list_active(edge_table, core, 0, edge_table.shape[1], mask, edge_active, 0)
+    run_blocks(edge_active, 0, edge_total, lambda index: fetch(index).start())
     half = give.shape[2]
     basis[pl.ds(core * own_boxes, own_boxes)] = mine[...]
     basis[pl.ds((1 - core) * own_boxes, own_boxes)] = theirs[...]
@@ -449,10 +425,10 @@
 
     lax.fori_loop(0, own_boxes * 9, clear, 0)
 
-    def project(index, slot, target):
+    def project(index, target):
         own, stencil = table[core, index, 0], table[core, index, 4]
         centre = jnp.where(stencil == 4, 1.0, 0.0)
-        values = jnp.dot(basis_t[own], buffers[slot], preferred_element_type=jnp.float32)
+        values = jnp.dot(basis_t[own], chip_held[index], preferred_element_type=jnp.float32)
         target[...] = (values + basis_t[own].astype(jnp.float32) * centre).astype(jnp.bfloat16)
 
     def use(both, index, rays):
@@ -464,8 +440,7 @@
 
     first = 0
     for both, count in enumerate(counts):
-        total = list_active(table, core, first, count, mask, active, first)
-        run_stored(active, first, total, buffers, store, sems, depth, project, functools.partial(use, both), (ray_a, ray_b))
+        run_stored(active, first, totals[both], chip_fetch, project, functools.partial(use, both), (ray_a, ray_b))
         first += count
 
     copies = []
@@ -480,79 +455,79 @@
     for copy in copies:
         copy.start()
 
-    def edge_project(index, slot, target):
-        own = edge_table[core, index, 0]
-        projected[index] = jnp.dot(
-            basis_t[own], buffers[slot], preferred_element_type=jnp.float32
-        ).astype(jnp.bfloat16)
-
-    total = list_active(edge_table, core, 0, edge_table.shape[1], mask, active, 0)
-    run_stored(active, 0, total, buffers, edge_store, sems, depth, edge_project, lambda index, rays: None, (ray_a, ray_b))
+    def edge_project(half_turn, carry):
+        indices = []
+        for turn in (2 * half_turn, 2 * half_turn + 1):
+            indices.append(edge_active[jnp.minimum(turn, edge_total - 1)])
+
+            @pl.when(turn < edge_total)
+            def _():
+                fetch(edge_active[turn]).wait()
+
+        rays = [
+            jnp.dot(basis_t[edge_table[core, index, 0]], blocks[index], preferred_element_type=jnp.float32)
+            for index in indices
+        ]
+        for index, values in zip(indices, rays):
+            projected[index] = values.astype(jnp.bfloat16)
+        return carry
+
+    lax.fori_loop(0, (edge_total + 1) // 2, edge_project, 0)
     for copy in copies:
         copy.wait()
 
 
 def edge_couple_kernel(core_ref, mask, edge_table, projected, first_col, second_col, row, corner_a, corner_b,
-                       taken, full_in, full, give, extended, results, active, load_sems, sems, move_sems):
+                       full_in, full, give, extended, results, load_sems, sems):
     core = core_ref[0]
     box_points = projected.shape[2]
-    own_boxes, _, half, _ = taken.shape
+    own_boxes, half = full.shape[0] // 2, full.shape[2]
     loads = load_edges(core, (first_col, second_col, row, corner_a, corner_b), extended, load_sems)
+    for copy in loads:
+        copy.start()
+    for load in loads:
+        load.wait()
+    copies = []
+    for index in range(edge_table.shape[1]):
+        own, other, stencil = (edge_table[core, index, field] for field in (0, 1, 4))
+        values = jnp.dot(projected[index], extended[other], preferred_element_type=jnp.float32) * (1.0 / box_points)
+        results[index] = jnp.where(mask[own, stencil] != 0, values, 0.0)
+        copies.append(pltpu.make_async_copy(
+            results.at[index, pl.ds(pl.multiple_of(core * half, half), half), :],
+            full.at[core * own_boxes + own, stencil],
+            sems.at[index],
+        ))
+    for index, copy in enumerate(copies):
+        copy.start()
+        give[index] = results[index, pl.ds(pl.multiple_of((1 - core) * half, half), half), :]
+    for copy in copies:
+        copy.wait()
+
+
+def settle_kernel(core_ref, edge_table, bulk, taken, full_in, full, bulk_sems, sems):
+    other = 1 - core_ref[0]
+    own_boxes = full.shape[0] // 2
     moves = [
-        pltpu.make_async_copy(taken.at[own], full.at[(1 - core) * own_boxes + own], move_sems.at[own])
+        pltpu.make_async_copy(bulk.at[own], full.at[other * own_boxes + own], bulk_sems.at[own])
         for own in range(own_boxes)
     ]
-    for copy in loads + moves:
-        copy.start()
-    total = list_active(edge_table, core, 0, edge_table.shape[1], mask, active, 0)
-    for load in loads:
-        load.wait()
-
-    def result_copy(turn):
-        index = active[turn]
-        own, stencil = edge_table[core, index, 0], edge_table[core, index, 4]
-        mine = results.at[turn, pl.ds(pl.multiple_of(core * half, half), half), :]
-        return pltpu.make_async_copy(mine, full.at[core * own_boxes + own, stencil], sems.at[turn])
-
-    def step(turn, carry):
-        index = active[turn]
-        results[turn] = jnp.dot(
-            projected[index], extended[edge_table[core, index, 1]], preferred_element_type=jnp.float32
-        ) * (1.0 / box_points)
-        give[index] = results[turn, pl.ds(pl.multiple_of((1 - core) * half, half), half), :]
-        result_copy(turn).start()
-        return carry
-
-    def finish(turn, carry):
-        result_copy(turn).wait()
-        return carry
-
-    lax.fori_loop(0, total, step, 0)
-    lax.fori_loop(0, total, finish, 0)
+    for move in moves:
+        move.start()
     for move in moves:
         move.wait()
 
-
-def settle_kernel(core_ref, mask, edge_table, taken, full_in, full, sems):
-    other = 1 - core_ref[0]
-    own_boxes = full.shape[0] // 2
-
-    def each(act):
-        def step(index, carry):
-            own, stencil = edge_table[other, index, 0], edge_table[other, index, 4]
-
-            @pl.when(mask[other * own_boxes + own, stencil] != 0)
-            def _():
-                act(pltpu.make_async_copy(
-                    taken.at[index], full.at[other * own_boxes + own, stencil], sems.at[index]
-                ))
-
-            return carry
-
-        lax.fori_loop(0, edge_table.shape[1], step, 0)
-
-    each(lambda copy: copy.start())
-    each(lambda copy: copy.wait())
+    copies = [
+        pltpu.make_async_copy(
+            taken.at[index],
+            full.at[other * own_boxes + edge_table[other, index, 0], edge_table[other, index, 4]],
+            sems.at[index],
+        )
+        for index in range(edge_table.shape[1])
+    ]
+    for copy in copies:
+        copy.start()
+    for copy in copies:
+        copy.wait()
 
 
 SMEM = pl.BlockSpec(memory_space=pltpu.SMEM)
@@ -635,11 +610,10 @@
             pltpu.VMEM((chip_boxes, 8, box_points), f32),
             pltpu.VMEM((own_boxes, 4, box_points, LANES), f32),
             pltpu.VMEM((own_boxes, skel_rank, box_points), f32),
-            pltpu.VMEM((2, box_points, box_points), bf16),
-            pltpu.VMEM((2, box_points, box_points), bf16),
+            pltpu.VMEM((chip_blocks, box_points, box_points), bf16),
             pltpu.SMEM((chip_blocks,), jnp.int32),
-            pltpu.SemaphoreType.DMA((2, 2)),
             pltpu.SemaphoreType.DMA((2,)),
+            pltpu.SemaphoreType.DMA((chip_blocks,)),
         ],
         compiler_params=params(50),
         cost_estimate=pl.CostEstimate(flops=8 * 10**9, bytes_accessed=24 * 10**6, transcendentals=0),
@@ -654,23 +628,24 @@
             jax.ShapeDtypeStruct((own_boxes, box_points, skel_rank), bf16),
             jax.ShapeDtypeStruct((edge_blocks, box_points, box_points), bf16),
         ),
-        in_specs=[SMEM, SMEM, SMEM, VMEM] + [ANY] * 6,
-        out_specs=(VMEM, ANY),
+        in_specs=[SMEM, SMEM, SMEM, VMEM, ANY] + [ANY] * 5,
+        out_specs=(VMEM, HBM),
         scratch_shapes=[
             pltpu.VMEM((edge_boxes, box_points + 16, skel_rank), bf16),
             pltpu.VMEM((edge_boxes, 8, box_points), f32),
-            pltpu.VMEM((own_boxes, 4, box_points, LANES), f32),
+            pltpu.VMEM((own_boxes, 8, box_points), f32),
+            pltpu.VMEM((1, 4, box_points, LANES), f32),
             pltpu.VMEM((own_boxes, box_points, skel_rank), f32),
-            pltpu.VMEM((2, box_points, box_points), bf16),
-            pltpu.VMEM((2, box_points, box_points), bf16),
+            pltpu.VMEM((edge_blocks, box_points, box_points), bf16),
             pltpu.SMEM((edge_blocks,), jnp.int32),
-            pltpu.SemaphoreType.DMA((2, 2)),
+            pltpu.SMEM((1,), jnp.int32),
             pltpu.SemaphoreType.DMA((6,)),
+            pltpu.SemaphoreType.DMA((edge_blocks,)),
             pltpu.VMEM((skel_rank, own_boxes, skel_rank), f32),
             pltpu.VMEM((BLOCK, own_boxes, skel_rank), f32),
             pltpu.VMEM((BLOCK, own_boxes, skel_rank), f32),
         ],
-        compiler_params=params(24),
+        compiler_params=params(50),
         name="edge_sketch",
     )(core_arg, own_mask, edge_table, points, sketched, col, second_col, row, corner_a, corner_b)
 
@@ -681,29 +656,31 @@
         jnp.concatenate([other_basis, basis], axis=0),
     ).reshape(tile_side, tile_side, box_points, skel_rank)
     col, row, corner_a, corner_b = exchange(whole, core, grid_side)
-    depth = 8
     coupling_shape = jax.ShapeDtypeStruct((chip_boxes, 9, half_rank, skel_rank), f32)
     coupling, give, projected = pl.pallas_call(
-        functools.partial(chip_couple_kernel, counts, depth),
+        functools.partial(chip_couple_kernel, counts),
         out_shape=(
             coupling_shape,
             jax.ShapeDtypeStruct((own_boxes, 9, half_rank, skel_rank), f32),
             jax.ShapeDtypeStruct((edge_blocks, skel_rank, box_points), bf16),
         ),
-        in_specs=[SMEM] * 4 + [VMEM, VMEM, HBM, ANY],
+        in_specs=[SMEM] * 4 + [VMEM] * 2 + [HBM] * 2,
         out_specs=(ANY, ANY, VMEM),
         scratch_shapes=[
             pltpu.VMEM((chip_boxes, box_points, skel_rank), bf16),
             pltpu.VMEM((own_boxes, skel_rank, box_points), bf16),
-            pltpu.VMEM((depth, box_points, box_points), bf16),
-            pltpu.SMEM((max(chip_blocks, edge_blocks),), jnp.int32),
+            pltpu.VMEM((chip_blocks, box_points, box_points), bf16),
+            pltpu.VMEM((edge_blocks, box_points, box_points), bf16),
+            pltpu.SMEM((chip_blocks,), jnp.int32),
+            pltpu.SMEM((edge_blocks,), jnp.int32),
             pltpu.VMEM((own_boxes, 9, skel_rank, skel_rank), f32),
             pltpu.VMEM((skel_rank, box_points), bf16),
             pltpu.VMEM((skel_rank, box_points), bf16),
-            pltpu.SemaphoreType.DMA((depth,)),
             pltpu.SemaphoreType.DMA((2 * own_boxes,)),
+            pltpu.SemaphoreType.DMA((chip_blocks,)),
+            pltpu.SemaphoreType.DMA((edge_blocks,)),
         ],
-        compiler_params=params(20),
+        compiler_params=params(46),
         cost_estimate=pl.CostEstimate(flops=8 * 10**9, bytes_accessed=32 * 10**6, transcendentals=0),
         name="chip_couple",
     )(core_arg, own_mask, chip_table, edge_table, basis, other_basis, store, edge_store)
@@ -711,35 +688,34 @@
     col, row, corner_a, corner_b, projected, give = lax.optimization_barrier(
         (col, row, corner_a, corner_b, projected, give)
     )
-    second_col = swap(col)
-    taken = swap(give)
+    second_col, give = lax.optimization_barrier((swap(col), give))
+    bulk = swap(give)
     coupling, give = pl.pallas_call(
         edge_couple_kernel,
         out_shape=(coupling_shape, jax.ShapeDtypeStruct((edge_blocks, half_rank, skel_rank), f32)),
-        in_specs=[SMEM] * 3 + [VMEM] + [ANY] * 7,
+        in_specs=[SMEM] * 3 + [VMEM] + [ANY] * 6,
         out_specs=(ANY, VMEM),
         scratch_shapes=[
             pltpu.VMEM((edge_boxes, box_points, skel_rank), bf16),
             pltpu.VMEM((edge_blocks, skel_rank, skel_rank), f32),
-            pltpu.SMEM((edge_blocks,), jnp.int32),
             pltpu.SemaphoreType.DMA((5,)),
             pltpu.SemaphoreType.DMA((edge_blocks,)),
-            pltpu.SemaphoreType.DMA((own_boxes,)),
         ],
-        input_output_aliases={10: 0},
+        input_output_aliases={9: 0},
         compiler_params=params(20),
         name="edge_couple",
-    )(core_arg, own_mask, edge_table, projected, col, second_col, row, corner_a, corner_b, taken, coupling)
+    )(core_arg, own_mask, edge_table, projected, col, second_col, row, corner_a, corner_b, coupling)
     taken = swap(give)
     coupling = pl.pallas_call(
         settle_kernel,
         out_shape=coupling_shape,
-        in_specs=[SMEM] * 3 + [VMEM, ANY],
+        in_specs=[SMEM] * 2 + [VMEM, VMEM, ANY],
         out_specs=ANY,
-        scratch_shapes=[pltpu.SemaphoreType.DMA((edge_blocks,))],
+        scratch_shapes=[pltpu.SemaphoreType.DMA((own_boxes,)), pltpu.SemaphoreType.DMA((edge_blocks,))],
         input_output_aliases={4: 0},
+        compiler_params=params(20),
         name="settle",
-    )(core_arg, near_mask, edge_table, taken, coupling)
+    )(core_arg, edge_table, bulk, taken, coupling)
     basis_out = lax.dynamic_slice_in_dim(
         whole.reshape(chip_boxes, box_points, skel_rank), core * half_points, half_points, 1
     )

time: 150 us -> 132 us (0.88); the launches traced: 148 us -> 132 us
  Pallas kernels: 87.9 us -> 77 us
  waiting for transfers between devices: 10.5 us -> 6.96 us
    pallas_call x1, Pallas kernels: 35.6 us -> 29.7 us  [body(): pl.pallas_call(edge_sketch_kernel, out_shape=(jax.ShapeDtypeStruct((own_b...]
    pallas_call x1, Pallas kernels: 27.9 us -> 22.3 us  [body(): pl.pallas_call(functools.partial(chip_sketch_kernel, counts), out_shape=(...]
    ppermute x6, waiting for transfers between devices: 10.5 us -> 6.94 us  [swap(): return lax.ppermute(value, 'col', [(0, 1), (1, 0)])]
    unnamed x9 -> x11, local copies, waits for them, and re-layouts: 2.45 us -> 0.88 us
  transfers between devices with their start and end apart: 14 -> 14, of which waited for: 5 -> 4; matrix products, arithmetic and copies ran while one was open for 2% -> 3% of each run, Pallas kernels for 31% -> 33%
where the time goes in v4:
time: 132 us
  Pallas kernels  77 us (58%)
  starting transfers between devices  40.5 us (31%)
  waiting for transfers between devices  6.96 us (5%)
  other arithmetic  3.45 us (3%)
  local copies, waits for them, and re-layouts  3.25 us (2%)
    ppermute x6, starting transfers between devices, swap(): return lax.ppermute(value, 'col', [(0, 1), (1, 0)])  35 us
    pallas_call x1, Pallas kernels, body(): pl.pallas_call(edge_sketch_kernel, out_shape=(jax.ShapeDtypeStruct((own_b...  29.7 us
    pallas_call x1, Pallas kernels, body(): pl.pallas_call(functools.partial(chip_sketch_kernel, counts), out_shape=(...  22.3 us
    pallas_call x1, Pallas kernels, body(): pl.pallas_call(functools.partial(chip_couple_kernel, counts), out_shape=(...  17.3 us
    ppermute x6, waiting for transfers between devices, swap(): return lax.ppermute(value, 'col', [(0, 1), (1, 0)])  6.94 us
    ppermute x8, starting transfers between devices, send(): return lax.ppermute(piece, ('box', 'col'), pairs)  5.59 us
    pallas_call x1, Pallas kernels, body(): pl.pallas_call(edge_couple_kernel, out_shape=(coupling_shape, jax.ShapeDt...  4.29 us
    pallas_call x1, Pallas kernels, body(): pl.pallas_call(settle_kernel, out_shape=coupling_shape, in_specs=[SMEM] *...  3.43 us
  transfers between devices with their start and end apart: 14, of which 4 were waited for; matrix products, arithmetic and copies ran while one was open for 3% of the time, Pallas kernels for 33%

profile of v4, /device:TPU:0, one launch (start us, length us, event | category | flops | bytes accessed | tf_op | source)
XLA Modules:
  0.0 132.4 jit_solution(9272452756726491444)
XLA Ops:
  0.6 0.5 collective-permute-start
  1.2 0.8 copy.14.points
  2.1 1.5 %collective-permute-done.theirs = bf16[16,256,128]{2,1,0:T(8,128)(2,1)S(1)} collective-permute-done((bf16[16,256,128]{2,1,0:T(8,128)(2,1)}, bf16[16,256,128]{2,1,0:T(8,128)(2,1)S(1)}, u32[]{:S(2)}, u32[]{:S(2)}) %collective-permute-start) | collective-permute-done | bytes 1048608 | tf_op jit(solution)/shard_map/ppermute | solution.py:567
  3.7 2.2 %fusion.1 = bf16[4,4,528,128]{3,2,1,0:T(8,128)(2,1)S(1)} fusion(bf16[4,4,16,128]{3,2,1,0:T(8,128)(2,1)S(1)} %bitcast.21, bf16[4,4,256,128]{3,2,1,0:T(8,128)(2,1)S(1)} %bitcast.18, bf16[4,4,256,128]{3,2,1,0:T(8,128)(2,1)} %bitcast.17, pred[]{:T(512)S(6)} %eq.2), kind=kLoop, calls=%fused_computation.5 | loop fusion | flops 12976128 | bytes 4325377 | tf_op jit(solution)/shard_map/jit(_where)/select_n | solution.py:591
  6.0 0.1 fusion.2
  6.0 0.8 collective-permute-start.3
  6.8 0.7 collective-permute-start.4
  7.5 0.7 collective-permute-start.1
  8.2 0.6 fusion
  8.8 0.1 slice_select_fusion
  8.9 0.7 collective-permute-start.2
  9.6 22.3 %chip_sketch.1 = (f32[8,512,128]{2,1,0:T(8,128)}, bf16[34,512,512]{2,1,0:T(8,128)(2,1)}) custom-call(s32[1]{0:T(128)} %bitcast.core_ref, s32[8,9]{1,0:T(8,128)S(1)} %constant_dynamic-slice_fusion.1.mask, s32[2,34,6]{2,1,0:T(8,128)S(1)} %copy-done.3, bf16[16,3,512]{2,1,0:T(4,128)(2,1)S(1)} %copy.14.points, bf16[16,256,128]{2,1,0:T(8,128)(2,1)S(1)} %copy-done.1, ...), custom_call_target="tpu_custom_call" | custom-call | flops 8000000000 | bytes 24000000 | tf_op jit(solution)/shard_map/chip_sketch/pallas_call | solution.py:599
  32.0 10.4 %collective-permute-start.5 = (bf16[4,528,128]{2,1,0:T(8,128)(2,1)S(1)}, bf16[4,528,128]{2,1,0:T(8,128)(2,1)S(1)}, u32[]{:S(2)}, u32[]{:S(2)}) collective-permute-start(bf16[4,528,128]{2,1,0:T(8,128)(2,1)S(1)} %collective-permute-done.1.first_col), channel_id=1, source_target_pairs={{0,1},{1,0},{2,3},{3,2},{4,5},{5,4},{6,7},{7,6},{8,9},{9,8},{10,11... | collective-permute-start | bytes 1622024 | tf_op jit(solution)/shard_map/ppermute | solution.py:567
  42.4 1.6 %collective-permute-done.5.second_col = bf16[4,528,128]{2,1,0:T(8,128)(2,1)S(1)} collective-permute-done((bf16[4,528,128]{2,1,0:T(8,128)(2,1)S(1)}, bf16[4,528,128]{2,1,0:T(8,128)(2,1)S(1)}, u32[]{:S(2)}, u32[]{:S(2)}) %collective-permute-start.5) | collective-permute-done | bytes 540704 | tf_op jit(solution)/shard_map/ppermute | solution.py:567
  44.0 29.7 %edge_sketch.1 = (bf16[8,512,128]{2,1,0:T(8,128)(2,1)S(1)}, bf16[22,512,512]{2,1,0:T(8,128)(2,1)}) custom-call(s32[1]{0:T(128)} %bitcast.core_ref, s32[8,9]{1,0:T(8,128)S(1)} %constant_dynamic-slice_fusion.1.mask, s32[2,22,6]{2,1,0:T(8,128)S(1)} %copy-done.2, bf16[16,3,512]{2,1,0:T(4,128)(2,1)S(1)} %copy.14.points, ...), custom_call_target="tpu_custom_call" | custom-call | tf_op jit(solution)/shard_map/edge_sketch/pallas_call | solution.py:625
  73.7 5.5 %collective-permute-start.6 = (bf16[8,512,128]{2,1,0:T(8,128)(2,1)S(1)}, bf16[8,512,128]{2,1,0:T(8,128)(2,1)S(1)}, u32[]{:S(2)}, u32[]{:S(2)}) collective-permute-start(bf16[8,512,128]{2,1,0:T(8,128)(2,1)S(1)} %get-tuple-element.30.mine), channel_id=1, source_target_pairs={{0,1},{1,0},{2,3},{3,2},{4,5},{5,4},{6,7},{7,6},{8,9},{9,8},{10,11... | collective-permute-start | bytes 3145736 | tf_op jit(solution)/shard_map/ppermute | solution.py:567
  79.1 2.3 %collective-permute-done.6.theirs = bf16[8,512,128]{2,1,0:T(8,128)(2,1)S(1)} collective-permute-done((bf16[8,512,128]{2,1,0:T(8,128)(2,1)S(1)}, bf16[8,512,128]{2,1,0:T(8,128)(2,1)S(1)}, u32[]{:S(2)}, u32[]{:S(2)}) %collective-permute-start.6) | collective-permute-done | bytes 1048608 | tf_op jit(solution)/shard_map/ppermute | solution.py:567
  81.4 0.3 maximum_select_fusion
  81.8 0.1 slice_select_fusion.2
  81.8 0.1 fusion.3
  81.9 0.7 collective-permute-start.7
  82.6 0.7 collective-permute-start.8
  83.3 0.7 collective-permute-start.10
  84.0 0.7 collective-permute-start.9
  84.7 17.3 %chip_couple.1 = (f32[16,9,64,128]{3,2,1,0:T(8,128)}, f32[8,9,64,128]{3,2,1,0:T(8,128)}, bf16[22,128,512]{2,1,0:T(8,128)(2,1)S(1)}) custom-call(s32[1]{0:T(128)} %bitcast.core_ref, s32[8,9]{1,0:T(8,128)S(1)} %constant_dynamic-slice_fusion.1.mask, s32[2,34,6]{2,1,0:T(8,128)S(1)} %copy-done.3, s32[2,22,6]{2,1,0:T(8,128)S(1)} %copy-done.2, ...), custom_call_target="tpu_custom_call" | custom-call | flops 8000000000 | bytes 32000000 | tf_op jit(solution)/shard_map/chip_couple/pallas_call | solution.py:660
  102.0 18.0 %collective-permute-start.11 = (bf16[4,512,128]{2,1,0:T(8,128)(2,1)S(1)}, bf16[4,512,128]{2,1,0:T(8,128)(2,1)S(1)}, u32[]{:S(2)}, u32[]{:S(2)}) collective-permute-start(bf16[4,512,128]{2,1,0:T(8,128)(2,1)S(1)} %collective-permute-done.7.first_col), channel_id=1, source_target_pairs={{0,1},{1,0},{2,3},{3,2},{4,5},{5,4},{6,7},{7,6},{8,9},{9,8},{10,11... | collective-permute-start | bytes 1572872 | tf_op jit(solution)/shard_map/ppermute | solution.py:567
  120.0 1.5 %collective-permute-done.11.second_col = bf16[4,512,128]{2,1,0:T(8,128)(2,1)S(1)} collective-permute-done((bf16[4,512,128]{2,1,0:T(8,128)(2,1)S(1)}, bf16[4,512,128]{2,1,0:T(8,128)(2,1)S(1)}, u32[]{:S(2)}, u32[]{:S(2)}) %collective-permute-start.11) | collective-permute-done | bytes 524320 | tf_op jit(solution)/shard_map/ppermute | solution.py:567
  121.6 0.4 collective-permute-start.12
  121.9 4.3 %edge_couple.1 = (f32[16,9,64,128]{3,2,1,0:T(8,128)}, f32[22,64,128]{2,1,0:T(8,128)}) custom-call(s32[1]{0:T(128)} %bitcast.core_ref, s32[8,9]{1,0:T(8,128)S(1)} %constant_dynamic-slice_fusion.1.mask, s32[2,22,6]{2,1,0:T(8,128)S(1)} %copy-done.2, bf16[22,128,512]{2,1,0:T(8,128)(2,1)S(1)} %get-tuple-element.38.projected, ...), custom_call_target="tpu_custom_call", output_to_operand_aliasing={{0}: (9, {})} | custom-call | tf_op jit(solution)/shard_map/edge_couple/pallas_call | solution.py:693
  126.2 0.2 collective-permute-start.13
  126.4 2.3 %constant_dynamic-slice_fusion = bf16[16,256,128]{2,1,0:T(8,128)(2,1)} fusion(bf16[16,512,128]{2,1,0:T(8,128)(2,1)} %copy-done.4, s32[]{:T(128)S(6)} %select_n.150), kind=kLoop, calls=%fused_computation.21 | loop fusion | bytes 2097156 | tf_op jit(solution)/shard_map/dynamic_slice | solution.py:719
  128.7 3.4 %settle.1 = f32[16,9,64,128]{3,2,1,0:T(8,128)} custom-call(s32[1]{0:T(128)} %bitcast.core_ref, s32[2,22,6]{2,1,0:T(8,128)S(1)} %copy-done.2, f32[8,9,64,128]{3,2,1,0:T(8,128)S(1)} %collective-permute-done.12.bulk, f32[22,64,128]{2,1,0:T(8,128)S(1)} %collective-permute-done.13.taken, ...), custom_call_target="tpu_custom_call", output_to_operand_aliasing={{}: (4, {})} | custom-call | tf_op jit(solution)/shard_map/settle/pallas_call | solution.py:709
  (25 shorter events, 0.2 us)
Async XLA Ops:
  0.6 1.5 %copy-start = (s32[16,9]{1,0:T(8,128)S(1)}, s32[16,9]{1,0:T(8,128)}, u32[]{:S(2)}) copy-start(s32[16,9]{1,0:T(8,128)} %param.7) | copy-start | bytes 1732
  0.6 3.0 %collective-permute-start = (bf16[16,256,128]{2,1,0:T(8,128)(2,1)}, bf16[16,256,128]{2,1,0:T(8,128)(2,1)S(1)}, u32[]{:S(2)}, u32[]{:S(2)}) collective-permute-start(bf16[16,256,128]{2,1,0:T(8,128)(2,1)} %mine.1), channel_id=1, source_target_pairs={{0,1},{1,0},{2,3},{3,2},{4,5},{5,4},{6,7},{7,6},{8,9},{9,8},{10,11... | collective-permute-start | bytes 3145736 | tf_op jit(solution)/shard_map/ppermute | solution.py:567
  5.9 2.3 %copy-start.1 = (bf16[16,256,128]{2,1,0:T(8,128)(2,1)S(1)}, bf16[16,256,128]{2,1,0:T(8,128)(2,1)}, u32[]{:S(2)}) copy-start(bf16[16,256,128]{2,1,0:T(8,128)(2,1)} %mine.1) | copy-start | bytes 3145732
  6.0 25.9 %collective-permute-start.3 = (bf16[1,528,128]{2,1,0:T(8,128)(2,1)S(1)}, bf16[1,528,128]{2,1,0:T(8,128)(2,1)S(1)}, u32[]{:S(2)}, u32[]{:S(2)}) collective-permute-start(bf16[1,528,128]{2,1,0:T(8,128)(2,1)S(1)} %get-tuple-element.47), channel_id=1, source_target_pairs={{1,10},{3,12},{5,14},{9,18},{10,1},{11,20},{12,3},{13,22},{14,5},{... | collective-permute-start | bytes 405512 | tf_op jit(solution)/shard_map/ppermute | solution.py:555
  6.8 2.8 %copy-start.3 = (s32[2,34,6]{2,1,0:T(8,128)S(1)}, s32[2,34,6]{2,1,0:T(8,128)}, u32[]{:S(2)}) copy-start(s32[2,34,6]{2,1,0:T(8,128)} %constant.20.clone.table) | copy-start | bytes 4900
  6.8 25.1 %collective-permute-start.4 = (bf16[1,528,128]{2,1,0:T(8,128)(2,1)S(1)}, bf16[1,528,128]{2,1,0:T(8,128)(2,1)S(1)}, u32[]{:S(2)}, u32[]{:S(2)}) collective-permute-start(bf16[1,528,128]{2,1,0:T(8,128)(2,1)S(1)} %get-tuple-element.46), channel_id=1, source_target_pairs={{3,8},{5,10},{7,12},{8,3},{10,5},{11,16},{12,7},{13,18},{15,20},{1... | collective-permute-start | bytes 405512 | tf_op jit(solution)/shard_map/ppermute | solution.py:555
  7.5 24.4 %collective-permute-start.1 = (bf16[4,528,128]{2,1,0:T(8,128)(2,1)S(1)}, bf16[4,528,128]{2,1,0:T(8,128)(2,1)S(1)}, u32[]{:S(2)}, u32[]{:S(2)}) collective-permute-start(bf16[4,528,128]{2,1,0:T(8,128)(2,1)S(1)} %fusion.2), channel_id=1, source_target_pairs={{1,2},{2,1},{3,4},{4,3},{5,6},{6,5},{9,10},{10,9},{11,12},{12,11},... | collective-permute-start | bytes 1622024 | tf_op jit(solution)/shard_map/ppermute | solution.py:555
  8.9 23.1 %collective-permute-start.2 = (bf16[4,528,128]{2,1,0:T(8,128)(2,1)S(1)}, bf16[4,528,128]{2,1,0:T(8,128)(2,1)S(1)}, u32[]{:S(2)}, u32[]{:S(2)}) collective-permute-start(bf16[4,528,128]{2,1,0:T(8,128)(2,1)S(1)} %slice_select_fusion), channel_id=1, source_target_pairs={{1,8},{3,10},{5,12},{7,14},{8,1},{9,16},{10,3},{11,18},{12,5},{13,... | collective-permute-start | bytes 1622024 | tf_op jit(solution)/shard_map/ppermute | solution.py:555
  9.6 34.3 %copy-start.2 = (s32[2,22,6]{2,1,0:T(8,128)S(1)}, s32[2,22,6]{2,1,0:T(8,128)}, u32[]{:S(2)}) copy-start(s32[2,22,6]{2,1,0:T(8,128)} %constant.21.clone.table.edge_table) | copy-start | bytes 3172
  32.0 12.0 %collective-permute-start.5 = (bf16[4,528,128]{2,1,0:T(8,128)(2,1)S(1)}, bf16[4,528,128]{2,1,0:T(8,128)(2,1)S(1)}, u32[]{:S(2)}, u32[]{:S(2)}) collective-permute-start(bf16[4,528,128]{2,1,0:T(8,128)(2,1)S(1)} %collective-permute-done.1.first_col), channel_id=1, source_target_pairs={{0,1},{1,0},{2,3},{3,2},{4,5},{5,4},{6,7},{7,6},{8,9},{9,8},{10,11... | collective-permute-start | bytes 1622024 | tf_op jit(solution)/shard_map/ppermute | solution.py:567
  73.7 7.7 %collective-permute-start.6 = (bf16[8,512,128]{2,1,0:T(8,128)(2,1)S(1)}, bf16[8,512,128]{2,1,0:T(8,128)(2,1)S(1)}, u32[]{:S(2)}, u32[]{:S(2)}) collective-permute-start(bf16[8,512,128]{2,1,0:T(8,128)(2,1)S(1)} %get-tuple-element.30.mine), channel_id=1, source_target_pairs={{0,1},{1,0},{2,3},{3,2},{4,5},{5,4},{6,7},{7,6},{8,9},{9,8},{10,11... | collective-permute-start | bytes 3145736 | tf_op jit(solution)/shard_map/ppermute | solution.py:567
  81.8 2.9 %copy-start.4 = (bf16[16,512,128]{2,1,0:T(8,128)(2,1)}, bf16[16,512,128]{2,1,0:T(8,128)(2,1)S(1)}, u32[]{:S(2)}) copy-start(bf16[16,512,128]{2,1,0:T(8,128)(2,1)S(1)} %maximum_select_fusion) | copy-start | bytes 6291460
  81.9 20.1 %collective-permute-start.7 = (bf16[4,512,128]{2,1,0:T(8,128)(2,1)S(1)}, bf16[4,512,128]{2,1,0:T(8,128)(2,1)S(1)}, u32[]{:S(2)}, u32[]{:S(2)}) collective-permute-start(bf16[4,512,128]{2,1,0:T(8,128)(2,1)S(1)} %fusion.3), channel_id=1, source_target_pairs={{1,2},{2,1},{3,4},{4,3},{5,6},{6,5},{9,10},{10,9},{11,12},{12,11},... | collective-permute-start | bytes 1572872 | tf_op jit(solution)/shard_map/ppermute | solution.py:555
  82.6 19.4 %collective-permute-start.8 = (bf16[4,512,128]{2,1,0:T(8,128)(2,1)S(1)}, bf16[4,512,128]{2,1,0:T(8,128)(2,1)S(1)}, u32[]{:S(2)}, u32[]{:S(2)}) collective-permute-start(bf16[4,512,128]{2,1,0:T(8,128)(2,1)S(1)} %slice_select_fusion.2), channel_id=1, source_target_pairs={{1,8},{3,10},{5,12},{7,14},{8,1},{9,16},{10,3},{11,18},{12,5},{13,... | collective-permute-start | bytes 1572872 | tf_op jit(solution)/shard_map/ppermute | solution.py:555
  83.3 18.7 %collective-permute-start.10 = (bf16[1,512,128]{2,1,0:T(8,128)(2,1)S(1)}, bf16[1,512,128]{2,1,0:T(8,128)(2,1)S(1)}, u32[]{:S(2)}, u32[]{:S(2)}) collective-permute-start(bf16[1,512,128]{2,1,0:T(8,128)(2,1)S(1)} %get-tuple-element.48), channel_id=1, source_target_pairs={{3,8},{5,10},{7,12},{8,3},{10,5},{11,16},{12,7},{13,18},{15,20},{1... | collective-permute-start | bytes 393224 | tf_op jit(solution)/shard_map/ppermute | solution.py:555
  84.0 18.0 %collective-permute-start.9 = (bf16[1,512,128]{2,1,0:T(8,128)(2,1)S(1)}, bf16[1,512,128]{2,1,0:T(8,128)(2,1)S(1)}, u32[]{:S(2)}, u32[]{:S(2)}) collective-permute-start(bf16[1,512,128]{2,1,0:T(8,128)(2,1)S(1)} %get-tuple-element.49), channel_id=1, source_target_pairs={{1,10},{3,12},{5,14},{9,18},{10,1},{11,20},{12,3},{13,22},{14,5},{... | collective-permute-start | bytes 393224 | tf_op jit(solution)/shard_map/ppermute | solution.py:555
  102.0 19.5 %collective-permute-start.11 = (bf16[4,512,128]{2,1,0:T(8,128)(2,1)S(1)}, bf16[4,512,128]{2,1,0:T(8,128)(2,1)S(1)}, u32[]{:S(2)}, u32[]{:S(2)}) collective-permute-start(bf16[4,512,128]{2,1,0:T(8,128)(2,1)S(1)} %collective-permute-done.7.first_col), channel_id=1, source_target_pairs={{0,1},{1,0},{2,3},{3,2},{4,5},{5,4},{6,7},{7,6},{8,9},{9,8},{10,11... | collective-permute-start | bytes 1572872 | tf_op jit(solution)/shard_map/ppermute | solution.py:567
  121.6 7.2 %collective-permute-start.12 = (f32[8,9,64,128]{3,2,1,0:T(8,128)}, f32[8,9,64,128]{3,2,1,0:T(8,128)S(1)}, u32[]{:S(2)}, u32[]{:S(2)}) collective-permute-start(f32[8,9,64,128]{3,2,1,0:T(8,128)} %get-tuple-element.37), channel_id=1, source_target_pairs={{0,1},{1,0},{2,3},{3,2},{4,5},{5,4},{6,7},{7,6},{8,9},{9,8},{10,11... | collective-permute-start | bytes 7077896 | tf_op jit(solution)/shard_map/ppermute | solution.py:567
  126.2 2.5 %collective-permute-start.13 = (f32[22,64,128]{2,1,0:T(8,128)}, f32[22,64,128]{2,1,0:T(8,128)S(1)}, u32[]{:S(2)}, u32[]{:S(2)}) collective-permute-start(f32[22,64,128]{2,1,0:T(8,128)} %get-tuple-element.44), channel_id=1, source_target_pairs={{0,1},{1,0},{2,3},{3,2},{4,5},{5,4},{6,7},{7,6},{8,9},{9,8},{10,11... | collective-permute-start | bytes 2162696 | tf_op jit(solution)/shard_map/ppermute | solution.py:567

commit v5 on v4

--- a/solution.py
+++ b/solution.py
@@ -390,8 +390,8 @@
 
 
 def chip_couple_kernel(counts, core_ref, mask, table, edge_table, mine, theirs, store, edge_store,
-                       full, give, projected, basis, basis_t, chip_held, blocks, active, edge_active, found, ray_a, ray_b, out_sems,
-                       chip_sems, fetch_sems):
+                       full, give, projected, basis_out, basis, basis_t, chip_held, blocks, active, edge_active, found, ray_a, ray_b, out_sems,
+                       chip_sems, fetch_sems, basis_sem):
     core = core_ref[0]
     own_boxes, box_points, skel_rank = mine.shape
 
@@ -411,6 +411,11 @@
     half = give.shape[2]
     basis[pl.ds(core * own_boxes, own_boxes)] = mine[...]
     basis[pl.ds((1 - core) * own_boxes, own_boxes)] = theirs[...]
+    half_points = box_points // 2
+    basis_copy = pltpu.make_async_copy(
+        basis.at[:, pl.ds(pl.multiple_of(core * half_points, half_points), half_points), :], basis_out, basis_sem.at[0]
+    )
+    basis_copy.start()
     for own in range(own_boxes):
         basis_t[own] = jnp.transpose(mine[own])
 
@@ -473,6 +478,7 @@
         return carry
 
     lax.fori_loop(0, (edge_total + 1) // 2, edge_project, 0)
+    basis_copy.wait()
     for copy in copies:
         copy.wait()
 
@@ -504,18 +510,22 @@
         copy.wait()
 
 
-def settle_kernel(core_ref, edge_table, bulk, taken, full_in, full, bulk_sems, sems):
+def bulk_kernel(core_ref, bulk, full_in, full, sems):
     other = 1 - core_ref[0]
     own_boxes = full.shape[0] // 2
-    moves = [
-        pltpu.make_async_copy(bulk.at[own], full.at[other * own_boxes + own], bulk_sems.at[own])
+    copies = [
+        pltpu.make_async_copy(bulk.at[own], full.at[other * own_boxes + own], sems.at[own])
         for own in range(own_boxes)
     ]
-    for move in moves:
-        move.start()
-    for move in moves:
-        move.wait()
-
+    for copy in copies:
+        copy.start()
+    for copy in copies:
+        copy.wait()
+
+
+def settle_kernel(core_ref, edge_table, taken, full_in, full, sems):
+    other = 1 - core_ref[0]
+    own_boxes = full.shape[0] // 2
     copies = [
         pltpu.make_async_copy(
             taken.at[index],
@@ -540,8 +550,8 @@
     return pltpu.CompilerParams(vmem_limit_bytes=mebibytes << 20)
 
 
-def exchange(boxes, core, grid_side):
-    side = boxes.shape[0]
+def exchange(parts, join, core, grid_side):
+    side = parts[0].shape[0]
 
     def send(piece, step_y, step_x):
         pairs = []
@@ -556,10 +566,15 @@
 
     last = side - 1
     low = core == 0
-    col = send(jnp.where(low, boxes[:, 0], boxes[:, last]), 0, 1)
-    row = send(jnp.where(low, boxes[0], boxes[last]), 1, 0)
-    corner_a = send(jnp.where(low, boxes[0, 0:1], boxes[last, last:]), 1, 1)
-    corner_b = send(jnp.where(low, boxes[0, last:], boxes[last, 0:1]), 1, -1)
+
+    def border(below, above):
+        return join(*(jnp.where(low, part[below], part[above]) for part in parts))
+
+    every = slice(None)
+    col = send(border((every, 0), (every, last)), 0, 1)
+    row = send(border((0,), (last,)), 1, 0)
+    corner_a = send(border((0, slice(0, 1)), (last, slice(last, side))), 1, 1)
+    corner_b = send(border((0, slice(last, side)), (last, slice(0, 1))), 1, -1)
     return col, row, corner_a, corner_b
 
 
@@ -588,12 +603,16 @@
     theirs = swap(sketch)
     packed = points.reshape(chip_boxes, 3 * box_points // skel_rank, skel_rank)
     packed = jnp.pad(packed, ((0, 0), (0, 16 - packed.shape[1]), (0, 0)))
-    whole = jnp.where(
-        low,
-        jnp.concatenate([sketch, theirs, packed], axis=1),
-        jnp.concatenate([theirs, sketch, packed], axis=1),
-    ).reshape(tile_side, tile_side, box_points + 16, skel_rank)
-    col, row, corner_a, corner_b = exchange(whole, core, grid_side)
+
+    def join(mine, other, coords):
+        return jnp.where(
+            low,
+            jnp.concatenate([mine, other, coords], axis=1),
+            jnp.concatenate([other, mine, coords], axis=1),
+        )
+
+    parts = [part.reshape((tile_side, tile_side) + part.shape[1:]) for part in (sketch, theirs, packed)]
+    col, row, corner_a, corner_b = exchange(parts, join, core, grid_side)
 
     bf16, f32 = jnp.bfloat16, jnp.float32
     sketched, store = pl.pallas_call(
@@ -655,17 +674,18 @@
         jnp.concatenate([basis, other_basis], axis=0),
         jnp.concatenate([other_basis, basis], axis=0),
     ).reshape(tile_side, tile_side, box_points, skel_rank)
-    col, row, corner_a, corner_b = exchange(whole, core, grid_side)
+    col, row, corner_a, corner_b = exchange([whole], lambda boxes: boxes, core, grid_side)
     coupling_shape = jax.ShapeDtypeStruct((chip_boxes, 9, half_rank, skel_rank), f32)
-    coupling, give, projected = pl.pallas_call(
+    coupling, give, projected, basis_out = pl.pallas_call(
         functools.partial(chip_couple_kernel, counts),
         out_shape=(
             coupling_shape,
             jax.ShapeDtypeStruct((own_boxes, 9, half_rank, skel_rank), f32),
             jax.ShapeDtypeStruct((edge_blocks, skel_rank, box_points), bf16),
+            jax.ShapeDtypeStruct((chip_boxes, half_points, skel_rank), bf16),
         ),
         in_specs=[SMEM] * 4 + [VMEM] * 2 + [HBM] * 2,
-        out_specs=(ANY, ANY, VMEM),
+        out_specs=(ANY, ANY, VMEM, ANY),
         scratch_shapes=[
             pltpu.VMEM((chip_boxes, box_points, skel_rank), bf16),
             pltpu.VMEM((own_boxes, skel_rank, box_points), bf16),
@@ -679,6 +699,7 @@
             pltpu.SemaphoreType.DMA((2 * own_boxes,)),
             pltpu.SemaphoreType.DMA((chip_blocks,)),
             pltpu.SemaphoreType.DMA((edge_blocks,)),
+            pltpu.SemaphoreType.DMA((1,)),
         ],
         compiler_params=params(46),
         cost_estimate=pl.CostEstimate(flops=8 * 10**9, bytes_accessed=32 * 10**6, transcendentals=0),
@@ -707,18 +728,26 @@
     )(core_arg, own_mask, edge_table, projected, col, second_col, row, corner_a, corner_b, coupling)
     taken = swap(give)
     coupling = pl.pallas_call(
+        bulk_kernel,
+        out_shape=coupling_shape,
+        in_specs=[SMEM, VMEM, ANY],
+        out_specs=ANY,
+        scratch_shapes=[pltpu.SemaphoreType.DMA((own_boxes,))],
+        input_output_aliases={2: 0},
+        compiler_params=params(12),
+        cost_estimate=pl.CostEstimate(flops=0, bytes_accessed=10 * 10**6, transcendentals=0),
+        name="bulk",
+    )(core_arg, bulk, coupling)
+    coupling = pl.pallas_call(
         settle_kernel,
         out_shape=coupling_shape,
-        in_specs=[SMEM] * 2 + [VMEM, VMEM, ANY],
+        in_specs=[SMEM] * 2 + [VMEM, ANY],
         out_specs=ANY,
-        scratch_shapes=[pltpu.SemaphoreType.DMA((own_boxes,)), pltpu.SemaphoreType.DMA((edge_blocks,))],
-        input_output_aliases={4: 0},
-        compiler_params=params(20),
+        scratch_shapes=[pltpu.SemaphoreType.DMA((edge_blocks,))],
+        input_output_aliases={3: 0},
+        compiler_params=params(12),
         name="settle",
-    )(core_arg, edge_table, bulk, taken, coupling)
-    basis_out = lax.dynamic_slice_in_dim(
-        whole.reshape(chip_boxes, box_points, skel_rank), core * half_points, half_points, 1
-    )
+    )(core_arg, edge_table, taken, coupling)
     return basis_out, coupling
 
 

time: 132 us -> 130 us (0.985)
  the two profiles are of different devices: /device:TPU:0 before, /device:TPU:21 now
where the time goes in v5:
time: 130 us; the launch traced here: 129 us
  Pallas kernels  89.1 us (69%)
  starting transfers between devices  28.5 us (22%)
  waiting for transfers between devices  5.99 us (5%)
  other arithmetic  2.98 us (2%)
    pallas_call x1, Pallas kernels, body(): pl.pallas_call(edge_sketch_kernel, out_shape=(jax.ShapeDtypeStruct((own_b...  38.9 us
    pallas_call x1, Pallas kernels, body(): pl.pallas_call(functools.partial(chip_sketch_kernel, counts), out_shape=(...  23.9 us
    ppermute x8, starting transfers between devices, send(): return lax.ppermute(piece, ('box', 'col'), pairs)  21.5 us
    pallas_call x1, Pallas kernels, body(): pl.pallas_call(functools.partial(chip_couple_kernel, counts), out_shape=(...  19.3 us
    ppermute x6, starting transfers between devices, swap(): return lax.ppermute(value, 'col', [(0, 1), (1, 0)])  7.02 us
    ppermute x6, waiting for transfers between devices, swap(): return lax.ppermute(value, 'col', [(0, 1), (1, 0)])  5.97 us
    pallas_call x1, Pallas kernels, body(): pl.pallas_call(edge_couple_kernel, out_shape=(coupling_shape, jax.ShapeDt...  3.43 us
  transfers between devices with their start and end apart: 14, of which 5 were waited for; matrix products, arithmetic and copies ran while one was open for 3% of the time, Pallas kernels for 37%

profile of v5, /device:TPU:21, one launch (start us, length us, event | category | flops | bytes accessed | tf_op | source)
XLA Modules:
  0.0 128.7 jit_solution(13931742408318514800)
XLA Ops:
  0.7 0.7 collective-permute-start
  1.4 0.8 copy.21.points
  2.4 1.0 fusion.11
  3.4 1.1 fusion.3
  4.6 4.1 %collective-permute-start.3 = (bf16[1,528,128]{2,1,0:T(8,128)(2,1)S(1)}, bf16[1,528,128]{2,1,0:T(8,128)(2,1)S(1)}, u32[]{:S(2)}, u32[]{:S(2)}) collective-permute-start(bf16[1,528,128]{2,1,0:T(8,128)(2,1)S(1)} %fusion.7), channel_id=1, source_target_pairs={{1,10},{3,12},{5,14},{9,18},{10,1},{11,20},{12,3},{13,22},{14,5},{... | collective-permute-start | bytes 405512 | tf_op jit(solution)/shard_map/ppermute | solution.py:565
  8.8 2.3 %collective-permute-start.4 = (bf16[1,528,128]{2,1,0:T(8,128)(2,1)S(1)}, bf16[1,528,128]{2,1,0:T(8,128)(2,1)S(1)}, u32[]{:S(2)}, u32[]{:S(2)}) collective-permute-start(bf16[1,528,128]{2,1,0:T(8,128)(2,1)S(1)} %fusion.6), channel_id=1, source_target_pairs={{3,8},{5,10},{7,12},{8,3},{10,5},{11,16},{12,7},{13,18},{15,20},{1... | collective-permute-start | bytes 405512 | tf_op jit(solution)/shard_map/ppermute | solution.py:565
  11.1 0.1 fusion
  11.3 1.9 %collective-permute-start.2 = (bf16[4,528,128]{2,1,0:T(8,128)(2,1)S(1)}, bf16[4,528,128]{2,1,0:T(8,128)(2,1)S(1)}, u32[]{:S(2)}, u32[]{:S(2)}) collective-permute-start(bf16[4,528,128]{2,1,0:T(8,128)(2,1)S(1)} %fusion), channel_id=1, source_target_pairs={{1,8},{3,10},{5,12},{7,14},{8,1},{9,16},{10,3},{11,18},{12,5},{13,... | collective-permute-start | bytes 1622024 | tf_op jit(solution)/shard_map/ppermute | solution.py:565
  13.2 0.1 fusion.1
  13.4 3.5 %collective-permute-start.1 = (bf16[4,528,128]{2,1,0:T(8,128)(2,1)S(1)}, bf16[4,528,128]{2,1,0:T(8,128)(2,1)S(1)}, u32[]{:S(2)}, u32[]{:S(2)}) collective-permute-start(bf16[4,528,128]{2,1,0:T(8,128)(2,1)S(1)} %fusion.1), channel_id=1, source_target_pairs={{1,2},{2,1},{3,4},{4,3},{5,6},{6,5},{9,10},{10,9},{11,12},{12,11},... | collective-permute-start | bytes 1622024 | tf_op jit(solution)/shard_map/ppermute | solution.py:565
  16.9 23.9 %chip_sketch.1 = (f32[8,512,128]{2,1,0:T(8,128)}, bf16[34,512,512]{2,1,0:T(8,128)(2,1)}) custom-call(s32[1]{0:T(128)} %bitcast.core_ref, s32[8,9]{1,0:T(8,128)S(1)} %constant_dynamic-slice_fusion.mask, s32[2,34,6]{2,1,0:T(8,128)S(1)} %copy-done.3, bf16[16,3,512]{2,1,0:T(4,128)(2,1)S(1)} %copy.21.points, bf16[16,256,128]{2,1,0:T(8,128)(2,1)S(1)} %copy-done.1, ...), custom_call_target="tpu_custom_call" | custom-call | flops 8000000000 | bytes 24000000 | tf_op jit(solution)/shard_map/chip_sketch/pallas_call | solution.py:618
  40.9 2.9 %collective-permute-start.5 = (bf16[4,528,128]{2,1,0:T(8,128)(2,1)S(1)}, bf16[4,528,128]{2,1,0:T(8,128)(2,1)S(1)}, u32[]{:S(2)}, u32[]{:S(2)}) collective-permute-start(bf16[4,528,128]{2,1,0:T(8,128)(2,1)S(1)} %collective-permute-done.1.first_col), channel_id=1, source_target_pairs={{0,1},{1,0},{2,3},{3,2},{4,5},{5,4},{6,7},{7,6},{8,9},{9,8},{10,11... | collective-permute-start | bytes 1622024 | tf_op jit(solution)/shard_map/ppermute | solution.py:582
  43.8 1.6 %collective-permute-done.5.second_col = bf16[4,528,128]{2,1,0:T(8,128)(2,1)S(1)} collective-permute-done((bf16[4,528,128]{2,1,0:T(8,128)(2,1)S(1)}, bf16[4,528,128]{2,1,0:T(8,128)(2,1)S(1)}, u32[]{:S(2)}, u32[]{:S(2)}) %collective-permute-start.5) | collective-permute-done | bytes 540704 | tf_op jit(solution)/shard_map/ppermute | solution.py:582
  45.3 38.9 %edge_sketch.1 = (bf16[8,512,128]{2,1,0:T(8,128)(2,1)S(1)}, bf16[22,512,512]{2,1,0:T(8,128)(2,1)}) custom-call(s32[1]{0:T(128)} %bitcast.core_ref, s32[8,9]{1,0:T(8,128)S(1)} %constant_dynamic-slice_fusion.mask, s32[2,22,6]{2,1,0:T(8,128)S(1)} %copy-done.2, bf16[16,3,512]{2,1,0:T(4,128)(2,1)S(1)} %copy.21.points, f32[8,512,128]{2,1,0:T(8,128)} %get-tuple-element.26.sketched, ...), custom_call_target="tpu_custom_call" | custom-call | tf_op jit(solution)/shard_map/edge_sketch/pallas_call | solution.py:644
  84.3 0.4 collective-permute-start.6
  84.7 2.3 %collective-permute-done.6.theirs = bf16[8,512,128]{2,1,0:T(8,128)(2,1)S(1)} collective-permute-done((bf16[8,512,128]{2,1,0:T(8,128)(2,1)S(1)}, bf16[8,512,128]{2,1,0:T(8,128)(2,1)S(1)}, u32[]{:S(2)}, u32[]{:S(2)}) %collective-permute-start.6) | collective-permute-done | bytes 1048608 | tf_op jit(solution)/shard_map/ppermute | solution.py:582
  87.0 0.3 maximum_select_fusion
  87.4 0.1 fusion.2
  87.5 1.9 %collective-permute-start.10 = (bf16[1,512,128]{2,1,0:T(8,128)(2,1)S(1)}, bf16[1,512,128]{2,1,0:T(8,128)(2,1)S(1)}, u32[]{:S(2)}, u32[]{:S(2)}) collective-permute-start(bf16[1,512,128]{2,1,0:T(8,128)(2,1)S(1)} %get-tuple-element.48), channel_id=1, source_target_pairs={{3,8},{5,10},{7,12},{8,3},{10,5},{11,16},{12,7},{13,18},{15,20},{1... | collective-permute-start | bytes 393224 | tf_op jit(solution)/shard_map/ppermute | solution.py:565
  89.4 1.9 %collective-permute-start.9 = (bf16[1,512,128]{2,1,0:T(8,128)(2,1)S(1)}, bf16[1,512,128]{2,1,0:T(8,128)(2,1)S(1)}, u32[]{:S(2)}, u32[]{:S(2)}) collective-permute-start(bf16[1,512,128]{2,1,0:T(8,128)(2,1)S(1)} %get-tuple-element.49), channel_id=1, source_target_pairs={{1,10},{3,12},{5,14},{9,18},{10,1},{11,20},{12,3},{13,22},{14,5},{... | collective-permute-start | bytes 393224 | tf_op jit(solution)/shard_map/ppermute | solution.py:565
  91.4 2.0 %collective-permute-start.8 = (bf16[4,512,128]{2,1,0:T(8,128)(2,1)S(1)}, bf16[4,512,128]{2,1,0:T(8,128)(2,1)S(1)}, u32[]{:S(2)}, u32[]{:S(2)}) collective-permute-start(bf16[4,512,128]{2,1,0:T(8,128)(2,1)S(1)} %slice_select_fusion), channel_id=1, source_target_pairs={{1,8},{3,10},{5,12},{7,14},{8,1},{9,16},{10,3},{11,18},{12,5},{13,... | collective-permute-start | bytes 1572872 | tf_op jit(solution)/shard_map/ppermute | solution.py:565
  93.3 3.8 %collective-permute-start.7 = (bf16[4,512,128]{2,1,0:T(8,128)(2,1)S(1)}, bf16[4,512,128]{2,1,0:T(8,128)(2,1)S(1)}, u32[]{:S(2)}, u32[]{:S(2)}) collective-permute-start(bf16[4,512,128]{2,1,0:T(8,128)(2,1)S(1)} %fusion.2), channel_id=1, source_target_pairs={{1,2},{2,1},{3,4},{4,3},{5,6},{6,5},{9,10},{10,9},{11,12},{12,11},... | collective-permute-start | bytes 1572872 | tf_op jit(solution)/shard_map/ppermute | solution.py:565
  97.1 19.3 %chip_couple.1 = (f32[16,9,64,128]{3,2,1,0:T(8,128)}, f32[8,9,64,128]{3,2,1,0:T(8,128)S(1)}, bf16[22,128,512]{2,1,0:T(8,128)(2,1)S(1)}, bf16[16,256,128]{2,1,0:T(8,128)(2,1)}) custom-call(s32[1]{0:T(128)} %bitcast.core_ref, s32[8,9]{1,0:T(8,128)S(1)} %constant_dynamic-slice_fusion.mask, s32[2,34,6]{2,1,0:T(8,128)S(1)} %copy-done.3, ...), custom_call_target="tpu_custom_call" | custom-call | flops 8000000000 | bytes 32000000 | tf_op jit(solution)/shard_map/chip_couple/pallas_call | solution.py:679
  116.5 2.4 %collective-permute-start.11 = (bf16[4,512,128]{2,1,0:T(8,128)(2,1)S(1)}, bf16[4,512,128]{2,1,0:T(8,128)(2,1)S(1)}, u32[]{:S(2)}, u32[]{:S(2)}) collective-permute-start(bf16[4,512,128]{2,1,0:T(8,128)(2,1)S(1)} %collective-permute-done.7.first_col), channel_id=1, source_target_pairs={{0,1},{1,0},{2,3},{3,2},{4,5},{5,4},{6,7},{7,6},{8,9},{9,8},{10,11... | collective-permute-start | bytes 1572872 | tf_op jit(solution)/shard_map/ppermute | solution.py:582
  118.9 1.5 %collective-permute-done.11.second_col = bf16[4,512,128]{2,1,0:T(8,128)(2,1)S(1)} collective-permute-done((bf16[4,512,128]{2,1,0:T(8,128)(2,1)S(1)}, bf16[4,512,128]{2,1,0:T(8,128)(2,1)S(1)}, u32[]{:S(2)}, u32[]{:S(2)}) %collective-permute-start.11) | collective-permute-done | bytes 524320 | tf_op jit(solution)/shard_map/ppermute | solution.py:582
  120.4 0.4 collective-permute-start.13
  120.8 3.4 %edge_couple.1 = (f32[16,9,64,128]{3,2,1,0:T(8,128)}, f32[22,64,128]{2,1,0:T(8,128)S(1)}) custom-call(s32[1]{0:T(128)} %bitcast.core_ref, s32[8,9]{1,0:T(8,128)S(1)} %constant_dynamic-slice_fusion.mask, s32[2,22,6]{2,1,0:T(8,128)S(1)} %copy-done.2, bf16[22,128,512]{2,1,0:T(8,128)(2,1)S(1)} %get-tuple-element.37.projected, ...), custom_call_target="tpu_custom_call", output_to_operand_aliasing={{0}: (9, {})} | custom-call | tf_op jit(solution)/shard_map/edge_couple/pallas_call | solution.py:714
  124.2 0.2 collective-permute-start.12
  124.4 0.5 collective-permute-done.13.bulk
  125.0 1.5 %bulk.1.full_in = f32[16,9,64,128]{3,2,1,0:T(8,128)} custom-call(s32[1]{0:T(128)} %bitcast.core_ref, f32[8,9,64,128]{3,2,1,0:T(8,128)S(1)} %collective-permute-done.13.bulk, f32[16,9,64,128]{3,2,1,0:T(8,128)} %get-tuple-element.47.full_in), custom_call_target="tpu_custom_call", output_to_operand_aliasing={{}: (2, {})} | custom-call | bytes 10000000 | tf_op jit(solution)/shard_map/bulk/pallas_call | solution.py:730
  126.4 0.1 collective-permute-done.12.taken
  126.5 2.0 %settle.1 = f32[16,9,64,128]{3,2,1,0:T(8,128)} custom-call(s32[1]{0:T(128)} %bitcast.core_ref, s32[2,22,6]{2,1,0:T(8,128)S(1)} %copy-done.2, f32[22,64,128]{2,1,0:T(8,128)S(1)} %collective-permute-done.12.taken, f32[16,9,64,128]{3,2,1,0:T(8,128)} %bulk.1.full_in), custom_call_target="tpu_custom_call", output_to_operand_aliasing={{}: (3, {})} | custom-call | tf_op jit(solution)/shard_map/settle/pallas_call | solution.py:741
  (31 shorter events, 0.4 us)
Async XLA Ops:
  0.6 1.7 %copy-start = (s32[16,9]{1,0:T(8,128)S(1)}, s32[16,9]{1,0:T(8,128)}, u32[]{:S(2)}) copy-start(s32[16,9]{1,0:T(8,128)} %param.7) | copy-start | bytes 1732
  0.6 3.8 %copy-start.1 = (bf16[16,256,128]{2,1,0:T(8,128)(2,1)S(1)}, bf16[16,256,128]{2,1,0:T(8,128)(2,1)}, u32[]{:S(2)}) copy-start(bf16[16,256,128]{2,1,0:T(8,128)(2,1)} %mine.1) | copy-start | bytes 3145732
  0.7 3.8 %collective-permute-start = (bf16[16,256,128]{2,1,0:T(8,128)(2,1)}, bf16[16,256,128]{2,1,0:T(8,128)(2,1)S(1)}, u32[]{:S(2)}, u32[]{:S(2)}) collective-permute-start(bf16[16,256,128]{2,1,0:T(8,128)(2,1)} %mine.1), channel_id=1, source_target_pairs={{0,1},{1,0},{2,3},{3,2},{4,5},{5,4},{6,7},{7,6},{8,9},{9,8},{10,11... | collective-permute-start | bytes 3145736 | tf_op jit(solution)/shard_map/ppermute | solution.py:582
  4.5 12.4 %copy-start.3 = (s32[2,34,6]{2,1,0:T(8,128)S(1)}, s32[2,34,6]{2,1,0:T(8,128)}, u32[]{:S(2)}) copy-start(s32[2,34,6]{2,1,0:T(8,128)} %constant.16.clone.table) | copy-start | bytes 4900
  4.6 36.2 %collective-permute-start.3 = (bf16[1,528,128]{2,1,0:T(8,128)(2,1)S(1)}, bf16[1,528,128]{2,1,0:T(8,128)(2,1)S(1)}, u32[]{:S(2)}, u32[]{:S(2)}) collective-permute-start(bf16[1,528,128]{2,1,0:T(8,128)(2,1)S(1)} %fusion.7), channel_id=1, source_target_pairs={{1,10},{3,12},{5,14},{9,18},{10,1},{11,20},{12,3},{13,22},{14,5},{... | collective-permute-start | bytes 405512 | tf_op jit(solution)/shard_map/ppermute | solution.py:565
  8.8 32.1 %collective-permute-start.4 = (bf16[1,528,128]{2,1,0:T(8,128)(2,1)S(1)}, bf16[1,528,128]{2,1,0:T(8,128)(2,1)S(1)}, u32[]{:S(2)}, u32[]{:S(2)}) collective-permute-start(bf16[1,528,128]{2,1,0:T(8,128)(2,1)S(1)} %fusion.6), channel_id=1, source_target_pairs={{3,8},{5,10},{7,12},{8,3},{10,5},{11,16},{12,7},{13,18},{15,20},{1... | collective-permute-start | bytes 405512 | tf_op jit(solution)/shard_map/ppermute | solution.py:565
  11.3 29.6 %collective-permute-start.2 = (bf16[4,528,128]{2,1,0:T(8,128)(2,1)S(1)}, bf16[4,528,128]{2,1,0:T(8,128)(2,1)S(1)}, u32[]{:S(2)}, u32[]{:S(2)}) collective-permute-start(bf16[4,528,128]{2,1,0:T(8,128)(2,1)S(1)} %fusion), channel_id=1, source_target_pairs={{1,8},{3,10},{5,12},{7,14},{8,1},{9,16},{10,3},{11,18},{12,5},{13,... | collective-permute-start | bytes 1622024 | tf_op jit(solution)/shard_map/ppermute | solution.py:565
  13.4 27.5 %collective-permute-start.1 = (bf16[4,528,128]{2,1,0:T(8,128)(2,1)S(1)}, bf16[4,528,128]{2,1,0:T(8,128)(2,1)S(1)}, u32[]{:S(2)}, u32[]{:S(2)}) collective-permute-start(bf16[4,528,128]{2,1,0:T(8,128)(2,1)S(1)} %fusion.1), channel_id=1, source_target_pairs={{1,2},{2,1},{3,4},{4,3},{5,6},{6,5},{9,10},{10,9},{11,12},{12,11},... | collective-permute-start | bytes 1622024 | tf_op jit(solution)/shard_map/ppermute | solution.py:565
  16.9 28.4 %copy-start.2 = (s32[2,22,6]{2,1,0:T(8,128)S(1)}, s32[2,22,6]{2,1,0:T(8,128)}, u32[]{:S(2)}) copy-start(s32[2,22,6]{2,1,0:T(8,128)} %constant.17.clone.table.edge_table) | copy-start | bytes 3172
  40.9 4.5 %collective-permute-start.5 = (bf16[4,528,128]{2,1,0:T(8,128)(2,1)S(1)}, bf16[4,528,128]{2,1,0:T(8,128)(2,1)S(1)}, u32[]{:S(2)}, u32[]{:S(2)}) collective-permute-start(bf16[4,528,128]{2,1,0:T(8,128)(2,1)S(1)} %collective-permute-done.1.first_col), channel_id=1, source_target_pairs={{0,1},{1,0},{2,3},{3,2},{4,5},{5,4},{6,7},{7,6},{8,9},{9,8},{10,11... | collective-permute-start | bytes 1622024 | tf_op jit(solution)/shard_map/ppermute | solution.py:582
  84.3 2.7 %collective-permute-start.6 = (bf16[8,512,128]{2,1,0:T(8,128)(2,1)S(1)}, bf16[8,512,128]{2,1,0:T(8,128)(2,1)S(1)}, u32[]{:S(2)}, u32[]{:S(2)}) collective-permute-start(bf16[8,512,128]{2,1,0:T(8,128)(2,1)S(1)} %get-tuple-element.31.mine), channel_id=1, source_target_pairs={{0,1},{1,0},{2,3},{3,2},{4,5},{5,4},{6,7},{7,6},{8,9},{9,8},{10,11... | collective-permute-start | bytes 3145736 | tf_op jit(solution)/shard_map/ppermute | solution.py:582
  87.5 29.0 %collective-permute-start.10 = (bf16[1,512,128]{2,1,0:T(8,128)(2,1)S(1)}, bf16[1,512,128]{2,1,0:T(8,128)(2,1)S(1)}, u32[]{:S(2)}, u32[]{:S(2)}) collective-permute-start(bf16[1,512,128]{2,1,0:T(8,128)(2,1)S(1)} %get-tuple-element.48), channel_id=1, source_target_pairs={{3,8},{5,10},{7,12},{8,3},{10,5},{11,16},{12,7},{13,18},{15,20},{1... | collective-permute-start | bytes 393224 | tf_op jit(solution)/shard_map/ppermute | solution.py:565
  89.4 27.1 %collective-permute-start.9 = (bf16[1,512,128]{2,1,0:T(8,128)(2,1)S(1)}, bf16[1,512,128]{2,1,0:T(8,128)(2,1)S(1)}, u32[]{:S(2)}, u32[]{:S(2)}) collective-permute-start(bf16[1,512,128]{2,1,0:T(8,128)(2,1)S(1)} %get-tuple-element.49), channel_id=1, source_target_pairs={{1,10},{3,12},{5,14},{9,18},{10,1},{11,20},{12,3},{13,22},{14,5},{... | collective-permute-start | bytes 393224 | tf_op jit(solution)/shard_map/ppermute | solution.py:565
  91.4 25.1 %collective-permute-start.8 = (bf16[4,512,128]{2,1,0:T(8,128)(2,1)S(1)}, bf16[4,512,128]{2,1,0:T(8,128)(2,1)S(1)}, u32[]{:S(2)}, u32[]{:S(2)}) collective-permute-start(bf16[4,512,128]{2,1,0:T(8,128)(2,1)S(1)} %slice_select_fusion), channel_id=1, source_target_pairs={{1,8},{3,10},{5,12},{7,14},{8,1},{9,16},{10,3},{11,18},{12,5},{13,... | collective-permute-start | bytes 1572872 | tf_op jit(solution)/shard_map/ppermute | solution.py:565
  93.3 23.2 %collective-permute-start.7 = (bf16[4,512,128]{2,1,0:T(8,128)(2,1)S(1)}, bf16[4,512,128]{2,1,0:T(8,128)(2,1)S(1)}, u32[]{:S(2)}, u32[]{:S(2)}) collective-permute-start(bf16[4,512,128]{2,1,0:T(8,128)(2,1)S(1)} %fusion.2), channel_id=1, source_target_pairs={{1,2},{2,1},{3,4},{4,3},{5,6},{6,5},{9,10},{10,9},{11,12},{12,11},... | collective-permute-start | bytes 1572872 | tf_op jit(solution)/shard_map/ppermute | solution.py:565
  116.5 3.9 %collective-permute-start.11 = (bf16[4,512,128]{2,1,0:T(8,128)(2,1)S(1)}, bf16[4,512,128]{2,1,0:T(8,128)(2,1)S(1)}, u32[]{:S(2)}, u32[]{:S(2)}) collective-permute-start(bf16[4,512,128]{2,1,0:T(8,128)(2,1)S(1)} %collective-permute-done.7.first_col), channel_id=1, source_target_pairs={{0,1},{1,0},{2,3},{3,2},{4,5},{5,4},{6,7},{7,6},{8,9},{9,8},{10,11... | collective-permute-start | bytes 1572872 | tf_op jit(solution)/shard_map/ppermute | solution.py:582
  120.4 4.5 %collective-permute-start.13 = (f32[8,9,64,128]{3,2,1,0:T(8,128)S(1)}, f32[8,9,64,128]{3,2,1,0:T(8,128)S(1)}, u32[]{:S(2)}, u32[]{:S(2)}) collective-permute-start(f32[8,9,64,128]{3,2,1,0:T(8,128)S(1)} %get-tuple-element.46), channel_id=1, source_target_pairs={{0,1},{1,0},{2,3},{3,2},{4,5},{5,4},{6,7},{7,6},{8,9},{9,8},{10,11... | collective-permute-start | bytes 7077896 | tf_op jit(solution)/shard_map/ppermute | solution.py:582
  124.2 2.3 %collective-permute-start.12 = (f32[22,64,128]{2,1,0:T(8,128)S(1)}, f32[22,64,128]{2,1,0:T(8,128)S(1)}, u32[]{:S(2)}, u32[]{:S(2)}) collective-permute-start(f32[22,64,128]{2,1,0:T(8,128)S(1)} %get-tuple-element.45), channel_id=1, source_target_pairs={{0,1},{1,0},{2,3},{3,2},{4,5},{5,4},{6,7},{7,6},{8,9},{9,8},{10,11... | collective-permute-start | bytes 2162696 | tf_op jit(solution)/shard_map/ppermute | solution.py:582

commit v6 on v5

--- a/solution.py
+++ b/solution.py
@@ -322,7 +322,7 @@
 
 
 def edge_sketch_kernel(core_ref, mask, table, points, sketched, first_col, second_col, row, corner_a, corner_b,
-                       basis, store, extended, coords, own_coords, rows, y_ref, blocks, active, filled, load_sems, store_sems,
+                       basis, store, extended, coords, own_coords, rows, y_ref, blocks, active, load_sems, store_sems,
                        work, pivots, weights):
     core = core_ref[0]
     own_boxes, box_points, skel_rank = y_ref.shape
@@ -334,7 +334,7 @@
     soften = (0.25 / box_points) * stretch * stretch
     for own in range(own_boxes):
         fill_coords(own_coords, own, points[core * own_boxes + own].astype(jnp.float32), stretch)
-    filled[0] = -1
+        fill_rows(rows, own_coords[own], own, soften)
     for load in loads:
         load.wait()
     for box in range(extended.shape[0]):
@@ -344,12 +344,7 @@
         own, other, offset_y, offset_x, _, _ = place(table, core, index)
         shift_y, shift_x = offset_y.astype(jnp.float32) * stretch, offset_x.astype(jnp.float32) * stretch
 
-        @pl.when(own != filled[0])
-        def _():
-            fill_rows(rows, own_coords[own], 0, soften)
-            filled[0] = own
-
-        make_entries(blocks.at[index], rows, 0, coords, other, shift_y, shift_x)
+        make_entries(blocks.at[index], rows, own, coords, other, shift_y, shift_x)
         send(index).start()
         y_ref[own] += jnp.dot(
             blocks[index], extended[other, 0:box_points, :], preferred_element_type=jnp.float32
@@ -653,11 +648,10 @@
             pltpu.VMEM((edge_boxes, box_points + 16, skel_rank), bf16),
             pltpu.VMEM((edge_boxes, 8, box_points), f32),
             pltpu.VMEM((own_boxes, 8, box_points), f32),
-            pltpu.VMEM((1, 4, box_points, LANES), f32),
+            pltpu.VMEM((own_boxes, 4, box_points, LANES), f32),
             pltpu.VMEM((own_boxes, box_points, skel_rank), f32),
             pltpu.VMEM((edge_blocks, box_points, box_points), bf16),
             pltpu.SMEM((edge_blocks,), jnp.int32),
-            pltpu.SMEM((1,), jnp.int32),
             pltpu.SemaphoreType.DMA((6,)),
             pltpu.SemaphoreType.DMA((edge_blocks,)),
             pltpu.VMEM((skel_rank, own_boxes, skel_rank), f32),

time: 130 us -> 127 us (0.977)
  the two profiles are of different devices: /device:TPU:21 before, /device:TPU:13 now
where the time goes in v6:
time: 127 us; the launch traced here: 128 us
  Pallas kernels  87.9 us (69%)
  starting transfers between devices  28.4 us (22%)
  waiting for transfers between devices  6.35 us (5%)
  other arithmetic  2.98 us (2%)
    pallas_call x1, Pallas kernels, body(): pl.pallas_call(edge_sketch_kernel, out_shape=(jax.ShapeDtypeStruct((own_b...  37.1 us
    pallas_call x1, Pallas kernels, body(): pl.pallas_call(functools.partial(chip_sketch_kernel, counts), out_shape=(...  24.5 us
    ppermute x8, starting transfers between devices, send(): return lax.ppermute(piece, ('box', 'col'), pairs)  21.2 us
    pallas_call x1, Pallas kernels, body(): pl.pallas_call(functools.partial(chip_couple_kernel, counts), out_shape=(...  19.4 us
    ppermute x6, starting transfers between devices, swap(): return lax.ppermute(value, 'col', [(0, 1), (1, 0)])  7.21 us
    ppermute x6, waiting for transfers between devices, swap(): return lax.ppermute(value, 'col', [(0, 1), (1, 0)])  6.33 us
    pallas_call x1, Pallas kernels, body(): pl.pallas_call(edge_couple_kernel, out_shape=(coupling_shape, jax.ShapeDt...  3.43 us
  transfers between devices with their start and end apart: 14, of which 5 were waited for; matrix products, arithmetic and copies ran while one was open for 3% of the time, Pallas kernels for 38%

profile of v6, /device:TPU:13, one launch (start us, length us, event | category | flops | bytes accessed | tf_op | source)
XLA Modules:
  0.0 127.8 jit_solution(17908663732995184814)
XLA Ops:
  0.7 0.7 collective-permute-start
  1.4 0.8 copy.21.points
  2.4 1.0 fusion.11
  3.4 1.1 fusion.3
  4.6 4.1 %collective-permute-start.3 = (bf16[1,528,128]{2,1,0:T(8,128)(2,1)S(1)}, bf16[1,528,128]{2,1,0:T(8,128)(2,1)S(1)}, u32[]{:S(2)}, u32[]{:S(2)}) collective-permute-start(bf16[1,528,128]{2,1,0:T(8,128)(2,1)S(1)} %fusion.7), channel_id=1, source_target_pairs={{1,10},{3,12},{5,14},{9,18},{10,1},{11,20},{12,3},{13,22},{14,5},{... | collective-permute-start | bytes 405512 | tf_op jit(solution)/shard_map/ppermute | solution.py:560
  8.8 2.3 %collective-permute-start.4 = (bf16[1,528,128]{2,1,0:T(8,128)(2,1)S(1)}, bf16[1,528,128]{2,1,0:T(8,128)(2,1)S(1)}, u32[]{:S(2)}, u32[]{:S(2)}) collective-permute-start(bf16[1,528,128]{2,1,0:T(8,128)(2,1)S(1)} %fusion.6), channel_id=1, source_target_pairs={{3,8},{5,10},{7,12},{8,3},{10,5},{11,16},{12,7},{13,18},{15,20},{1... | collective-permute-start | bytes 405512 | tf_op jit(solution)/shard_map/ppermute | solution.py:560
  11.1 0.1 fusion
  11.3 1.9 %collective-permute-start.2 = (bf16[4,528,128]{2,1,0:T(8,128)(2,1)S(1)}, bf16[4,528,128]{2,1,0:T(8,128)(2,1)S(1)}, u32[]{:S(2)}, u32[]{:S(2)}) collective-permute-start(bf16[4,528,128]{2,1,0:T(8,128)(2,1)S(1)} %fusion), channel_id=1, source_target_pairs={{1,8},{3,10},{5,12},{7,14},{8,1},{9,16},{10,3},{11,18},{12,5},{13,... | collective-permute-start | bytes 1622024 | tf_op jit(solution)/shard_map/ppermute | solution.py:560
  13.2 0.1 fusion.1
  13.4 3.5 %collective-permute-start.1 = (bf16[4,528,128]{2,1,0:T(8,128)(2,1)S(1)}, bf16[4,528,128]{2,1,0:T(8,128)(2,1)S(1)}, u32[]{:S(2)}, u32[]{:S(2)}) collective-permute-start(bf16[4,528,128]{2,1,0:T(8,128)(2,1)S(1)} %fusion.1), channel_id=1, source_target_pairs={{1,2},{2,1},{3,4},{4,3},{5,6},{6,5},{9,10},{10,9},{11,12},{12,11},... | collective-permute-start | bytes 1622024 | tf_op jit(solution)/shard_map/ppermute | solution.py:560
  16.9 24.5 %chip_sketch.1 = (f32[8,512,128]{2,1,0:T(8,128)}, bf16[34,512,512]{2,1,0:T(8,128)(2,1)}) custom-call(s32[1]{0:T(128)} %bitcast.core_ref, s32[8,9]{1,0:T(8,128)S(1)} %constant_dynamic-slice_fusion.mask, s32[2,34,6]{2,1,0:T(8,128)S(1)} %copy-done.3, bf16[16,3,512]{2,1,0:T(4,128)(2,1)S(1)} %copy.21.points, bf16[16,256,128]{2,1,0:T(8,128)(2,1)S(1)} %copy-done.1, ...), custom_call_target="tpu_custom_call" | custom-call | flops 8000000000 | bytes 24000000 | tf_op jit(solution)/shard_map/chip_sketch/pallas_call | solution.py:613
  41.5 2.9 %collective-permute-start.5 = (bf16[4,528,128]{2,1,0:T(8,128)(2,1)S(1)}, bf16[4,528,128]{2,1,0:T(8,128)(2,1)S(1)}, u32[]{:S(2)}, u32[]{:S(2)}) collective-permute-start(bf16[4,528,128]{2,1,0:T(8,128)(2,1)S(1)} %collective-permute-done.1.first_col), channel_id=1, source_target_pairs={{0,1},{1,0},{2,3},{3,2},{4,5},{5,4},{6,7},{7,6},{8,9},{9,8},{10,11... | collective-permute-start | bytes 1622024 | tf_op jit(solution)/shard_map/ppermute | solution.py:577
  44.4 1.6 %collective-permute-done.5.second_col = bf16[4,528,128]{2,1,0:T(8,128)(2,1)S(1)} collective-permute-done((bf16[4,528,128]{2,1,0:T(8,128)(2,1)S(1)}, bf16[4,528,128]{2,1,0:T(8,128)(2,1)S(1)}, u32[]{:S(2)}, u32[]{:S(2)}) %collective-permute-start.5) | collective-permute-done | bytes 540704 | tf_op jit(solution)/shard_map/ppermute | solution.py:577
  45.9 37.1 %edge_sketch.1 = (bf16[8,512,128]{2,1,0:T(8,128)(2,1)S(1)}, bf16[22,512,512]{2,1,0:T(8,128)(2,1)}) custom-call(s32[1]{0:T(128)} %bitcast.core_ref, s32[8,9]{1,0:T(8,128)S(1)} %constant_dynamic-slice_fusion.mask, s32[2,22,6]{2,1,0:T(8,128)S(1)} %copy-done.2, bf16[16,3,512]{2,1,0:T(4,128)(2,1)S(1)} %copy.21.points, f32[8,512,128]{2,1,0:T(8,128)} %get-tuple-element.26.sketched, ...), custom_call_target="tpu_custom_call" | custom-call | tf_op jit(solution)/shard_map/edge_sketch/pallas_call | solution.py:639
  83.0 0.1 collective-permute-start.6
  83.1 2.6 %collective-permute-done.6.theirs = bf16[8,512,128]{2,1,0:T(8,128)(2,1)S(1)} collective-permute-done((bf16[8,512,128]{2,1,0:T(8,128)(2,1)S(1)}, bf16[8,512,128]{2,1,0:T(8,128)(2,1)S(1)}, u32[]{:S(2)}, u32[]{:S(2)}) %collective-permute-start.6) | collective-permute-done | bytes 1048608 | tf_op jit(solution)/shard_map/ppermute | solution.py:577
  85.8 0.3 maximum_select_fusion
  86.1 0.1 fusion.2
  86.3 1.9 %collective-permute-start.10 = (bf16[1,512,128]{2,1,0:T(8,128)(2,1)S(1)}, bf16[1,512,128]{2,1,0:T(8,128)(2,1)S(1)}, u32[]{:S(2)}, u32[]{:S(2)}) collective-permute-start(bf16[1,512,128]{2,1,0:T(8,128)(2,1)S(1)} %get-tuple-element.48), channel_id=1, source_target_pairs={{3,8},{5,10},{7,12},{8,3},{10,5},{11,16},{12,7},{13,18},{15,20},{1... | collective-permute-start | bytes 393224 | tf_op jit(solution)/shard_map/ppermute | solution.py:560
  88.2 1.9 %collective-permute-start.9 = (bf16[1,512,128]{2,1,0:T(8,128)(2,1)S(1)}, bf16[1,512,128]{2,1,0:T(8,128)(2,1)S(1)}, u32[]{:S(2)}, u32[]{:S(2)}) collective-permute-start(bf16[1,512,128]{2,1,0:T(8,128)(2,1)S(1)} %get-tuple-element.49), channel_id=1, source_target_pairs={{1,10},{3,12},{5,14},{9,18},{10,1},{11,20},{12,3},{13,22},{14,5},{... | collective-permute-start | bytes 393224 | tf_op jit(solution)/shard_map/ppermute | solution.py:560
  90.1 1.9 %collective-permute-start.8 = (bf16[4,512,128]{2,1,0:T(8,128)(2,1)S(1)}, bf16[4,512,128]{2,1,0:T(8,128)(2,1)S(1)}, u32[]{:S(2)}, u32[]{:S(2)}) collective-permute-start(bf16[4,512,128]{2,1,0:T(8,128)(2,1)S(1)} %slice_select_fusion), channel_id=1, source_target_pairs={{1,8},{3,10},{5,12},{7,14},{8,1},{9,16},{10,3},{11,18},{12,5},{13,... | collective-permute-start | bytes 1572872 | tf_op jit(solution)/shard_map/ppermute | solution.py:560
  92.1 3.6 %collective-permute-start.7 = (bf16[4,512,128]{2,1,0:T(8,128)(2,1)S(1)}, bf16[4,512,128]{2,1,0:T(8,128)(2,1)S(1)}, u32[]{:S(2)}, u32[]{:S(2)}) collective-permute-start(bf16[4,512,128]{2,1,0:T(8,128)(2,1)S(1)} %fusion.2), channel_id=1, source_target_pairs={{1,2},{2,1},{3,4},{4,3},{5,6},{6,5},{9,10},{10,9},{11,12},{12,11},... | collective-permute-start | bytes 1572872 | tf_op jit(solution)/shard_map/ppermute | solution.py:560
  95.6 19.4 %chip_couple.1 = (f32[16,9,64,128]{3,2,1,0:T(8,128)}, f32[8,9,64,128]{3,2,1,0:T(8,128)S(1)}, bf16[22,128,512]{2,1,0:T(8,128)(2,1)S(1)}, bf16[16,256,128]{2,1,0:T(8,128)(2,1)}) custom-call(s32[1]{0:T(128)} %bitcast.core_ref, s32[8,9]{1,0:T(8,128)S(1)} %constant_dynamic-slice_fusion.mask, s32[2,34,6]{2,1,0:T(8,128)S(1)} %copy-done.3, ...), custom_call_target="tpu_custom_call" | custom-call | flops 8000000000 | bytes 32000000 | tf_op jit(solution)/shard_map/chip_couple/pallas_call | solution.py:673
  115.1 2.9 %collective-permute-start.11 = (bf16[4,512,128]{2,1,0:T(8,128)(2,1)S(1)}, bf16[4,512,128]{2,1,0:T(8,128)(2,1)S(1)}, u32[]{:S(2)}, u32[]{:S(2)}) collective-permute-start(bf16[4,512,128]{2,1,0:T(8,128)(2,1)S(1)} %collective-permute-done.7.first_col), channel_id=1, source_target_pairs={{0,1},{1,0},{2,3},{3,2},{4,5},{5,4},{6,7},{7,6},{8,9},{9,8},{10,11... | collective-permute-start | bytes 1572872 | tf_op jit(solution)/shard_map/ppermute | solution.py:577
  118.0 1.5 %collective-permute-done.11.second_col = bf16[4,512,128]{2,1,0:T(8,128)(2,1)S(1)} collective-permute-done((bf16[4,512,128]{2,1,0:T(8,128)(2,1)S(1)}, bf16[4,512,128]{2,1,0:T(8,128)(2,1)S(1)}, u32[]{:S(2)}, u32[]{:S(2)}) %collective-permute-start.11) | collective-permute-done | bytes 524320 | tf_op jit(solution)/shard_map/ppermute | solution.py:577
  119.5 0.4 collective-permute-start.13
  119.9 3.4 %edge_couple.1 = (f32[16,9,64,128]{3,2,1,0:T(8,128)}, f32[22,64,128]{2,1,0:T(8,128)S(1)}) custom-call(s32[1]{0:T(128)} %bitcast.core_ref, s32[8,9]{1,0:T(8,128)S(1)} %constant_dynamic-slice_fusion.mask, s32[2,22,6]{2,1,0:T(8,128)S(1)} %copy-done.2, bf16[22,128,512]{2,1,0:T(8,128)(2,1)S(1)} %get-tuple-element.37.projected, ...), custom_call_target="tpu_custom_call", output_to_operand_aliasing={{0}: (9, {})} | custom-call | tf_op jit(solution)/shard_map/edge_couple/pallas_call | solution.py:708
  123.4 0.2 collective-permute-start.12
  123.6 0.5 collective-permute-done.13.bulk
  124.1 1.5 %bulk.1.full_in = f32[16,9,64,128]{3,2,1,0:T(8,128)} custom-call(s32[1]{0:T(128)} %bitcast.core_ref, f32[8,9,64,128]{3,2,1,0:T(8,128)S(1)} %collective-permute-done.13.bulk, f32[16,9,64,128]{3,2,1,0:T(8,128)} %get-tuple-element.47.full_in), custom_call_target="tpu_custom_call", output_to_operand_aliasing={{}: (2, {})} | custom-call | bytes 10000000 | tf_op jit(solution)/shard_map/bulk/pallas_call | solution.py:724
  125.5 0.1 collective-permute-done.12.taken
  125.6 2.0 %settle.1 = f32[16,9,64,128]{3,2,1,0:T(8,128)} custom-call(s32[1]{0:T(128)} %bitcast.core_ref, s32[2,22,6]{2,1,0:T(8,128)S(1)} %copy-done.2, f32[22,64,128]{2,1,0:T(8,128)S(1)} %collective-permute-done.12.taken, f32[16,9,64,128]{3,2,1,0:T(8,128)} %bulk.1.full_in), custom_call_target="tpu_custom_call", output_to_operand_aliasing={{}: (3, {})} | custom-call | tf_op jit(solution)/shard_map/settle/pallas_call | solution.py:735
  (31 shorter events, 0.4 us)
Async XLA Ops:
  0.6 1.7 %copy-start = (s32[16,9]{1,0:T(8,128)S(1)}, s32[16,9]{1,0:T(8,128)}, u32[]{:S(2)}) copy-start(s32[16,9]{1,0:T(8,128)} %param.7) | copy-start | bytes 1732
  0.6 3.8 %copy-start.1 = (bf16[16,256,128]{2,1,0:T(8,128)(2,1)S(1)}, bf16[16,256,128]{2,1,0:T(8,128)(2,1)}, u32[]{:S(2)}) copy-start(bf16[16,256,128]{2,1,0:T(8,128)(2,1)} %mine.1) | copy-start | bytes 3145732
  0.7 3.8 %collective-permute-start = (bf16[16,256,128]{2,1,0:T(8,128)(2,1)}, bf16[16,256,128]{2,1,0:T(8,128)(2,1)S(1)}, u32[]{:S(2)}, u32[]{:S(2)}) collective-permute-start(bf16[16,256,128]{2,1,0:T(8,128)(2,1)} %mine.1), channel_id=1, source_target_pairs={{0,1},{1,0},{2,3},{3,2},{4,5},{5,4},{6,7},{7,6},{8,9},{9,8},{10,11... | collective-permute-start | bytes 3145736 | tf_op jit(solution)/shard_map/ppermute | solution.py:577
  4.5 12.4 %copy-start.3 = (s32[2,34,6]{2,1,0:T(8,128)S(1)}, s32[2,34,6]{2,1,0:T(8,128)}, u32[]{:S(2)}) copy-start(s32[2,34,6]{2,1,0:T(8,128)} %constant.16.clone.table) | copy-start | bytes 4900
  4.6 36.8 %collective-permute-start.3 = (bf16[1,528,128]{2,1,0:T(8,128)(2,1)S(1)}, bf16[1,528,128]{2,1,0:T(8,128)(2,1)S(1)}, u32[]{:S(2)}, u32[]{:S(2)}) collective-permute-start(bf16[1,528,128]{2,1,0:T(8,128)(2,1)S(1)} %fusion.7), channel_id=1, source_target_pairs={{1,10},{3,12},{5,14},{9,18},{10,1},{11,20},{12,3},{13,22},{14,5},{... | collective-permute-start | bytes 405512 | tf_op jit(solution)/shard_map/ppermute | solution.py:560
  8.8 32.7 %collective-permute-start.4 = (bf16[1,528,128]{2,1,0:T(8,128)(2,1)S(1)}, bf16[1,528,128]{2,1,0:T(8,128)(2,1)S(1)}, u32[]{:S(2)}, u32[]{:S(2)}) collective-permute-start(bf16[1,528,128]{2,1,0:T(8,128)(2,1)S(1)} %fusion.6), channel_id=1, source_target_pairs={{3,8},{5,10},{7,12},{8,3},{10,5},{11,16},{12,7},{13,18},{15,20},{1... | collective-permute-start | bytes 405512 | tf_op jit(solution)/shard_map/ppermute | solution.py:560
  11.3 30.2 %collective-permute-start.2 = (bf16[4,528,128]{2,1,0:T(8,128)(2,1)S(1)}, bf16[4,528,128]{2,1,0:T(8,128)(2,1)S(1)}, u32[]{:S(2)}, u32[]{:S(2)}) collective-permute-start(bf16[4,528,128]{2,1,0:T(8,128)(2,1)S(1)} %fusion), channel_id=1, source_target_pairs={{1,8},{3,10},{5,12},{7,14},{8,1},{9,16},{10,3},{11,18},{12,5},{13,... | collective-permute-start | bytes 1622024 | tf_op jit(solution)/shard_map/ppermute | solution.py:560
  13.4 28.1 %collective-permute-start.1 = (bf16[4,528,128]{2,1,0:T(8,128)(2,1)S(1)}, bf16[4,528,128]{2,1,0:T(8,128)(2,1)S(1)}, u32[]{:S(2)}, u32[]{:S(2)}) collective-permute-start(bf16[4,528,128]{2,1,0:T(8,128)(2,1)S(1)} %fusion.1), channel_id=1, source_target_pairs={{1,2},{2,1},{3,4},{4,3},{5,6},{6,5},{9,10},{10,9},{11,12},{12,11},... | collective-permute-start | bytes 1622024 | tf_op jit(solution)/shard_map/ppermute | solution.py:560
  16.9 29.0 %copy-start.2 = (s32[2,22,6]{2,1,0:T(8,128)S(1)}, s32[2,22,6]{2,1,0:T(8,128)}, u32[]{:S(2)}) copy-start(s32[2,22,6]{2,1,0:T(8,128)} %constant.17.clone.table.edge_table) | copy-start | bytes 3172
  41.5 4.4 %collective-permute-start.5 = (bf16[4,528,128]{2,1,0:T(8,128)(2,1)S(1)}, bf16[4,528,128]{2,1,0:T(8,128)(2,1)S(1)}, u32[]{:S(2)}, u32[]{:S(2)}) collective-permute-start(bf16[4,528,128]{2,1,0:T(8,128)(2,1)S(1)} %collective-permute-done.1.first_col), channel_id=1, source_target_pairs={{0,1},{1,0},{2,3},{3,2},{4,5},{5,4},{6,7},{7,6},{8,9},{9,8},{10,11... | collective-permute-start | bytes 1622024 | tf_op jit(solution)/shard_map/ppermute | solution.py:577
  83.0 2.7 %collective-permute-start.6 = (bf16[8,512,128]{2,1,0:T(8,128)(2,1)S(1)}, bf16[8,512,128]{2,1,0:T(8,128)(2,1)S(1)}, u32[]{:S(2)}, u32[]{:S(2)}) collective-permute-start(bf16[8,512,128]{2,1,0:T(8,128)(2,1)S(1)} %get-tuple-element.31.mine), channel_id=1, source_target_pairs={{0,1},{1,0},{2,3},{3,2},{4,5},{5,4},{6,7},{7,6},{8,9},{9,8},{10,11... | collective-permute-start | bytes 3145736 | tf_op jit(solution)/shard_map/ppermute | solution.py:577
  86.3 28.8 %collective-permute-start.10 = (bf16[1,512,128]{2,1,0:T(8,128)(2,1)S(1)}, bf16[1,512,128]{2,1,0:T(8,128)(2,1)S(1)}, u32[]{:S(2)}, u32[]{:S(2)}) collective-permute-start(bf16[1,512,128]{2,1,0:T(8,128)(2,1)S(1)} %get-tuple-element.48), channel_id=1, source_target_pairs={{3,8},{5,10},{7,12},{8,3},{10,5},{11,16},{12,7},{13,18},{15,20},{1... | collective-permute-start | bytes 393224 | tf_op jit(solution)/shard_map/ppermute | solution.py:560
  88.2 26.8 %collective-permute-start.9 = (bf16[1,512,128]{2,1,0:T(8,128)(2,1)S(1)}, bf16[1,512,128]{2,1,0:T(8,128)(2,1)S(1)}, u32[]{:S(2)}, u32[]{:S(2)}) collective-permute-start(bf16[1,512,128]{2,1,0:T(8,128)(2,1)S(1)} %get-tuple-element.49), channel_id=1, source_target_pairs={{1,10},{3,12},{5,14},{9,18},{10,1},{11,20},{12,3},{13,22},{14,5},{... | collective-permute-start | bytes 393224 | tf_op jit(solution)/shard_map/ppermute | solution.py:560
  90.1 24.9 %collective-permute-start.8 = (bf16[4,512,128]{2,1,0:T(8,128)(2,1)S(1)}, bf16[4,512,128]{2,1,0:T(8,128)(2,1)S(1)}, u32[]{:S(2)}, u32[]{:S(2)}) collective-permute-start(bf16[4,512,128]{2,1,0:T(8,128)(2,1)S(1)} %slice_select_fusion), channel_id=1, source_target_pairs={{1,8},{3,10},{5,12},{7,14},{8,1},{9,16},{10,3},{11,18},{12,5},{13,... | collective-permute-start | bytes 1572872 | tf_op jit(solution)/shard_map/ppermute | solution.py:560
  92.1 23.0 %collective-permute-start.7 = (bf16[4,512,128]{2,1,0:T(8,128)(2,1)S(1)}, bf16[4,512,128]{2,1,0:T(8,128)(2,1)S(1)}, u32[]{:S(2)}, u32[]{:S(2)}) collective-permute-start(bf16[4,512,128]{2,1,0:T(8,128)(2,1)S(1)} %fusion.2), channel_id=1, source_target_pairs={{1,2},{2,1},{3,4},{4,3},{5,6},{6,5},{9,10},{10,9},{11,12},{12,11},... | collective-permute-start | bytes 1572872 | tf_op jit(solution)/shard_map/ppermute | solution.py:560
  115.1 4.5 %collective-permute-start.11 = (bf16[4,512,128]{2,1,0:T(8,128)(2,1)S(1)}, bf16[4,512,128]{2,1,0:T(8,128)(2,1)S(1)}, u32[]{:S(2)}, u32[]{:S(2)}) collective-permute-start(bf16[4,512,128]{2,1,0:T(8,128)(2,1)S(1)} %collective-permute-done.7.first_col), channel_id=1, source_target_pairs={{0,1},{1,0},{2,3},{3,2},{4,5},{5,4},{6,7},{7,6},{8,9},{9,8},{10,11... | collective-permute-start | bytes 1572872 | tf_op jit(solution)/shard_map/ppermute | solution.py:577
  119.5 4.5 %collective-permute-start.13 = (f32[8,9,64,128]{3,2,1,0:T(8,128)S(1)}, f32[8,9,64,128]{3,2,1,0:T(8,128)S(1)}, u32[]{:S(2)}, u32[]{:S(2)}) collective-permute-start(f32[8,9,64,128]{3,2,1,0:T(8,128)S(1)} %get-tuple-element.46), channel_id=1, source_target_pairs={{0,1},{1,0},{2,3},{3,2},{4,5},{5,4},{6,7},{7,6},{8,9},{9,8},{10,11... | collective-permute-start | bytes 7077896 | tf_op jit(solution)/shard_map/ppermute | solution.py:577
  123.4 2.3 %collective-permute-start.12 = (f32[22,64,128]{2,1,0:T(8,128)S(1)}, f32[22,64,128]{2,1,0:T(8,128)S(1)}, u32[]{:S(2)}, u32[]{:S(2)}) collective-permute-start(f32[22,64,128]{2,1,0:T(8,128)S(1)} %get-tuple-element.45), channel_id=1, source_target_pairs={{0,1},{1,0},{2,3},{3,2},{4,5},{5,4},{6,7},{7,6},{8,9},{9,8},{10,11... | collective-permute-start | bytes 2162696 | tf_op jit(solution)/shard_map/ppermute | solution.py:577
